TPU v7x, 32 devices: a whole 2x2x4 slice. The times are simulated.
32 devices in a mesh: groups: 2 (over x), fsdp: 2 (over core), tp: 8 (over z, y).
Axes of the slice: x: 2, y: 2, z: 4, core: 2. Of those that a mesh axis runs over, the one named last changes fastest.
Arguments:
- hidden_in: bfloat16 [32, 8, 8192], P(('groups', 'fsdp')), parts along dimension 0, may hold values from -6 to 6
- input_gain: bfloat16 [8192], replicated, may hold values from 0.3984375 to 1.59375
- post_gain: bfloat16 [8192], replicated, may hold values from 0.3984375 to 1.59375
- query_base_weight: bfloat16 [8192, 8192], P('fsdp', 'tp'), may hold values from -6 to 6
- query_bias: bfloat16 [8192], P('tp'), may hold values from -5 to 5
- output_base_weight: bfloat16 [8192, 8192], P('tp', 'fsdp'), may hold values from -6 to 6
- query_lower_factor: bfloat16 [8192, 64], P(('fsdp', 'tp')), may hold values from -6 to 6
- query_upper_factor: bfloat16 [64, 8192], P('fsdp', 'tp'), may hold values from -0.75 to 0.75
- output_lower_factor: bfloat16 [8192, 64], P('tp', 'fsdp'), may hold values from -6 to 6
- output_upper_factor: bfloat16 [64, 8192], P(None, ('fsdp', 'tp')), may hold values from -0.75 to 0.75
- cache_keys: bfloat16 [32, 8, 2048, 128], P(('groups', 'fsdp'), 'tp'), parts along dimension 0, as said below
- cache_values: bfloat16 [32, 8, 2048, 128], P(('groups', 'fsdp'), 'tp'), parts along dimension 0, as said below
- cache_lengths: int32 [32], P(('groups', 'fsdp')), parts along dimension 0, may hold values from 512 to 2048, as said below
Outputs:
- residual_out: bfloat16 [32, 8, 8192], P(('groups', 'fsdp')), parts along dimension 0
- normed_out: bfloat16 [32, 8, 8192], P(('groups', 'fsdp')), parts along dimension 0
- query_effective: bfloat16 [16384, 8192], P(('groups', 'fsdp'), 'tp'), parts along dimension 0
- output_effective: bfloat16 [16384, 8192], P(('groups', 'tp'), 'fsdp'), parts along dimension 0
There are 2 independent parts, one for each index of `groups`. A program takes and returns all parts, laid end to end along the dimension named above; an argument that names none is the same for every part. Nothing has to cross between parts.
Inputs may be any that keep to these rules, and one draw needn't show every extreme that they name: `cache_keys`: cache slots whose tp indices share a key head, that is whose index times 8 // 8 agree, hold equal keys. `cache_values`: laid out as cache_keys: slots sharing a value head hold equal values. `cache_lengths`: some row has exactly 2048 and some other row exactly 512.
All inputs are finite; a program needn't handle non-finite values.
Results may differ from a plain program's by a relative error of at most 0.006.
The roundings to bfloat16 on the way count: a program that leaves them out, or rounds other values in their place, can miss the bound.
Values may be sent and summed in bfloat16 or wider, within the bound.
No kernel may reach another device: no remote copies, remote signals or barrier semaphores. Data moves between devices by JAX's collectives and lax.ppermute only.
A program may use at most 192 MiB of HBM per device.

v0:
```python
import jax
import jax.numpy as jnp
from jax import lax
from jax.sharding import PartitionSpec as P

NORM_EPS = 1e-06
ROPE_BASE = 1000000.0
ADAPTER_SCALE = 0.5


def rms_scale(values, gain):
    mean_square = jnp.mean(values * values, axis=-1, keepdims=True)
    return values * lax.rsqrt(mean_square + NORM_EPS) * gain.astype(jnp.float32)


def rotate(query, lengths, steps):
    half = query.shape[-1] // 2
    inverse = ROPE_BASE ** (-(jnp.arange(half, dtype=jnp.float32) * 2.0) / query.shape[-1])
    positions = (lengths[:, None] - steps + jnp.arange(steps, dtype=jnp.int32)[None, :]).astype(
        jnp.float32
    )
    angles = positions[:, :, None, None] * inverse
    cosine = jnp.cos(angles)
    sine = jnp.sin(angles)
    first = query[..., :half]
    second = query[..., half:]
    return jnp.concatenate(
        [first * cosine - second * sine, second * cosine + first * sine], axis=-1
    )


def attend(query, keys, values, lengths):
    steps = query.shape[1]
    slots = keys.shape[1]
    scores = jnp.einsum("rshd,rkd->rhsk", query, keys, preferred_element_type=jnp.float32)
    limits = lengths[:, None] - steps + jnp.arange(steps, dtype=jnp.int32)[None, :]
    allowed = jnp.arange(slots, dtype=jnp.int32)[None, None, None, :] <= limits[:, None, :, None]
    scores = jnp.where(allowed, scores, jnp.float32(-1e30))
    top = jnp.max(scores, axis=-1, keepdims=True)
    weights = jnp.exp(scores - top)
    probs = (weights / jnp.sum(weights, axis=-1, keepdims=True)).astype(jnp.bfloat16)
    return jnp.einsum("rhsk,rkd->rshd", probs, values, preferred_element_type=jnp.float32).astype(
        jnp.bfloat16
    )


def local(
    hidden_in,
    input_gain,
    post_gain,
    query_base_weight,
    query_bias,
    output_base_weight,
    query_lower_factor,
    query_upper_factor,
    output_lower_factor,
    output_upper_factor,
    cache_keys,
    cache_values,
    cache_lengths,
):
    lower_factor_block, upper_factor_block = (
        lax.all_gather(query_lower_factor, "tp", axis=0, tiled=True),
        lax.all_gather(output_upper_factor, "tp", axis=1, tiled=True),
    )
    query_inner_width, output_inner_width = (
        lax.all_gather(query_upper_factor, "fsdp", axis=0, tiled=True),
        lax.all_gather(output_lower_factor, "fsdp", axis=1, tiled=True),
    )
    query_effective = (
        query_base_weight.astype(jnp.float32)
        + ADAPTER_SCALE
        * jnp.dot(lower_factor_block, query_inner_width, preferred_element_type=jnp.float32)
    ).astype(jnp.bfloat16)
    output_effective = (
        output_base_weight.astype(jnp.float32)
        + ADAPTER_SCALE
        * jnp.dot(output_inner_width, upper_factor_block, preferred_element_type=jnp.float32)
    ).astype(jnp.bfloat16)
    rows, steps, width = hidden_in.shape
    head_dim = cache_keys.shape[-1]
    local_heads = query_base_weight.shape[1] // head_dim
    feature_total = local_heads * head_dim * lax.axis_size("tp")
    inputs32 = hidden_in.astype(jnp.float32)
    normed = rms_scale(inputs32, input_gain).astype(jnp.bfloat16).reshape(rows * steps, width)
    query_sum = jnp.dot(
        normed,
        lax.all_gather(query_effective, "fsdp", axis=0, tiled=True),
        preferred_element_type=jnp.float32,
    )
    query = query_sum * width ** (-0.5) + query_bias.astype(jnp.float32)
    query = rotate(query.reshape(rows, steps, local_heads, head_dim), cache_lengths, steps)
    query = (query * head_dim ** (-0.5)).astype(jnp.bfloat16)
    context = attend(query, cache_keys[:, 0], cache_values[:, 0], cache_lengths)
    context = context.reshape(rows * steps, local_heads * head_dim)
    partial_value = jnp.dot(
        context,
        lax.all_gather(output_effective, "fsdp", axis=1, tiled=True),
        preferred_element_type=jnp.float32,
    )
    total = lax.psum(partial_value, "tp").reshape(rows, steps, width) * feature_total ** (-0.5)
    combined = inputs32 + total
    return (
        combined.astype(jnp.bfloat16),
        rms_scale(combined, post_gain).astype(jnp.bfloat16),
        query_effective,
        output_effective,
    )


def solution(mesh):
    in_specs = (
        P(("groups", "fsdp"), None, None),
        P(),
        P(),
        P("fsdp", "tp"),
        P("tp"),
        P("tp", "fsdp"),
        P(("fsdp", "tp"), None),
        P("fsdp", "tp"),
        P("tp", "fsdp"),
        P(None, ("fsdp", "tp")),
        P(("groups", "fsdp"), "tp", None, None),
        P(("groups", "fsdp"), "tp", None, None),
        P(("groups", "fsdp")),
    )
    out_specs = (
        P(("groups", "fsdp"), None, None),
        P(("groups", "fsdp"), None, None),
        P(("groups", "fsdp"), "tp"),
        P(("groups", "tp"), "fsdp"),
    )
    return jax.shard_map(local, mesh=mesh, in_specs=in_specs, out_specs=out_specs, check_vma=False)
```

profile of v0, /device:TPU:0, one launch (start us, length us, event | category | flops | bytes accessed | tf_op | source)
XLA Modules:
  0.0 250.0 jit_solution(11627739938552344973)
XLA Ops:
  7.2 0.0 all-gather.3.cloned.1.call-start
  7.2 33.2 %all_gather.18 = bf16[4096,64]{0,1:T(8,128)(2,1)S(1)} all-gather(bf16[512,64]{0,1:T(8,128)(2,1)} %param.19), channel_id=1, replica_groups=mesh['groups'=2,'fsdp'=2,'tp'=8] {'tp'}, dimensions={0}, use_global_device_ids=true | all-gather | bytes 589824 | tf_op jit(solution)/shard_map/all_gather | solution.py:63
  40.4 2.1 all_gather.19
  42.5 9.2 %add_convert_fusion.1 = bf16[4096,1024]{1,0:T(8,128)(2,1)} fusion(bf16[4096,1024]{1,0:T(8,128)(2,1)} %param.16, bf16[4096,64]{0,1:T(8,128)(2,1)S(1)} %all_gather.18, bf16[64,1024]{1,0:T(8,128)(2,1)S(1)} %all_gather.19), kind=kOutput, calls=%fused_computation.2 | convolution fusion | flops 553648128 | bytes 17432576 | tf_op jit(solution)/shard_map/dot_general | solution.py:73
  51.7 0.0 all-gather.3.cloned.1.call-update
  51.7 0.0 all-gather.5.cloned.1.call-start
  51.8 0.8 copy-done.3
  52.5 1.9 all_gather.21
  54.4 31.6 %all_gather.22 = bf16[64,4096]{1,0:T(8,128)(2,1)S(1)} all-gather(bf16[64,512]{1,0:T(8,128)(2,1)S(1)} %copy-done.4), channel_id=1, replica_groups=mesh['groups'=2,'fsdp'=2,'tp'=8] {'tp'}, dimensions={1}, use_global_device_ids=true | all-gather | bytes 589824 | tf_op jit(solution)/shard_map/all_gather | solution.py:64
  86.0 9.1 %add_convert_fusion = bf16[1024,4096]{1,0:T(8,128)(2,1)} fusion(bf16[1024,4096]{1,0:T(8,128)(2,1)} %param.18, bf16[1024,64]{0,1:T(8,128)(2,1)S(1)} %all_gather.21, bf16[64,4096]{1,0:T(8,128)(2,1)S(1)} %all_gather.22), kind=kOutput, calls=%fused_computation.1 | convolution fusion | flops 553648128 | bytes 17432576 | tf_op jit(solution)/shard_map/dot_general | solution.py:78
  95.1 0.0 all-gather.5.cloned.1.call-update
  95.2 0.2 all-reduce.2.cloned.1.call-start
  95.4 0.5 copy-done.5
  95.9 0.5 copy-done
  96.4 0.3 fusion.10
  96.7 0.1 iota_add_fusion
  96.8 0.2 multiply_cosine_fusion
  97.0 0.1 iota_compare_fusion
  97.1 0.0 all-gather.3.cloned.1.call-done
  97.2 9.9 %fusion.17 = f32[8,8,8,128]{3,1,2,0:T(8,128)S(1)} fusion(bf16[8192,1024]{1,0:T(8,128)(2,1)} %all-gather.3.cloned.1.call-done, bf16[8,8,8192]{2,1,0:T(8,128)(2,1)S(1)} %copy-done, f32[8192]{0:T(1024)S(1)} %convert_element_type.53, f32[8,8]{1,0:T(8,128)S(1)} %add_rsqrt_fusion.1, f32[1024]{0:T(1024)S(1)} %convert_element_type.57), kind=kOutput, calls=%fused_computation.26 | convolution fusion | flops 1075970048 | bytes 18125056 | tf_op jit(solution)/shard_map/dot_general | solution.py:86
  107.1 0.1 fusion.33
  107.2 0.1 multiply_subtract_fusion
  107.4 1.6 fusion.3
  109.0 12.7 %fusion.34 = (f32[8,8,8]{1,2,0:T(8,128)S(1)}, f32[8,8,8,2048]{3,1,2,0:T(8,128)S(1)}) fusion(f32[8,8,8,2048]{3,2,1,0:T(8,128)S(1)} %fusion.3, pred[8,8,2048]{2,1,0:T(8,128)(4,1)S(1)} %iota_compare_fusion), kind=kOutput, calls=%fused_computation.52 | output fusion | flops 4196351 | bytes 8521728 | tf_op jit(solution)/shard_map/sub | solution.py:40
  121.8 0.9 fusion.1
  122.6 3.6 %all-gather.5.cloned.1.call-done = bf16[1024,8192]{1,0:T(8,128)(2,1)} async-done(((bf16[1024,4096]{1,0:T(8,128)(2,1)}), bf16[1024,8192]{1,0:T(8,128)(2,1)}) %all-gather.5.cloned.1.call-update) | async-done | bytes 16777232 | tf_op jit(solution)/shard_map/all_gather | solution.py:98
  126.2 10.1 %fusion.25 = f32[64,8192]{1,0:T(8,128)} fusion(bf16[1024,8192]{1,0:T(8,128)(2,1)} %all-gather.5.cloned.1.call-done, bf16[8,8,8,128]{3,1,2,0:T(8,128)(2,1)S(1)} %fusion.1), kind=kOutput, calls=%fused_computation.38 | convolution fusion | flops 1073741824 | bytes 19005440 | tf_op jit(solution)/shard_map/dot_general | solution.py:96
  136.4 0.0 all-reduce.2.cloned.1.call-update
  136.4 103.1 %all-reduce.2.cloned.1.call-done = f32[64,8192]{1,0:T(8,128)} async-done(((f32[64,8192]{1,0:T(8,128)}), f32[64,8192]{1,0:T(8,128)}) %all-reduce.2.cloned.1.call-update) | async-done | bytes 2097168 | tf_op jit(solution)/shard_map/psum | solution.py:101
  239.5 2.2 multiply_reduce_fusion
  241.7 0.0 copy-done.1
  241.7 1.8 multiply_convert_fusion
  (23 shorter events, 0.1 us)
Async XLA Ops:
  7.2 90.0 %all-gather.3.cloned.1.call-start = ((), (), s32[]{:S(2)}) async-start(), calls=%async_computation | async-start | bytes 25165824 | tf_op jit(solution)/shard_map/all_gather | solution.py:88
  51.7 0.8 copy-start.3
  51.7 2.7 %copy-start.4 = (bf16[64,512]{1,0:T(8,128)(2,1)S(1)}, bf16[64,512]{1,0:T(8,128)(2,1)}, u32[]{:S(2)}) copy-start(bf16[64,512]{1,0:T(8,128)(2,1)} %param.22) | copy-start | bytes 196612
  51.7 74.5 %all-gather.5.cloned.1.call-start = ((), (), s32[]{:S(2)}) async-start(), calls=%async_computation.1 | async-start | bytes 25165824 | tf_op jit(solution)/shard_map/all_gather | solution.py:98
  95.1 0.7 copy-start.5
  95.1 0.7 copy-start.7
  95.1 1.3 copy-start
  95.1 1.6 copy-start.9
  95.2 144.3 %all-reduce.2.cloned.1.call-start = ((), (), s32[]{:S(2)}) async-start(), calls=%async_computation.2 | async-start | bytes 4194304 | tf_op jit(solution)/shard_map/psum | solution.py:101
  97.2 10.2 %copy-start.2 = (bf16[8,1,2048,128]{3,2,1,0:T(8,128)(2,1)S(1)}, bf16[8,1,2048,128]{3,2,1,0:T(8,128)(2,1)}, u32[]{:S(2)}) copy-start(bf16[8,1,2048,128]{3,2,1,0:T(8,128)(2,1)} %param.23) | copy-start | bytes 12582916
  109.0 12.7 %copy-start.8 = (bf16[8,1,2048,128]{3,2,1,0:T(8,128)(2,1)S(1)}, bf16[8,1,2048,128]{3,2,1,0:T(8,128)(2,1)}, u32[]{:S(2)}) copy-start(bf16[8,1,2048,128]{3,2,1,0:T(8,128)(2,1)} %param.24) | copy-start | bytes 12582916
  122.6 13.8 %copy-start.6 = (bf16[8192]{0:T(1024)(128)(2,1)S(1)}, bf16[8192]{0:T(1024)(128)(2,1)}, u32[]{:S(2)}) copy-start(bf16[8192]{0:T(1024)(128)(2,1)} %param.15) | copy-start | bytes 49156
  239.5 2.2 copy-start.1
Sparse Core Ops, SparseCore 0:
  51.8 31.1 all-gather.2
  95.3 30.9 all-gather.4
  136.5 102.9 all-reduce.1
where the time goes:
time: 250 us
  waiting for transfers between devices  107 us (43%)
  blocking collectives  68.8 us (28%)
  matrix products  40.8 us (16%)
  other arithmetic  17.6 us (7%)
  between operations  13.9 us (6%)
    psum x1, waiting for transfers between devices, local(): lax.psum(partial_value, 'tp').reshape(rows, steps, width)  103 us
    all_gather x1, blocking collectives, local(): lax.all_gather(query_lower_factor, 'tp', axis=0, tiled=True)  33.2 us
    all_gather x1, blocking collectives, local(): lax.all_gather(output_upper_factor, 'tp', axis=1, tiled=True)  31.6 us
    sub x1, other arithmetic, attend(): weights = jnp.exp(scores - top)  12.7 us
    dot_general x1, matrix products, local(): jnp.dot(context, lax.all_gather(output_effective, 'fsdp', axis=1, tiled=T...  10.1 us
    dot_general x1, matrix products, local(): jnp.dot(normed, lax.all_gather(query_effective, 'fsdp', axis=0, tiled=Tru...  9.92 us
    dot_general x1, matrix products, local(): jnp.dot(lower_factor_block, query_inner_width, preferred_element_type=jnp...  9.15 us
    dot_general x1, matrix products, local(): jnp.dot(output_inner_width, upper_factor_block, preferred_element_type=jn...  9.15 us
  transfers between devices with their start and end apart: 3, of which 2 were waited for; matrix products, arithmetic and copies ran while one was open for 14% of the time, Pallas kernels for 0%

commit v1 on v0

v1 whole, which is shorter than its diff:
```python
import functools

import jax
import jax.numpy as jnp
import numpy as np
from jax import lax
from jax.experimental import pallas as pl
from jax.experimental.pallas import tpu as pltpu
from jax.sharding import PartitionSpec as P

NORM_EPS = 1e-06
ROPE_BASE = 1000000.0
ADAPTER_SCALE = 0.5
VMEM_LIMIT = 32 * 1024 * 1024
BF16 = jnp.bfloat16
F16 = jnp.float16
F32 = jnp.float32
SWAP = [(0, 1), (1, 0)]


def params():
    return pltpu.CompilerParams(vmem_limit_bytes=VMEM_LIMIT)


def cost(flops, read):
    return pl.CostEstimate(flops=flops, bytes_accessed=read, transcendentals=0)


def hop(value, distance):
    total = lax.axis_size("tp")
    return lax.ppermute(value, "tp", [(i, i ^ distance) for i in range(total)])


def swap(value):
    return lax.ppermute(value, "fsdp", SWAP)


def contract_first(left, right):
    return lax.dot_general(left, right, (((0,), (0,)), ((), ())), preferred_element_type=F32)


def query_kernel(place, lower, upper, base, mine, theirs, effective, own, other):
    step = pl.program_id(0)

    @pl.when(step == 0)
    def _():
        own[...] = jnp.zeros_like(own)
        other[...] = jnp.zeros_like(other)

    update = contract_first(lower[0], upper[...])
    fresh = (base[...].astype(F32) + ADAPTER_SCALE * update).astype(BF16)
    effective[...] = fresh
    both = jnp.concatenate([mine[...], theirs[...]], axis=0)
    product = jnp.dot(both, fresh, preferred_element_type=F32)
    rows = own.shape[0]
    own[...] += product[:rows]
    other[...] += product[rows:]


def query_project(tp_index, lower, upper, base, mine, theirs):
    blocks, rank, depth = lower.shape
    width = base.shape[1]
    rows = mine.shape[0]
    spec = pltpu.PrefetchScalarGridSpec(
        num_scalar_prefetch=1,
        grid=(blocks,),
        in_specs=[
            pl.BlockSpec((1, rank, depth), lambda k, t: (k, 0, 0)),
            pl.BlockSpec((rank, width), lambda k, t: (0, 0)),
            pl.BlockSpec((depth, width), lambda k, t: (k ^ t[0], 0)),
            pl.BlockSpec((rows, depth), lambda k, t: (0, k ^ t[0])),
            pl.BlockSpec((rows, depth), lambda k, t: (0, k ^ t[0])),
        ],
        out_specs=[
            pl.BlockSpec((depth, width), lambda k, t: (k ^ t[0], 0)),
            pl.BlockSpec((rows, width), lambda k, t: (0, 0)),
            pl.BlockSpec((rows, width), lambda k, t: (0, 0)),
        ],
    )
    return pl.pallas_call(
        query_kernel,
        grid_spec=spec,
        out_shape=[
            jax.ShapeDtypeStruct(base.shape, BF16),
            jax.ShapeDtypeStruct((rows, width), F32),
            jax.ShapeDtypeStruct((rows, width), F32),
        ],
        compiler_params=params(),
        cost_estimate=cost(2 * base.size * (rank + 2 * rows), 4 * base.size),
        name="query_project",
    )(tp_index, lower, upper, base, mine, theirs)


def attend_kernel(steps, heads, head_dim, scale, lengths, own, other, bias, cosine, sine, keys, values, context):
    group = keys.shape[0]
    slots = keys.shape[1]
    first = pl.program_id(0) * group
    query = (own[...] + other[...]) * scale + bias[...].astype(F32)
    turned = []
    for head in range(heads):
        part = query[:, head * head_dim : (head + 1) * head_dim]
        part = part * cosine[...] + pltpu.roll(part, head_dim // 2, 1) * sine[...]
        turned.append(part * head_dim ** (-0.5))
    slot = lax.broadcasted_iota(jnp.int32, (heads * steps, slots), 1)
    step = lax.broadcasted_iota(jnp.int32, (heads * steps, slots), 0) % steps
    gathered = []
    for row in range(group):
        rows = jnp.concatenate([q[row * steps : (row + 1) * steps] for q in turned], axis=0).astype(BF16)
        scores = lax.dot_general(
            rows, keys[row], (((1,), (1,)), ((), ())), preferred_element_type=F32
        )
        scores = jnp.where(slot - step <= lengths[first + row] - steps, scores, F32(-1e30))
        top = jnp.max(scores, axis=-1, keepdims=True)
        weights = jnp.exp(scores - top)
        probs = (weights / jnp.sum(weights, axis=-1, keepdims=True)).astype(BF16)
        gathered.append(jnp.dot(probs, values[row], preferred_element_type=F32))
    for head in range(heads):
        context[:, head * head_dim : (head + 1) * head_dim] = jnp.concatenate(
            [g[head * steps : (head + 1) * steps] for g in gathered], axis=0
        ).astype(BF16)


def attend(lengths, own, other, bias, cosine, sine, keys, values, steps, scale):
    rows, slots, head_dim = keys.shape
    width = own.shape[1]
    heads = width // head_dim
    group = 2
    tall = group * steps
    spec = pltpu.PrefetchScalarGridSpec(
        num_scalar_prefetch=1,
        grid=(rows // group,),
        in_specs=[
            pl.BlockSpec((tall, width), lambda r, n: (r, 0)),
            pl.BlockSpec((tall, width), lambda r, n: (r, 0)),
            pl.BlockSpec((1, width), lambda r, n: (0, 0)),
            pl.BlockSpec((tall, head_dim), lambda r, n: (r, 0)),
            pl.BlockSpec((tall, head_dim), lambda r, n: (r, 0)),
            pl.BlockSpec((group, slots, head_dim), lambda r, n: (r, 0, 0)),
            pl.BlockSpec((group, slots, head_dim), lambda r, n: (r, 0, 0)),
        ],
        out_specs=pl.BlockSpec((tall, width), lambda r, n: (r, 0)),
    )
    return pl.pallas_call(
        functools.partial(attend_kernel, steps, heads, head_dim, scale),
        grid_spec=spec,
        out_shape=jax.ShapeDtypeStruct((rows * steps, width), BF16),
        compiler_params=params(),
        cost_estimate=cost(4 * keys.size * heads * steps, 4 * keys.size),
        name="attend",
    )(lengths, own, other, bias, cosine, sine, keys, values)


def output_kernel(place, lower, upper, base, mine, theirs, effective, own, other):
    update = contract_first(lower[...], upper[0])
    fresh = (base[...].astype(F32) + ADAPTER_SCALE * update).astype(BF16)
    effective[...] = fresh
    both = jnp.concatenate([mine[...], theirs[...]], axis=0)
    product = jnp.dot(both, fresh, preferred_element_type=F32)
    rows = mine.shape[0]
    own[0, 0] = product[:rows]
    other[0, 0] = product[rows:]


def output_project(tp_index, lower, upper, base, mine, theirs):
    blocks = lax.axis_size("tp")
    depth, whole = base.shape
    width = whole // blocks
    rank = lower.shape[0]
    rows = mine.shape[0]
    spec = pltpu.PrefetchScalarGridSpec(
        num_scalar_prefetch=1,
        grid=(blocks,),
        in_specs=[
            pl.BlockSpec((rank, depth), lambda k, t: (0, 0)),
            pl.BlockSpec((1, rank, width), lambda k, t: (k, 0, 0)),
            pl.BlockSpec((depth, width), lambda k, t: (0, k ^ t[0])),
            pl.BlockSpec((rows, depth), lambda k, t: (0, 0)),
            pl.BlockSpec((rows, depth), lambda k, t: (0, 0)),
        ],
        out_specs=[
            pl.BlockSpec((depth, width), lambda k, t: (0, k ^ t[0])),
            pl.BlockSpec((1, 1, rows, width), lambda k, t: (k % 2, k // 2, 0, 0)),
            pl.BlockSpec((1, 1, rows, width), lambda k, t: (k // 2, k % 2, 0, 0)),
        ],
    )
    return pl.pallas_call(
        output_kernel,
        grid_spec=spec,
        out_shape=[
            jax.ShapeDtypeStruct(base.shape, BF16),
            jax.ShapeDtypeStruct((2, blocks // 2, rows, width), F32),
            jax.ShapeDtypeStruct((blocks // 2, 2, rows, width), F32),
        ],
        compiler_params=params(),
        cost_estimate=cost(2 * base.size * (rank + 2 * rows), 4 * base.size),
        name="output_project",
    )(tp_index, lower, upper, base, mine, theirs)


def finish_kernel(place, bound, hidden, gain, near, far, residual, normed, combined):
    blocks, rows, width = near.shape
    half = blocks * width
    squares = jnp.zeros((rows, 1), F32)
    for pieces, which in ((near, place[1]), (far, 1 - place[1])):
        for k in range(blocks):
            start = pl.multiple_of(which * half + (place[0] ^ k) * width, width)
            total = hidden[:, pl.ds(start, width)].astype(F32) + pieces[k] * bound[0]
            combined[:, pl.ds(start, width)] = total
            residual[:, pl.ds(start, width)] = total.astype(BF16)
            squares += jnp.sum(total * total, axis=-1, keepdims=True)
    inverse = lax.rsqrt(squares / (2 * half) + NORM_EPS)
    normed[...] = (combined[...] * inverse * gain[...].astype(F32)).astype(BF16)


def finish(place, bound, hidden, gain, near, far):
    rows, whole = hidden.shape
    blocks, _, width = near.shape
    tall = 16
    spec = pltpu.PrefetchScalarGridSpec(
        num_scalar_prefetch=2,
        grid=(rows // tall,),
        in_specs=[
            pl.BlockSpec((tall, whole), lambda r, p, b: (r, 0)),
            pl.BlockSpec((1, whole), lambda r, p, b: (0, 0)),
            pl.BlockSpec((blocks, tall, width), lambda r, p, b: (0, r, 0)),
            pl.BlockSpec((blocks, tall, width), lambda r, p, b: (0, r, 0)),
        ],
        out_specs=[
            pl.BlockSpec((tall, whole), lambda r, p, b: (r, 0)),
            pl.BlockSpec((tall, whole), lambda r, p, b: (r, 0)),
        ],
        scratch_shapes=[pltpu.VMEM((tall, whole), F32)],
    )
    return pl.pallas_call(
        finish_kernel,
        grid_spec=spec,
        out_shape=[jax.ShapeDtypeStruct((rows, whole), BF16)] * 2,
        compiler_params=params(),
        cost_estimate=cost(8 * hidden.size, 14 * hidden.size),
        name="finish",
    )(place, bound, hidden, gain, near, far)


def gather_blocks(value):
    outer = lax.axis_size("tp") // 2
    cut = value.shape[0] // 2
    low, high = value[:cut], value[cut:]
    pair = jnp.stack([high, hop(high, 1)])
    along = jnp.stack([low] + [hop(low, 2 * k) for k in range(1, outer)])
    pairs = jnp.stack([pair] + [hop(pair, 2 * k) for k in range(1, outer)])
    lows = jnp.stack([along, hop(along, 1)], axis=1)
    both = jnp.concatenate([lows, pairs], axis=2)
    return both.reshape((2 * outer,) + value.shape)


def reduce_blocks(own, other, shrink):
    outer = other.shape[0]

    def narrow(value):
        return value.astype(F16)

    across = hop(narrow(shrink(own[1])), 1)
    arrived = [hop(narrow(shrink(other[k])), 2 * k) for k in range(1, outer)]
    summed = shrink(own[0]) + across.astype(F32)
    pair = shrink(other[0]) + sum(a.astype(F32) for a in arrived)
    rest = hop(narrow(pair[1]), 1)
    total = summed[0] + sum(hop(narrow(summed[k]), 2 * k).astype(F32) for k in range(1, outer))
    return narrow(total), narrow(pair[0] + rest.astype(F32))


def local(
    hidden_in,
    input_gain,
    post_gain,
    query_base_weight,
    query_bias,
    output_base_weight,
    query_lower_factor,
    query_upper_factor,
    output_lower_factor,
    output_upper_factor,
    cache_keys,
    cache_values,
    cache_lengths,
):
    rows, steps, width = hidden_in.shape
    tall = rows * steps
    half = width // 2
    slots, head_dim = cache_keys.shape[2:]
    features = query_base_weight.shape[1] * lax.axis_size("tp")
    t = lax.axis_index("tp").astype(jnp.int32)
    f = lax.axis_index("fsdp").astype(jnp.int32)
    place = jnp.stack([t, f])
    outer = lax.axis_size("tp") // 2

    lower = gather_blocks(query_lower_factor.T)

    flat = hidden_in.reshape(tall, width)
    inputs32 = flat.astype(F32)
    mean_square = jnp.mean(inputs32 * inputs32, axis=-1, keepdims=True)
    normed = (inputs32 * lax.rsqrt(mean_square + NORM_EPS) * input_gain.astype(F32)).astype(BF16)
    mine = lax.dynamic_slice_in_dim(normed, f * half, half, 1)
    theirs = swap(lax.dynamic_slice_in_dim(normed, (1 - f) * half, half, 1))

    reach = jnp.arange(slots, dtype=jnp.int32)[None, :, None] < cache_lengths[:, None, None]
    bound = jnp.max(jnp.where(reach, jnp.abs(cache_values[:, 0].astype(F32)), 0.0)).astype(BF16)
    rank_part = query_upper_factor.shape[0]
    lower_o = output_lower_factor.T
    columns = query_upper_factor.shape[1]
    sent = jnp.concatenate(
        [query_upper_factor, lower_o, jnp.broadcast_to(bound, (16, columns))], axis=0
    )
    came = swap(sent)

    def in_order(a, b):
        return jnp.where(f == 0, jnp.concatenate([a, b]), jnp.concatenate([b, a]))

    upper = in_order(sent[:rank_part], came[:rank_part])
    lower_o = in_order(sent[rank_part : 2 * rank_part], came[rank_part : 2 * rank_part])
    bound = jnp.maximum(sent[2 * rank_part :], came[2 * rank_part :])

    rank = output_upper_factor.shape[0]
    block = output_upper_factor.shape[1]
    message = jnp.concatenate([output_upper_factor, bound[:, :block]], axis=0)
    message, lower = lax.optimization_barrier((message, lower))
    message = jnp.concatenate([message, message[-16:]], axis=0)
    gathered = gather_blocks(message)
    upper_o = gathered[:, :rank]
    bound = jnp.max(gathered[:, rank:]).astype(F32)

    query_effective, own, other = query_project(
        t[None], lower, upper, query_base_weight, mine, theirs
    )
    other = swap(other)

    inverse = ROPE_BASE ** (-(np.arange(head_dim // 2) * 2.0) / head_dim)
    inverse = jnp.asarray(inverse.astype(np.float32))
    positions = cache_lengths[:, None] - steps + jnp.arange(steps, dtype=jnp.int32)[None, :]
    angles = positions.astype(F32).reshape(tall, 1) * inverse
    cosine, sine = jnp.cos(angles), jnp.sin(angles)
    context = attend(
        cache_lengths,
        own,
        other,
        query_bias[None, :],
        jnp.concatenate([cosine, cosine], axis=1),
        jnp.concatenate([-sine, sine], axis=1),
        cache_keys[:, 0],
        cache_values[:, 0],
        steps,
        width ** (-0.5),
    )

    output_effective, own, other = output_project(
        t[None], lower_o, upper_o, output_base_weight, context, swap(context)
    )

    small = 2.0**-16
    unit = jnp.maximum(bound, 1e-30) * small
    shrink_by = 1.0 / unit

    def shrink(value):
        return (value * shrink_by) * (features ** (-0.5) * small)

    near, far = reduce_blocks(own, other, shrink)
    far = swap(far)

    along = jnp.stack([near] + [hop(near, 2 * k) for k in range(1, outer)])
    pair = jnp.stack([far, hop(far, 1)])
    pairs = jnp.stack([pair] + [hop(pair, 2 * k) for k in range(1, outer)])
    near = jnp.stack([along, hop(along, 1)], axis=1)
    near = near.reshape((2 * outer,) + near.shape[2:]).astype(F32)
    far = pairs.reshape((2 * outer,) + pairs.shape[2:]).astype(F32)

    residual, normed_out = finish(
        place, jnp.maximum(bound, 1e-30)[None], flat, post_gain[None, :], near, far
    )
    return (
        residual.reshape(hidden_in.shape),
        normed_out.reshape(hidden_in.shape),
        query_effective,
        output_effective,
    )


def solution(mesh):
    in_specs = (
        P(("groups", "fsdp"), None, None),
        P(),
        P(),
        P("fsdp", "tp"),
        P("tp"),
        P("tp", "fsdp"),
        P(("fsdp", "tp"), None),
        P("fsdp", "tp"),
        P("tp", "fsdp"),
        P(None, ("fsdp", "tp")),
        P(("groups", "fsdp"), "tp", None, None),
        P(("groups", "fsdp"), "tp", None, None),
        P(("groups", "fsdp")),
    )
    out_specs = (
        P(("groups", "fsdp"), None, None),
        P(("groups", "fsdp"), None, None),
        P(("groups", "fsdp"), "tp"),
        P(("groups", "tp"), "fsdp"),
    )
    return jax.shard_map(local, mesh=mesh, in_specs=in_specs, out_specs=out_specs, check_vma=False)
```

time: 250 us -> 123 us (0.49)
  waiting for transfers between devices: 107 us -> 31.6 us
  blocking collectives: 68.8 us -> 0 us
  starting transfers between devices: 0.3 us -> 46.5 us
  matrix products: 40.8 us -> 0 us
  Pallas kernels: 0 us -> 22.6 us
  between operations: 13.9 us -> 1.89 us
  local copies, waits for them, and re-layouts: 1.93 us -> 8.84 us
  other arithmetic: 17.6 us -> 11.2 us
    psum x1 -> x0, waiting for transfers between devices: 103 us -> none  [local(): lax.psum(partial_value, 'tp').reshape(rows, steps, width)]
    all_gather x4 -> x0, blocking collectives: 68.8 us -> none  [the longest x1 33.2 us: local(): lax.all_gather(query_lower_factor, 'tp', axis=0, tiled=True)]
    ppermute x0 -> x37, starting transfers between devices: none -> 46.5 us  [the longest x32 45.7 us: hop(): return lax.ppermute(value, 'tp', [(i, i ^ distance) for i in range(total)])]
    dot_general x6 -> x0, matrix products: 40.8 us -> none  [the longest x1 10.1 us: local(): jnp.dot(context, lax.all_gather(output_effective, 'fsdp', axis=1, tiled=T...]
    ppermute x0 -> x37, waiting for transfers between devices: none -> 31.6 us  [the longest x32 31.6 us: hop(): return lax.ppermute(value, 'tp', [(i, i ^ distance) for i in range(total)])]
    pallas_call x0 -> x4, Pallas kernels: none -> 22.6 us  [the longest x1 6.96 us: output_project(): pl.pallas_call(output_kernel, grid_spec=spec, out_shape=[jax.ShapeDtypeSt...]
    sub x3 -> x1, other arithmetic: 12.8 us -> 0.01 us  [local(): cache_lengths[:, None] - steps + jnp.arange(steps, dtype=jnp.int32)[None, :]]
    reduce_max x0 -> x2, other arithmetic: none -> 7.48 us  [the longest x1 6.74 us: local(): jnp.max(jnp.where(reach, jnp.abs(cache_values[:, 0].astype(F32)), 0.0))]
  transfers between devices with their start and end apart: 3 -> 37, of which waited for: 2 -> 11; matrix products, arithmetic and copies ran while one was open for 14% -> 10% of each run, Pallas kernels for 0% -> 10%
where the time goes in v1:
time: 123 us
  starting transfers between devices  46.5 us (38%)
  waiting for transfers between devices  31.6 us (26%)
  Pallas kernels  22.6 us (18%)
  other arithmetic  11.2 us (9%)
  local copies, waits for them, and re-layouts  8.84 us (7%)
  between operations  1.89 us (2%)
    ppermute x32, starting transfers between devices, hop(): return lax.ppermute(value, 'tp', [(i, i ^ distance) for i in range(total)])  45.7 us
    ppermute x32, waiting for transfers between devices, hop(): return lax.ppermute(value, 'tp', [(i, i ^ distance) for i in range(total)])  31.6 us
    unnamed x26, local copies, waits for them, and re-layouts  6.98 us
    pallas_call x1, Pallas kernels, output_project(): pl.pallas_call(output_kernel, grid_spec=spec, out_shape=[jax.ShapeDtypeSt...  6.96 us
    reduce_max x1, other arithmetic, local(): jnp.max(jnp.where(reach, jnp.abs(cache_values[:, 0].astype(F32)), 0.0))  6.74 us
    pallas_call x1, Pallas kernels, query_project(): pl.pallas_call(query_kernel, grid_spec=spec, out_shape=[jax.ShapeDtypeStr...  6.65 us
    pallas_call x1, Pallas kernels, attend(): pl.pallas_call(functools.partial(attend_kernel, steps, heads, head_dim, s...  6.06 us
    pallas_call x1, Pallas kernels, finish(): pl.pallas_call(finish_kernel, grid_spec=spec, out_shape=[jax.ShapeDtypeSt...  2.94 us
  transfers between devices with their start and end apart: 37, of which 11 were waited for; matrix products, arithmetic and copies ran while one was open for 10% of the time, Pallas kernels for 10%

profile of v1, /device:TPU:0, one launch (start us, length us, event | category | flops | bytes accessed | tf_op | source)
XLA Modules:
  0.0 122.7 jit_solution(2382079559376931378)
XLA Ops:
  1.4 4.1 %collective-permute-start.2 = (bf16[32,512]{1,0:T(8,128)(2,1)S(1)}, bf16[32,512]{1,0:T(8,128)(2,1)S(1)}, u32[]{:S(2)}, u32[]{:S(2)}) collective-permute-start(bf16[32,512]{1,0:T(8,128)(2,1)S(1)} %get-tuple-element.52), channel_id=1, source_target_pairs={{0,4},{1,5},{2,6},{3,7},{4,0},{5,1},{6,2},{7,3},{8,12},{9,13},{10,... | collective-permute-start | bytes 98312 | tf_op jit(solution)/shard_map/ppermute | solution.py:31
  5.5 1.6 %collective-permute-start.1 = (bf16[32,512]{1,0:T(8,128)(2,1)S(1)}, bf16[32,512]{1,0:T(8,128)(2,1)S(1)}, u32[]{:S(2)}, u32[]{:S(2)}) collective-permute-start(bf16[32,512]{1,0:T(8,128)(2,1)S(1)} %get-tuple-element.52), channel_id=1, source_target_pairs={{0,2},{1,3},{2,0},{3,1},{4,6},{5,7},{6,4},{7,5},{8,10},{9,11},{10,... | collective-permute-start | bytes 98312 | tf_op jit(solution)/shard_map/ppermute | solution.py:31
  7.1 1.7 %collective-permute-start.5 = (bf16[32,512]{1,0:T(8,128)(2,1)S(1)}, bf16[32,512]{1,0:T(8,128)(2,1)S(1)}, u32[]{:S(2)}, u32[]{:S(2)}) collective-permute-start(bf16[32,512]{1,0:T(8,128)(2,1)S(1)} %get-tuple-element.51), channel_id=1, source_target_pairs={{0,1},{1,0},{2,3},{3,2},{4,5},{5,4},{6,7},{7,6},{8,9},{9,8},{10,11... | collective-permute-start | bytes 98312 | tf_op jit(solution)/shard_map/ppermute | solution.py:31
  9.6 6.7 %select_reduce_fusion = bf16[]{:T(256)} fusion(pred[8,2048]{1,0:T(8,128)(4,1)S(1)} %iota_compare_fusion, bf16[8,1,2048,128]{3,2,1,0:T(8,128)(2,1)} %param.25), kind=kLoop, calls=%fused_computation | loop fusion | flops 8388607 | bytes 4210690 | tf_op jit(solution)/shard_map/reduce_max | solution.py:306
  19.2 1.8 %collective-permute-start.7 = (bf16[2,32,512]{2,1,0:T(8,128)(2,1)S(1)}, bf16[2,32,512]{2,1,0:T(8,128)(2,1)S(1)}, u32[]{:S(2)}, u32[]{:S(2)}) collective-permute-start(bf16[2,32,512]{2,1,0:T(8,128)(2,1)S(1)} %get-tuple-element.54), channel_id=1, source_target_pairs={{0,4},{1,5},{2,6},{3,7},{4,0},{5,1},{6,2},{7,3},{8,12},{9,13},{10,... | collective-permute-start | bytes 196616 | tf_op jit(solution)/shard_map/ppermute | solution.py:31
  21.0 2.5 %collective-permute-start.6 = (bf16[2,32,512]{2,1,0:T(8,128)(2,1)S(1)}, bf16[2,32,512]{2,1,0:T(8,128)(2,1)S(1)}, u32[]{:S(2)}, u32[]{:S(2)}) collective-permute-start(bf16[2,32,512]{2,1,0:T(8,128)(2,1)S(1)} %get-tuple-element.54), channel_id=1, source_target_pairs={{0,2},{1,3},{2,0},{3,1},{4,6},{5,7},{6,4},{7,5},{8,10},{9,11},{10,... | collective-permute-start | bytes 196616 | tf_op jit(solution)/shard_map/ppermute | solution.py:31
  26.2 3.4 %collective-permute-done.8 = bf16[2,32,512]{2,1,0:T(8,128)(2,1)S(1)} collective-permute-done((bf16[2,32,512]{2,1,0:T(8,128)(2,1)S(1)}, bf16[2,32,512]{2,1,0:T(8,128)(2,1)S(1)}, u32[]{:S(2)}, u32[]{:S(2)}) %collective-permute-start.8) | collective-permute-done | bytes 65568 | tf_op jit(solution)/shard_map/ppermute | solution.py:31
  30.6 2.5 %collective-permute-start.9 = (bf16[48,512]{1,0:T(8,128)(2,1)S(1)}, bf16[48,512]{1,0:T(8,128)(2,1)S(1)}, u32[]{:S(2)}, u32[]{:S(2)}) collective-permute-start(bf16[48,512]{1,0:T(8,128)(2,1)S(1)} %get-tuple-element.48), channel_id=1, source_target_pairs={{0,2},{1,3},{2,0},{3,1},{4,6},{5,7},{6,4},{7,5},{8,10},{9,11},{10,... | collective-permute-start | bytes 147464 | tf_op jit(solution)/shard_map/ppermute | solution.py:31
  34.7 3.4 %copy-done.2 = bf16[4096,1024]{1,0:T(8,128)(2,1)S(1)} copy-done((bf16[4096,1024]{1,0:T(8,128)(2,1)S(1)}, bf16[4096,1024]{1,0:T(8,128)(2,1)}, u32[]{:S(2)}) %copy-start.2) | copy-done | bytes 8388632
  38.0 6.7 %query_project.1 = (bf16[4096,1024]{1,0:T(8,128)(2,1)}, f32[64,1024]{1,0:T(8,128)S(1)}, f32[64,1024]{1,0:T(8,128)S(1)}) custom-call(s32[1]{0:T(128)} %bitcast.place, bf16[8,64,512]{2,1,0:T(8,128)(2,1)S(1)} %bitcast.104, bf16[64,1024]{1,0:T(8,128)(2,1)S(1)} %maximum_select_fusion.1.upper, bf16[4096,1024]{1,0:T(8,128)(2,1)S(1)} %copy-done.2, ...), custom_call_target="tpu_custom_call" | custom-call | flops 1610612736 | bytes 16777216 | tf_op jit(solution)/shard_map/query_project/pallas_call | solution.py:80
  44.8 1.6 %collective-permute-start.12 = (bf16[4,48,512]{2,1,0:T(8,128)(2,1)S(1)}, bf16[4,48,512]{2,1,0:T(8,128)(2,1)S(1)}, u32[]{:S(2)}, u32[]{:S(2)}) collective-permute-start(bf16[4,48,512]{2,1,0:T(8,128)(2,1)S(1)} %get-tuple-element.37), channel_id=1, source_target_pairs={{0,1},{1,0},{2,3},{3,2},{4,5},{5,4},{6,7},{7,6},{8,9},{9,8},{10,11... | collective-permute-start | bytes 589832 | tf_op jit(solution)/shard_map/ppermute | solution.py:31
  46.9 2.9 %collective-permute-start.14 = (bf16[2,48,512]{2,1,0:T(8,128)(2,1)S(1)}, bf16[2,48,512]{2,1,0:T(8,128)(2,1)S(1)}, u32[]{:S(2)}, u32[]{:S(2)}) collective-permute-start(bf16[2,48,512]{2,1,0:T(8,128)(2,1)S(1)} %get-tuple-element.45), channel_id=1, source_target_pairs={{0,2},{1,3},{2,0},{3,1},{4,6},{5,7},{6,4},{7,5},{8,10},{9,11},{10,... | collective-permute-start | bytes 294920 | tf_op jit(solution)/shard_map/ppermute | solution.py:31
  50.9 6.1 %attend.1.mine = bf16[64,1024]{1,0:T(8,128)(2,1)S(1)} custom-call(s32[8]{0:T(128)S(1)} %copy-done.5, f32[64,1024]{1,0:T(8,128)S(1)} %get-tuple-element.16.own, f32[64,1024]{1,0:T(8,128)S(1)} %collective-permute-done.18.other, bf16[1,1024]{1,0:T(2,128)(2,1)S(1)} %broadcast_in_dim.38.bias, f32[64,128]{1,0:T(8,128)S(1)} %get-tuple-element.58.cosine, ...), custom_call_target="tpu_custom_call" | custom-call | flops 536870912 | bytes 8388608 | tf_op jit(solution)/shard_map/attend/pallas_call | solution.py:143
  58.6 3.4 %copy-done.3 = bf16[1024,4096]{1,0:T(8,128)(2,1)S(1)} copy-done((bf16[1024,4096]{1,0:T(8,128)(2,1)S(1)}, bf16[1024,4096]{1,0:T(8,128)(2,1)}, u32[]{:S(2)}) %copy-start.3) | copy-done | bytes 8388632
  62.0 7.0 %output_project.1 = (bf16[1024,4096]{1,0:T(8,128)(2,1)}, f32[2,4,64,512]{3,2,1,0:T(8,128)S(1)}, f32[4,2,64,512]{3,2,1,0:T(8,128)S(1)}) custom-call(s32[1]{0:T(128)} %bitcast.place, bf16[64,1024]{1,0:T(8,128)(2,1)S(1)} %maximum_select_fusion.lower, bf16[8,64,512]{2,1,0:T(8,128)(2,1)S(1)} %slice.102.upper, bf16[1024,4096]{1,0:T(8,128)(2,1)S(1)} %copy-done.3, ...), custom_call_target="tpu_custom_call" | custom-call | flops 1610612736 | bytes 16777216 | tf_op jit(solution)/shard_map/output_project/pallas_call | solution.py:186
  69.1 2.2 %collective-permute-start.28 = (f16[2,64,512]{2,1,0:T(8,128)(2,1)S(1)}, f16[2,64,512]{2,1,0:T(8,128)(2,1)S(1)}, u32[]{:S(2)}, u32[]{:S(2)}) collective-permute-start(f16[2,64,512]{2,1,0:T(8,128)(2,1)S(1)} %get-tuple-element.26), channel_id=1, source_target_pairs={{0,2},{1,3},{2,0},{3,1},{4,6},{5,7},{6,4},{7,5},{8,10},{9,11},{10,... | collective-permute-start | bytes 393224 | tf_op jit(solution)/shard_map/ppermute | solution.py:31
  72.8 2.4 %collective-permute-done.28 = f16[2,64,512]{2,1,0:T(8,128)(2,1)S(1)} collective-permute-done((f16[2,64,512]{2,1,0:T(8,128)(2,1)S(1)}, f16[2,64,512]{2,1,0:T(8,128)(2,1)S(1)}, u32[]{:S(2)}, u32[]{:S(2)}) %collective-permute-start.28) | collective-permute-done | bytes 131104 | tf_op jit(solution)/shard_map/ppermute | solution.py:31
  75.1 4.7 %collective-permute-done.30 = f16[2,64,512]{2,1,0:T(8,128)(2,1)S(1)} collective-permute-done((f16[2,64,512]{2,1,0:T(8,128)(2,1)S(1)}, f16[2,64,512]{2,1,0:T(8,128)(2,1)S(1)}, u32[]{:S(2)}, u32[]{:S(2)}) %collective-permute-start.30) | collective-permute-done | bytes 131104 | tf_op jit(solution)/shard_map/ppermute | solution.py:31
  79.8 5.0 %collective-permute-done.29 = f16[2,64,512]{2,1,0:T(8,128)(2,1)S(1)} collective-permute-done((f16[2,64,512]{2,1,0:T(8,128)(2,1)S(1)}, f16[2,64,512]{2,1,0:T(8,128)(2,1)S(1)}, u32[]{:S(2)}, u32[]{:S(2)}) %collective-permute-start.29) | collective-permute-done | bytes 131104 | tf_op jit(solution)/shard_map/ppermute | solution.py:31
  85.6 1.6 %collective-permute-start.20 = (f16[4,64,512]{2,1,0:T(8,128)(2,1)S(1)}, f16[4,64,512]{2,1,0:T(8,128)(2,1)S(1)}, u32[]{:S(2)}, u32[]{:S(2)}) collective-permute-start(f16[4,64,512]{2,1,0:T(8,128)(2,1)S(1)} %fusion), channel_id=1, source_target_pairs={{0,1},{1,0},{2,3},{3,2},{4,5},{5,4},{6,7},{7,6},{8,9},{9,8},{10,11... | collective-permute-start | bytes 786440 | tf_op jit(solution)/shard_map/ppermute | solution.py:31
  87.1 2.9 %collective-permute-done.31 = f16[64,512]{1,0:T(8,128)(2,1)S(1)} collective-permute-done((f16[64,512]{1,0:T(8,128)(2,1)S(1)}, f16[64,512]{1,0:T(8,128)(2,1)S(1)}, u32[]{:S(2)}, u32[]{:S(2)}) %collective-permute-start.31) | collective-permute-done | bytes 65568 | tf_op jit(solution)/shard_map/ppermute | solution.py:31
  90.1 3.9 %collective-permute-done.20 = f16[4,64,512]{2,1,0:T(8,128)(2,1)S(1)} collective-permute-done((f16[4,64,512]{2,1,0:T(8,128)(2,1)S(1)}, f16[4,64,512]{2,1,0:T(8,128)(2,1)S(1)}, u32[]{:S(2)}, u32[]{:S(2)}) %collective-permute-start.20) | collective-permute-done | bytes 262176 | tf_op jit(solution)/shard_map/ppermute | solution.py:31
  94.3 2.7 %collective-permute-start.23 = (f16[64,512]{1,0:T(8,128)(2,1)S(1)}, f16[64,512]{1,0:T(8,128)(2,1)S(1)}, u32[]{:S(2)}, u32[]{:S(2)}) collective-permute-start(f16[64,512]{1,0:T(8,128)(2,1)S(1)} %get-tuple-element.34), channel_id=1, source_target_pairs={{0,6},{1,7},{2,4},{3,5},{4,2},{5,3},{6,0},{7,1},{8,14},{9,15},{10,... | collective-permute-start | bytes 196616 | tf_op jit(solution)/shard_map/ppermute | solution.py:31
  98.9 1.6 %collective-permute-done.23 = f16[64,512]{1,0:T(8,128)(2,1)S(1)} collective-permute-done((f16[64,512]{1,0:T(8,128)(2,1)S(1)}, f16[64,512]{1,0:T(8,128)(2,1)S(1)}, u32[]{:S(2)}, u32[]{:S(2)}) %collective-permute-start.23) | collective-permute-done | bytes 65568 | tf_op jit(solution)/shard_map/ppermute | solution.py:31
  100.5 2.4 %collective-permute-done.22 = f16[64,512]{1,0:T(8,128)(2,1)S(1)} collective-permute-done((f16[64,512]{1,0:T(8,128)(2,1)S(1)}, f16[64,512]{1,0:T(8,128)(2,1)S(1)}, u32[]{:S(2)}, u32[]{:S(2)}) %collective-permute-start.22) | collective-permute-done | bytes 65568 | tf_op jit(solution)/shard_map/ppermute | solution.py:31
  102.9 2.3 %collective-permute-start.26 = (f16[64,512]{1,0:T(8,128)(2,1)S(1)}, f16[64,512]{1,0:T(8,128)(2,1)S(1)}, u32[]{:S(2)}, u32[]{:S(2)}) collective-permute-start(f16[64,512]{1,0:T(8,128)(2,1)S(1)} %fusion.7), channel_id=1, source_target_pairs={{0,6},{1,7},{2,4},{3,5},{4,2},{5,3},{6,0},{7,1},{8,14},{9,15},{10,... | collective-permute-start | bytes 196616 | tf_op jit(solution)/shard_map/ppermute | solution.py:31
  105.1 2.2 %collective-permute-start.24 = (f16[64,512]{1,0:T(8,128)(2,1)S(1)}, f16[64,512]{1,0:T(8,128)(2,1)S(1)}, u32[]{:S(2)}, u32[]{:S(2)}) collective-permute-start(f16[64,512]{1,0:T(8,128)(2,1)S(1)} %fusion.7), channel_id=1, source_target_pairs={{0,2},{1,3},{2,0},{3,1},{4,6},{5,7},{6,4},{7,5},{8,10},{9,11},{10,... | collective-permute-start | bytes 196616 | tf_op jit(solution)/shard_map/ppermute | solution.py:31
  108.2 2.0 %collective-permute-start.34 = (f16[2,64,512]{2,1,0:T(8,128)(2,1)S(1)}, f16[2,64,512]{2,1,0:T(8,128)(2,1)S(1)}, u32[]{:S(2)}, u32[]{:S(2)}) collective-permute-start(f16[2,64,512]{2,1,0:T(8,128)(2,1)S(1)} %get-tuple-element.41), channel_id=1, source_target_pairs={{0,2},{1,3},{2,0},{3,1},{4,6},{5,7},{6,4},{7,5},{8,10},{9,11},{10,... | collective-permute-start | bytes 393224 | tf_op jit(solution)/shard_map/ppermute | solution.py:31
  110.2 1.8 %collective-permute-start.36 = (f16[2,64,512]{2,1,0:T(8,128)(2,1)S(1)}, f16[2,64,512]{2,1,0:T(8,128)(2,1)S(1)}, u32[]{:S(2)}, u32[]{:S(2)}) collective-permute-start(f16[2,64,512]{2,1,0:T(8,128)(2,1)S(1)} %get-tuple-element.41), channel_id=1, source_target_pairs={{0,6},{1,7},{2,4},{3,5},{4,2},{5,3},{6,0},{7,1},{8,14},{9,15},{10,... | collective-permute-start | bytes 393224 | tf_op jit(solution)/shard_map/ppermute | solution.py:31
  112.3 2.8 %collective-permute-start.27 = (f16[4,64,512]{2,1,0:T(8,128)(2,1)S(1)}, f16[4,64,512]{2,1,0:T(8,128)(2,1)S(1)}, u32[]{:S(2)}, u32[]{:S(2)}) collective-permute-start(f16[4,64,512]{2,1,0:T(8,128)(2,1)S(1)} %get-tuple-element.32), channel_id=1, source_target_pairs={{0,1},{1,0},{2,3},{3,2},{4,5},{5,4},{6,7},{7,6},{8,9},{9,8},{10,11... | collective-permute-start | bytes 786440 | tf_op jit(solution)/shard_map/ppermute | solution.py:31
  115.1 4.1 %collective-permute-done.35 = f16[2,64,512]{2,1,0:T(8,128)(2,1)S(1)} collective-permute-done((f16[2,64,512]{2,1,0:T(8,128)(2,1)S(1)}, f16[2,64,512]{2,1,0:T(8,128)(2,1)S(1)}, u32[]{:S(2)}, u32[]{:S(2)}) %collective-permute-start.35) | collective-permute-done | bytes 131104 | tf_op jit(solution)/shard_map/ppermute | solution.py:31
  119.7 2.9 %finish.1 = (bf16[64,8192]{1,0:T(8,128)(2,1)}, bf16[64,8192]{1,0:T(8,128)(2,1)}) custom-call(s32[2]{0:T(128)S(1)} %pad_add_fusion.place, f32[1]{0:T(128)} %bitcast.33.bound, bf16[64,8192]{1,0:T(8,128)(2,1)S(1)} %bitcast.101, bf16[1,8192]{1,0:T(2,128)(2,1)S(1)} %broadcast_in_dim.37.gain, f32[8,64,512]{2,1,0:T(8,128)S(1)} %bitcast.103, ...), custom_call_target="tpu_custom_call" | custom-call | flops 4194304 | bytes 7340032 | tf_op jit(solution)/shard_map/finish/pallas_call | solution.py:234
  (121 shorter events, 18.3 us)
Async XLA Ops:
  1.4 17.8 %collective-permute-start.2 = (bf16[32,512]{1,0:T(8,128)(2,1)S(1)}, bf16[32,512]{1,0:T(8,128)(2,1)S(1)}, u32[]{:S(2)}, u32[]{:S(2)}) collective-permute-start(bf16[32,512]{1,0:T(8,128)(2,1)S(1)} %get-tuple-element.52), channel_id=1, source_target_pairs={{0,4},{1,5},{2,6},{3,7},{4,0},{5,1},{6,2},{7,3},{8,12},{9,13},{10,... | collective-permute-start | bytes 98312 | tf_op jit(solution)/shard_map/ppermute | solution.py:31
  5.5 15.5 %collective-permute-start.1 = (bf16[32,512]{1,0:T(8,128)(2,1)S(1)}, bf16[32,512]{1,0:T(8,128)(2,1)S(1)}, u32[]{:S(2)}, u32[]{:S(2)}) collective-permute-start(bf16[32,512]{1,0:T(8,128)(2,1)S(1)} %get-tuple-element.52), channel_id=1, source_target_pairs={{0,2},{1,3},{2,0},{3,1},{4,6},{5,7},{6,4},{7,5},{8,10},{9,11},{10,... | collective-permute-start | bytes 98312 | tf_op jit(solution)/shard_map/ppermute | solution.py:31
  7.1 16.4 %collective-permute-start.3 = (bf16[32,512]{1,0:T(8,128)(2,1)S(1)}, bf16[32,512]{1,0:T(8,128)(2,1)S(1)}, u32[]{:S(2)}, u32[]{:S(2)}) collective-permute-start(bf16[32,512]{1,0:T(8,128)(2,1)S(1)} %get-tuple-element.52), channel_id=1, source_target_pairs={{0,6},{1,7},{2,4},{3,5},{4,2},{5,3},{6,0},{7,1},{8,14},{9,15},{10,... | collective-permute-start | bytes 98312 | tf_op jit(solution)/shard_map/ppermute | solution.py:31
  7.1 11.6 %collective-permute-start.5 = (bf16[32,512]{1,0:T(8,128)(2,1)S(1)}, bf16[32,512]{1,0:T(8,128)(2,1)S(1)}, u32[]{:S(2)}, u32[]{:S(2)}) collective-permute-start(bf16[32,512]{1,0:T(8,128)(2,1)S(1)} %get-tuple-element.51), channel_id=1, source_target_pairs={{0,1},{1,0},{2,3},{3,2},{4,5},{5,4},{6,7},{7,6},{8,9},{9,8},{10,11... | collective-permute-start | bytes 98312 | tf_op jit(solution)/shard_map/ppermute | solution.py:31
  17.1 6.6 %collective-permute-start = (bf16[80,1024]{1,0:T(8,128)(2,1)S(1)}, bf16[80,1024]{1,0:T(8,128)(2,1)S(1)}, u32[]{:S(2)}, u32[]{:S(2)}) collective-permute-start(bf16[80,1024]{1,0:T(8,128)(2,1)S(1)} %pad_maximum_fusion.3), channel_id=1, source_target_pairs={{0,8},{8,0},{1,9},{9,1},{2,10},{10,2},{3,11},{11,3},{4,12},{12,4},... | collective-permute-start | bytes 491528 | tf_op jit(solution)/shard_map/ppermute | solution.py:35
  18.7 16.0 %collective-permute-start.17 = (bf16[64,4096]{1,0:T(8,128)(2,1)S(1)}, bf16[64,4096]{1,0:T(8,128)(2,1)S(1)}, u32[]{:S(2)}, u32[]{:S(2)}) collective-permute-start(bf16[64,4096]{1,0:T(8,128)(2,1)S(1)} %get-tuple-element.29), channel_id=1, source_target_pairs={{0,8},{8,0},{1,9},{9,1},{2,10},{10,2},{3,11},{11,3},{4,12},{12,4},... | collective-permute-start | bytes 1572872 | tf_op jit(solution)/shard_map/ppermute | solution.py:35
  19.2 6.9 %collective-permute-start.7 = (bf16[2,32,512]{2,1,0:T(8,128)(2,1)S(1)}, bf16[2,32,512]{2,1,0:T(8,128)(2,1)S(1)}, u32[]{:S(2)}, u32[]{:S(2)}) collective-permute-start(bf16[2,32,512]{2,1,0:T(8,128)(2,1)S(1)} %get-tuple-element.54), channel_id=1, source_target_pairs={{0,4},{1,5},{2,6},{3,7},{4,0},{5,1},{6,2},{7,3},{8,12},{9,13},{10,... | collective-permute-start | bytes 196616 | tf_op jit(solution)/shard_map/ppermute | solution.py:31
  23.5 6.1 %collective-permute-start.8 = (bf16[2,32,512]{2,1,0:T(8,128)(2,1)S(1)}, bf16[2,32,512]{2,1,0:T(8,128)(2,1)S(1)}, u32[]{:S(2)}, u32[]{:S(2)}) collective-permute-start(bf16[2,32,512]{2,1,0:T(8,128)(2,1)S(1)} %get-tuple-element.54), channel_id=1, source_target_pairs={{0,6},{1,7},{2,4},{3,5},{4,2},{5,3},{6,0},{7,1},{8,14},{9,15},{10,... | collective-permute-start | bytes 196616 | tf_op jit(solution)/shard_map/ppermute | solution.py:31
  29.6 15.1 %collective-permute-start.10 = (bf16[48,512]{1,0:T(8,128)(2,1)S(1)}, bf16[48,512]{1,0:T(8,128)(2,1)S(1)}, u32[]{:S(2)}, u32[]{:S(2)}) collective-permute-start(bf16[48,512]{1,0:T(8,128)(2,1)S(1)} %get-tuple-element.48), channel_id=1, source_target_pairs={{0,4},{1,5},{2,6},{3,7},{4,0},{5,1},{6,2},{7,3},{8,12},{9,13},{10,... | collective-permute-start | bytes 147464 | tf_op jit(solution)/shard_map/ppermute | solution.py:31
  30.6 14.1 %collective-permute-start.9 = (bf16[48,512]{1,0:T(8,128)(2,1)S(1)}, bf16[48,512]{1,0:T(8,128)(2,1)S(1)}, u32[]{:S(2)}, u32[]{:S(2)}) collective-permute-start(bf16[48,512]{1,0:T(8,128)(2,1)S(1)} %get-tuple-element.48), channel_id=1, source_target_pairs={{0,2},{1,3},{2,0},{3,1},{4,6},{5,7},{6,4},{7,5},{8,10},{9,11},{10,... | collective-permute-start | bytes 147464 | tf_op jit(solution)/shard_map/ppermute | solution.py:31
  33.1 11.6 %collective-permute-start.11 = (bf16[48,512]{1,0:T(8,128)(2,1)S(1)}, bf16[48,512]{1,0:T(8,128)(2,1)S(1)}, u32[]{:S(2)}, u32[]{:S(2)}) collective-permute-start(bf16[48,512]{1,0:T(8,128)(2,1)S(1)} %get-tuple-element.48), channel_id=1, source_target_pairs={{0,6},{1,7},{2,4},{3,5},{4,2},{5,3},{6,0},{7,1},{8,14},{9,15},{10,... | collective-permute-start | bytes 147464 | tf_op jit(solution)/shard_map/ppermute | solution.py:31
  34.1 12.3 %collective-permute-start.13 = (bf16[48,512]{1,0:T(8,128)(2,1)S(1)}, bf16[48,512]{1,0:T(8,128)(2,1)S(1)}, u32[]{:S(2)}, u32[]{:S(2)}) collective-permute-start(bf16[48,512]{1,0:T(8,128)(2,1)S(1)} %get-tuple-element.47), channel_id=1, source_target_pairs={{0,1},{1,0},{2,3},{3,2},{4,5},{5,4},{6,7},{7,6},{8,9},{9,8},{10,11... | collective-permute-start | bytes 147464 | tf_op jit(solution)/shard_map/ppermute | solution.py:31
  44.7 6.2 %collective-permute-start.18 = (f32[64,1024]{1,0:T(8,128)S(1)}, f32[64,1024]{1,0:T(8,128)S(1)}, u32[]{:S(2)}, u32[]{:S(2)}) collective-permute-start(f32[64,1024]{1,0:T(8,128)S(1)} %get-tuple-element.17), channel_id=1, source_target_pairs={{0,8},{8,0},{1,9},{9,1},{2,10},{10,2},{3,11},{11,3},{4,12},{12,4},... | collective-permute-start | bytes 786440 | tf_op jit(solution)/shard_map/ppermute | solution.py:35
  44.8 12.3 %collective-permute-start.12 = (bf16[4,48,512]{2,1,0:T(8,128)(2,1)S(1)}, bf16[4,48,512]{2,1,0:T(8,128)(2,1)S(1)}, u32[]{:S(2)}, u32[]{:S(2)}) collective-permute-start(bf16[4,48,512]{2,1,0:T(8,128)(2,1)S(1)} %get-tuple-element.37), channel_id=1, source_target_pairs={{0,1},{1,0},{2,3},{3,2},{4,5},{5,4},{6,7},{7,6},{8,9},{9,8},{10,11... | collective-permute-start | bytes 589832 | tf_op jit(solution)/shard_map/ppermute | solution.py:31
  46.4 10.7 %collective-permute-start.15 = (bf16[2,48,512]{2,1,0:T(8,128)(2,1)S(1)}, bf16[2,48,512]{2,1,0:T(8,128)(2,1)S(1)}, u32[]{:S(2)}, u32[]{:S(2)}) collective-permute-start(bf16[2,48,512]{2,1,0:T(8,128)(2,1)S(1)} %get-tuple-element.45), channel_id=1, source_target_pairs={{0,4},{1,5},{2,6},{3,7},{4,0},{5,1},{6,2},{7,3},{8,12},{9,13},{10,... | collective-permute-start | bytes 294920 | tf_op jit(solution)/shard_map/ppermute | solution.py:31
  46.9 10.1 %collective-permute-start.14 = (bf16[2,48,512]{2,1,0:T(8,128)(2,1)S(1)}, bf16[2,48,512]{2,1,0:T(8,128)(2,1)S(1)}, u32[]{:S(2)}, u32[]{:S(2)}) collective-permute-start(bf16[2,48,512]{2,1,0:T(8,128)(2,1)S(1)} %get-tuple-element.45), channel_id=1, source_target_pairs={{0,2},{1,3},{2,0},{3,1},{4,6},{5,7},{6,4},{7,5},{8,10},{9,11},{10,... | collective-permute-start | bytes 294920 | tf_op jit(solution)/shard_map/ppermute | solution.py:31
  49.8 7.2 %collective-permute-start.16 = (bf16[2,48,512]{2,1,0:T(8,128)(2,1)S(1)}, bf16[2,48,512]{2,1,0:T(8,128)(2,1)S(1)}, u32[]{:S(2)}, u32[]{:S(2)}) collective-permute-start(bf16[2,48,512]{2,1,0:T(8,128)(2,1)S(1)} %get-tuple-element.45), channel_id=1, source_target_pairs={{0,6},{1,7},{2,4},{3,5},{4,2},{5,3},{6,0},{7,1},{8,14},{9,15},{10,... | collective-permute-start | bytes 294920 | tf_op jit(solution)/shard_map/ppermute | solution.py:31
  69.1 6.1 %collective-permute-start.28 = (f16[2,64,512]{2,1,0:T(8,128)(2,1)S(1)}, f16[2,64,512]{2,1,0:T(8,128)(2,1)S(1)}, u32[]{:S(2)}, u32[]{:S(2)}) collective-permute-start(f16[2,64,512]{2,1,0:T(8,128)(2,1)S(1)} %get-tuple-element.26), channel_id=1, source_target_pairs={{0,2},{1,3},{2,0},{3,1},{4,6},{5,7},{6,4},{7,5},{8,10},{9,11},{10,... | collective-permute-start | bytes 393224 | tf_op jit(solution)/shard_map/ppermute | solution.py:31
  71.2 8.6 %collective-permute-start.30 = (f16[2,64,512]{2,1,0:T(8,128)(2,1)S(1)}, f16[2,64,512]{2,1,0:T(8,128)(2,1)S(1)}, u32[]{:S(2)}, u32[]{:S(2)}) collective-permute-start(f16[2,64,512]{2,1,0:T(8,128)(2,1)S(1)} %get-tuple-element.27), channel_id=1, source_target_pairs={{0,6},{1,7},{2,4},{3,5},{4,2},{5,3},{6,0},{7,1},{8,14},{9,15},{10,... | collective-permute-start | bytes 393224 | tf_op jit(solution)/shard_map/ppermute | solution.py:31
  72.6 12.2 %collective-permute-start.29 = (f16[2,64,512]{2,1,0:T(8,128)(2,1)S(1)}, f16[2,64,512]{2,1,0:T(8,128)(2,1)S(1)}, u32[]{:S(2)}, u32[]{:S(2)}) collective-permute-start(f16[2,64,512]{2,1,0:T(8,128)(2,1)S(1)} %get-tuple-element.28), channel_id=1, source_target_pairs={{0,4},{1,5},{2,6},{3,7},{4,0},{5,1},{6,2},{7,3},{8,12},{9,13},{10,... | collective-permute-start | bytes 393224 | tf_op jit(solution)/shard_map/ppermute | solution.py:31
  85.6 8.5 %collective-permute-start.20 = (f16[4,64,512]{2,1,0:T(8,128)(2,1)S(1)}, f16[4,64,512]{2,1,0:T(8,128)(2,1)S(1)}, u32[]{:S(2)}, u32[]{:S(2)}) collective-permute-start(f16[4,64,512]{2,1,0:T(8,128)(2,1)S(1)} %fusion), channel_id=1, source_target_pairs={{0,1},{1,0},{2,3},{3,2},{4,5},{5,4},{6,7},{7,6},{8,9},{9,8},{10,11... | collective-permute-start | bytes 786440 | tf_op jit(solution)/shard_map/ppermute | solution.py:31
  90.0 7.7 %collective-permute-start.32 = (f16[64,512]{1,0:T(8,128)(2,1)S(1)}, f16[64,512]{1,0:T(8,128)(2,1)S(1)}, u32[]{:S(2)}, u32[]{:S(2)}) collective-permute-start(f16[64,512]{1,0:T(8,128)(2,1)S(1)} %fusion.5), channel_id=1, source_target_pairs={{0,8},{8,0},{1,9},{9,1},{2,10},{10,2},{3,11},{11,3},{4,12},{12,4},... | collective-permute-start | bytes 196616 | tf_op jit(solution)/shard_map/ppermute | solution.py:35
  94.3 6.2 %collective-permute-start.23 = (f16[64,512]{1,0:T(8,128)(2,1)S(1)}, f16[64,512]{1,0:T(8,128)(2,1)S(1)}, u32[]{:S(2)}, u32[]{:S(2)}) collective-permute-start(f16[64,512]{1,0:T(8,128)(2,1)S(1)} %get-tuple-element.34), channel_id=1, source_target_pairs={{0,6},{1,7},{2,4},{3,5},{4,2},{5,3},{6,0},{7,1},{8,14},{9,15},{10,... | collective-permute-start | bytes 196616 | tf_op jit(solution)/shard_map/ppermute | solution.py:31
  96.9 5.9 %collective-permute-start.22 = (f16[64,512]{1,0:T(8,128)(2,1)S(1)}, f16[64,512]{1,0:T(8,128)(2,1)S(1)}, u32[]{:S(2)}, u32[]{:S(2)}) collective-permute-start(f16[64,512]{1,0:T(8,128)(2,1)S(1)} %get-tuple-element.35), channel_id=1, source_target_pairs={{0,4},{1,5},{2,6},{3,7},{4,0},{5,1},{6,2},{7,3},{8,12},{9,13},{10,... | collective-permute-start | bytes 196616 | tf_op jit(solution)/shard_map/ppermute | solution.py:31
  97.7 9.6 %collective-permute-start.33 = (f16[64,512]{1,0:T(8,128)(2,1)S(1)}, f16[64,512]{1,0:T(8,128)(2,1)S(1)}, u32[]{:S(2)}, u32[]{:S(2)}) collective-permute-start(f16[64,512]{1,0:T(8,128)(2,1)S(1)} %collective-permute-done.32), channel_id=1, source_target_pairs={{0,1},{1,0},{2,3},{3,2},{4,5},{5,4},{6,7},{7,6},{8,9},{9,8},{10,11... | collective-permute-start | bytes 196616 | tf_op jit(solution)/shard_map/ppermute | solution.py:31
  102.9 7.3 %collective-permute-start.26 = (f16[64,512]{1,0:T(8,128)(2,1)S(1)}, f16[64,512]{1,0:T(8,128)(2,1)S(1)}, u32[]{:S(2)}, u32[]{:S(2)}) collective-permute-start(f16[64,512]{1,0:T(8,128)(2,1)S(1)} %fusion.7), channel_id=1, source_target_pairs={{0,6},{1,7},{2,4},{3,5},{4,2},{5,3},{6,0},{7,1},{8,14},{9,15},{10,... | collective-permute-start | bytes 196616 | tf_op jit(solution)/shard_map/ppermute | solution.py:31
  105.1 7.0 %collective-permute-start.25 = (f16[64,512]{1,0:T(8,128)(2,1)S(1)}, f16[64,512]{1,0:T(8,128)(2,1)S(1)}, u32[]{:S(2)}, u32[]{:S(2)}) collective-permute-start(f16[64,512]{1,0:T(8,128)(2,1)S(1)} %fusion.7), channel_id=1, source_target_pairs={{0,4},{1,5},{2,6},{3,7},{4,0},{5,1},{6,2},{7,3},{8,12},{9,13},{10,... | collective-permute-start | bytes 196616 | tf_op jit(solution)/shard_map/ppermute | solution.py:31
  105.1 7.0 %collective-permute-start.24 = (f16[64,512]{1,0:T(8,128)(2,1)S(1)}, f16[64,512]{1,0:T(8,128)(2,1)S(1)}, u32[]{:S(2)}, u32[]{:S(2)}) collective-permute-start(f16[64,512]{1,0:T(8,128)(2,1)S(1)} %fusion.7), channel_id=1, source_target_pairs={{0,2},{1,3},{2,0},{3,1},{4,6},{5,7},{6,4},{7,5},{8,10},{9,11},{10,... | collective-permute-start | bytes 196616 | tf_op jit(solution)/shard_map/ppermute | solution.py:31
  107.4 11.8 %collective-permute-start.35 = (f16[2,64,512]{2,1,0:T(8,128)(2,1)S(1)}, f16[2,64,512]{2,1,0:T(8,128)(2,1)S(1)}, u32[]{:S(2)}, u32[]{:S(2)}) collective-permute-start(f16[2,64,512]{2,1,0:T(8,128)(2,1)S(1)} %get-tuple-element.41), channel_id=1, source_target_pairs={{0,4},{1,5},{2,6},{3,7},{4,0},{5,1},{6,2},{7,3},{8,12},{9,13},{10,... | collective-permute-start | bytes 393224 | tf_op jit(solution)/shard_map/ppermute | solution.py:31
  108.2 11.0 %collective-permute-start.34 = (f16[2,64,512]{2,1,0:T(8,128)(2,1)S(1)}, f16[2,64,512]{2,1,0:T(8,128)(2,1)S(1)}, u32[]{:S(2)}, u32[]{:S(2)}) collective-permute-start(f16[2,64,512]{2,1,0:T(8,128)(2,1)S(1)} %get-tuple-element.41), channel_id=1, source_target_pairs={{0,2},{1,3},{2,0},{3,1},{4,6},{5,7},{6,4},{7,5},{8,10},{9,11},{10,... | collective-permute-start | bytes 393224 | tf_op jit(solution)/shard_map/ppermute | solution.py:31
  110.2 9.0 %collective-permute-start.36 = (f16[2,64,512]{2,1,0:T(8,128)(2,1)S(1)}, f16[2,64,512]{2,1,0:T(8,128)(2,1)S(1)}, u32[]{:S(2)}, u32[]{:S(2)}) collective-permute-start(f16[2,64,512]{2,1,0:T(8,128)(2,1)S(1)} %get-tuple-element.41), channel_id=1, source_target_pairs={{0,6},{1,7},{2,4},{3,5},{4,2},{5,3},{6,0},{7,1},{8,14},{9,15},{10,... | collective-permute-start | bytes 393224 | tf_op jit(solution)/shard_map/ppermute | solution.py:31
  112.3 7.2 %collective-permute-start.27 = (f16[4,64,512]{2,1,0:T(8,128)(2,1)S(1)}, f16[4,64,512]{2,1,0:T(8,128)(2,1)S(1)}, u32[]{:S(2)}, u32[]{:S(2)}) collective-permute-start(f16[4,64,512]{2,1,0:T(8,128)(2,1)S(1)} %get-tuple-element.32), channel_id=1, source_target_pairs={{0,1},{1,0},{2,3},{3,2},{4,5},{5,4},{6,7},{7,6},{8,9},{9,8},{10,11... | collective-permute-start | bytes 786440 | tf_op jit(solution)/shard_map/ppermute | solution.py:31
  (18 other events, 136.1 us)

commit v2 on v1

v2 whole, which is shorter than its diff:
```python
import functools

import jax
import jax.numpy as jnp
import numpy as np
from jax import lax
from jax.experimental import pallas as pl
from jax.experimental.pallas import tpu as pltpu
from jax.sharding import PartitionSpec as P

NORM_EPS = 1e-06
ROPE_BASE = 1000000.0
ADAPTER_SCALE = 0.5
MIB = 1024 * 1024
BF16 = jnp.bfloat16
F16 = jnp.float16
F32 = jnp.float32
SWAP = [(0, 1), (1, 0)]


def params(room):
    return pltpu.CompilerParams(vmem_limit_bytes=room * MIB)


def cost(flops, read):
    return pl.CostEstimate(flops=flops, bytes_accessed=read, transcendentals=0)


def hop(value, distance):
    total = lax.axis_size("tp")
    return lax.ppermute(value, "tp", [(i, i ^ distance) for i in range(total)])


def swap(value):
    return lax.ppermute(value, "fsdp", SWAP)


def contract_first(left, right):
    return lax.dot_general(left, right, (((0,), (0,)), ((), ())), preferred_element_type=F32)


VMEM = pl.BlockSpec(memory_space=pltpu.VMEM)
SMEM = pl.BlockSpec(memory_space=pltpu.SMEM)
ANY = pl.BlockSpec(memory_space=pl.ANY)


def in_vmem(value):
    return pltpu.with_memory_space_constraint(value, pltpu.VMEM)


def in_hbm(value):
    return pltpu.with_memory_space_constraint(value, pltpu.HBM)


def fetch_kernel(source, target, arrived):
    copy = pltpu.make_async_copy(source, target, arrived)
    copy.start()
    copy.wait()


def fetch(value, name):
    return pl.pallas_call(
        fetch_kernel,
        in_specs=[ANY],
        out_specs=VMEM,
        out_shape=pltpu.VMEM(value.shape, value.dtype),
        scratch_shapes=[pltpu.SemaphoreType.DMA],
        compiler_params=params(2),
        cost_estimate=cost(0, 2 * value.size),
        name=name,
    )(in_hbm(value))


def reach_kernel(lengths, values, bound, held, arrived):
    rows, slots, head_dim = values.shape
    copies = [
        pltpu.make_async_copy(values.at[row], held.at[row], arrived.at[row]) for row in range(rows)
    ]
    for copy in copies:
        copy.start()
    slot = lax.broadcasted_iota(jnp.int32, (slots, head_dim), 0)
    top = jnp.zeros((8, head_dim), F32)
    for row in range(rows):
        copies[row].wait()
        size = jnp.where(slot < lengths[row], jnp.abs(held[row].astype(F32)), 0.0)
        top = jnp.maximum(top, jnp.max(size.reshape(-1, 8, head_dim), axis=0))
    bound[...] = jnp.broadcast_to(jnp.max(top), bound.shape).astype(BF16)


def largest_in_reach(lengths, values, columns):
    return pl.pallas_call(
        reach_kernel,
        in_specs=[SMEM, ANY],
        out_specs=VMEM,
        out_shape=jax.ShapeDtypeStruct((16, columns), BF16),
        scratch_shapes=[
            pltpu.VMEM(values.shape, BF16),
            pltpu.SemaphoreType.DMA((values.shape[0],)),
        ],
        compiler_params=params(8),
        cost_estimate=cost(4 * values.size, 2 * values.size),
        name="largest_in_reach",
    )(lengths, in_hbm(values))


def query_kernel(
    place, near, far, upper, base, mine, theirs, effective, own, other, fresh, total, left
):
    outer, _, depth = near.shape
    rows = mine.shape[0]
    total[...] = jnp.zeros_like(total)

    def pair(z, _):
        for y, lower in ((0, near), (1, far)):
            start = pl.multiple_of(((2 * z + y) ^ place[0]) * depth, depth)
            block = pl.ds(start, depth)
            out = pltpu.make_async_copy(fresh.at[y], effective.at[block], left.at[y])

            @pl.when(z > 0)
            def _():
                out.wait()

            update = contract_first(lower[z], upper[...])
            fresh[y] = (base[block, :].astype(F32) + update).astype(BF16)
            out.start()
            both = jnp.concatenate([mine[:, block], theirs[:, block]], axis=0)
            total[...] += jnp.dot(both, fresh[y], preferred_element_type=F32)
        return 0

    lax.fori_loop(0, outer, pair, 0)
    own[...] = total[:rows]
    other[...] = total[rows:]
    for y in range(2):
        pltpu.make_async_copy(fresh.at[y], effective.at[pl.ds(0, depth)], left.at[y]).wait()


def query_project(place, near, far, upper, base, mine, theirs):
    depth = near.shape[2]
    width = base.shape[1]
    rows = mine.shape[0]
    return pl.pallas_call(
        query_kernel,
        in_specs=[SMEM] + [VMEM] * 6,
        out_specs=[ANY, VMEM, VMEM],
        out_shape=[
            jax.ShapeDtypeStruct(base.shape, BF16),
            jax.ShapeDtypeStruct((rows, width), F32),
            jax.ShapeDtypeStruct((rows, width), F32),
        ],
        scratch_shapes=[
            pltpu.VMEM((2, depth, width), BF16),
            pltpu.VMEM((2 * rows, width), F32),
            pltpu.SemaphoreType.DMA((2,)),
        ],
        compiler_params=params(14),
        cost_estimate=cost(2 * base.size * (near.shape[1] + 2 * rows), 2 * base.size),
        name="query_project",
    )(place, near, far, upper, in_vmem(base), mine, theirs)


def attend_kernel(
    steps, scale, lengths, own, other, bias, cosine, sine, keys, values, context,
    keys_held, values_held, arrived
):
    rows, slots, head_dim = keys.shape
    heads = own.shape[1] // head_dim
    group = 2
    copies = []
    for row in range(rows):
        copies.append(
            [
                pltpu.make_async_copy(keys.at[row], keys_held.at[row], arrived.at[0, row]),
                pltpu.make_async_copy(values.at[row], values_held.at[row], arrived.at[1, row]),
            ]
        )
        for copy in copies[row]:
            copy.start()
    slot = lax.broadcasted_iota(jnp.int32, (heads * steps, slots), 1)
    step = lax.broadcasted_iota(jnp.int32, (heads * steps, slots), 0) % steps
    behind = slot - step
    for first in range(0, rows, group):
        span = slice(first * steps, (first + group) * steps)
        query = (own[span] + other[span]) * scale + bias[...].astype(F32)
        turned = []
        for head in range(heads):
            part = query[:, head * head_dim : (head + 1) * head_dim]
            part = part * cosine[span] + pltpu.roll(part, head_dim // 2, 1) * sine[span]
            turned.append(part * head_dim ** (-0.5))
        gathered = []
        for row in range(group):
            for copy in copies[first + row]:
                copy.wait()
            queries = jnp.concatenate(
                [q[row * steps : (row + 1) * steps] for q in turned], axis=0
            ).astype(BF16)
            scores = lax.dot_general(
                queries,
                keys_held[first + row],
                (((1,), (1,)), ((), ())),
                preferred_element_type=F32,
            )
            scores = jnp.where(behind <= lengths[first + row] - steps, scores, F32(-1e30))
            top = jnp.max(scores, axis=-1, keepdims=True)
            weights = jnp.exp(scores - top)
            probs = (weights / jnp.sum(weights, axis=-1, keepdims=True)).astype(BF16)
            gathered.append(
                jnp.dot(probs, values_held[first + row], preferred_element_type=F32)
            )
        for head in range(heads):
            context[span, head * head_dim : (head + 1) * head_dim] = jnp.concatenate(
                [g[head * steps : (head + 1) * steps] for g in gathered], axis=0
            ).astype(BF16)


def attend(lengths, own, other, bias, cosine, sine, keys, values, steps, scale):
    rows = keys.shape[0]
    width = own.shape[1]
    return pl.pallas_call(
        functools.partial(attend_kernel, steps, scale),
        in_specs=[SMEM] + [VMEM] * 5 + [ANY] * 2,
        out_specs=VMEM,
        out_shape=jax.ShapeDtypeStruct((rows * steps, width), BF16),
        scratch_shapes=[
            pltpu.VMEM(keys.shape, BF16),
            pltpu.VMEM(values.shape, BF16),
            pltpu.SemaphoreType.DMA((2, rows)),
        ],
        compiler_params=params(18),
        cost_estimate=cost(4 * keys.size * width // keys.shape[2] * steps, 4 * keys.size),
        name="attend",
    )(lengths, own, other, bias, cosine, sine, in_hbm(keys), in_hbm(values))


def output_kernel(
    place, lower, upper, base, mine, theirs, effective, own, other, held, fresh, arrived, left
):
    outer = upper.shape[0]
    rank = lower.shape[0]
    width = upper.shape[3]
    rows = mine.shape[0]

    def columns(k):
        return pl.ds(pl.multiple_of((k ^ place[0]) * width, width), width)

    def fetch(k):
        return pltpu.make_async_copy(base.at[:, columns(k)], held.at[k], arrived.at[k])

    def ask(k, _):
        fetch(k).start()
        return 0

    lax.fori_loop(0, 2 * outer, ask, 0)
    both = jnp.concatenate([mine[...], theirs[...]], axis=0)

    def pair(z, _):
        for y in range(2):
            k = 2 * z + y
            out = pltpu.make_async_copy(fresh.at[y], effective.at[:, columns(k)], left.at[y])

            @pl.when(z > 0)
            def _():
                out.wait()

            update = contract_first(lower[...], upper[z, y, :rank])
            fetch(k).wait()
            fresh[y] = (held[k].astype(F32) + update).astype(BF16)
            out.start()
            product = jnp.dot(both, fresh[y], preferred_element_type=F32)
            own[y, z] = product[:rows]
            other[z, y] = product[rows:]
        return 0

    lax.fori_loop(0, outer, pair, 0)
    for y in range(2):
        pltpu.make_async_copy(fresh.at[y], effective.at[:, pl.ds(0, width)], left.at[y]).wait()


def output_project(place, lower, upper, base, mine, theirs):
    outer = upper.shape[0]
    width = upper.shape[3]
    depth = base.shape[0]
    rows = mine.shape[0]
    return pl.pallas_call(
        output_kernel,
        in_specs=[SMEM, VMEM, VMEM, ANY, VMEM, VMEM],
        out_specs=[ANY, VMEM, VMEM],
        out_shape=[
            jax.ShapeDtypeStruct(base.shape, BF16),
            jax.ShapeDtypeStruct((2, outer, rows, width), F32),
            jax.ShapeDtypeStruct((outer, 2, rows, width), F32),
        ],
        scratch_shapes=[
            pltpu.VMEM((2 * outer, depth, width), BF16),
            pltpu.VMEM((2, depth, width), BF16),
            pltpu.SemaphoreType.DMA((2 * outer,)),
            pltpu.SemaphoreType.DMA((2,)),
        ],
        compiler_params=params(24),
        cost_estimate=cost(2 * base.size * (lower.shape[0] + 2 * rows), 4 * base.size),
        name="output_project",
    )(place, lower, upper, in_hbm(base), mine, theirs)


def finish_kernel(place, bound, hidden, gain, near, far, residual, normed, combined):
    blocks, rows, width = near.shape
    half = blocks * width
    squares = jnp.zeros((rows, 1), F32)
    for pieces, which in ((near, place[1]), (far, 1 - place[1])):
        for k in range(blocks):
            start = pl.multiple_of(which * half + (place[0] ^ k) * width, width)
            total = hidden[:, pl.ds(start, width)].astype(F32) + pieces[k] * bound[0]
            combined[:, pl.ds(start, width)] = total
            residual[:, pl.ds(start, width)] = total.astype(BF16)
            squares += jnp.sum(total * total, axis=-1, keepdims=True)
    inverse = lax.rsqrt(squares / (2 * half) + NORM_EPS)
    normed[...] = (combined[...] * inverse * gain[...].astype(F32)).astype(BF16)


def finish(place, bound, hidden, gain, near, far):
    rows, whole = hidden.shape
    blocks, _, width = near.shape
    tall = 16
    spec = pltpu.PrefetchScalarGridSpec(
        num_scalar_prefetch=2,
        grid=(rows // tall,),
        in_specs=[
            pl.BlockSpec((tall, whole), lambda r, p, b: (r, 0)),
            pl.BlockSpec((1, whole), lambda r, p, b: (0, 0)),
            pl.BlockSpec((blocks, tall, width), lambda r, p, b: (0, r, 0)),
            pl.BlockSpec((blocks, tall, width), lambda r, p, b: (0, r, 0)),
        ],
        out_specs=[
            pl.BlockSpec((tall, whole), lambda r, p, b: (r, 0)),
            pl.BlockSpec((tall, whole), lambda r, p, b: (r, 0)),
        ],
        scratch_shapes=[pltpu.VMEM((tall, whole), F32)],
    )
    return pl.pallas_call(
        finish_kernel,
        grid_spec=spec,
        out_shape=[jax.ShapeDtypeStruct((rows, whole), BF16)] * 2,
        compiler_params=params(14),
        cost_estimate=cost(8 * hidden.size, 14 * hidden.size),
        name="finish",
    )(place, bound, hidden, gain, near, far)


def cross(value):
    total = lax.axis_size("tp")
    pairs = [(f * total + i, (1 - f) * total + (i ^ 1)) for f in range(2) for i in range(total)]
    return lax.ppermute(value, ("fsdp", "tp"), pairs)


def along_z(value):
    outer = lax.axis_size("tp") // 2
    return jnp.stack([value] + [hop(value, 2 * k) for k in range(1, outer)])


def along_y(value):
    return jnp.stack([value, hop(value, 1)])


def reduce_blocks(own, other, shrink):
    outer = other.shape[0]

    def narrow(value):
        return value.astype(F16)

    across = hop(narrow(shrink(own[1])), 1)
    arrived = [hop(narrow(shrink(other[k])), 2 * k) for k in range(1, outer)]
    summed = shrink(own[0]) + across.astype(F32)
    ended = [hop(narrow(summed[k]), 2 * k) for k in range(1, outer)]
    arrived, ended = lax.optimization_barrier((arrived, ended))
    total = summed[0] + sum(e.astype(F32) for e in ended)
    pair = narrow(shrink(other[0]) + sum(a.astype(F32) for a in arrived))
    far = swap(pair[0]).astype(F32) + cross(pair[1]).astype(F32)
    return narrow(total), narrow(far)


def local(
    hidden_in,
    input_gain,
    post_gain,
    query_base_weight,
    query_bias,
    output_base_weight,
    query_lower_factor,
    query_upper_factor,
    output_lower_factor,
    output_upper_factor,
    cache_keys,
    cache_values,
    cache_lengths,
):
    rows, steps, width = hidden_in.shape
    tall = rows * steps
    half = width // 2
    slots, head_dim = cache_keys.shape[2:]
    features = query_base_weight.shape[1] * lax.axis_size("tp")
    t = lax.axis_index("tp").astype(jnp.int32)
    f = lax.axis_index("fsdp").astype(jnp.int32)
    place = jnp.stack([t, f])
    outer = lax.axis_size("tp") // 2

    lower_near = along_z(query_lower_factor.T)
    lower_far = hop(lower_near, 1)

    flat = hidden_in.reshape(tall, width)
    inputs32 = flat.astype(F32)
    mean_square = jnp.mean(inputs32 * inputs32, axis=-1, keepdims=True)
    normed = (inputs32 * lax.rsqrt(mean_square + NORM_EPS) * input_gain.astype(F32)).astype(BF16)
    mine = lax.dynamic_slice_in_dim(normed, f * half, half, 1)
    theirs = swap(lax.dynamic_slice_in_dim(normed, (1 - f) * half, half, 1))

    columns = query_upper_factor.shape[1]
    bound = largest_in_reach(cache_lengths, cache_values[:, 0], columns)
    rank_part = query_upper_factor.shape[0]
    sent = jnp.concatenate([query_upper_factor, output_lower_factor.T, bound], axis=0)
    came = swap(sent)

    def in_order(a, b):
        return jnp.where(f == 0, jnp.concatenate([a, b]), jnp.concatenate([b, a]))

    upper = in_order(sent[:rank_part], came[:rank_part]) * BF16(ADAPTER_SCALE)
    lower_o = in_order(sent[rank_part : 2 * rank_part], came[rank_part : 2 * rank_part])
    lower_o = lower_o * BF16(ADAPTER_SCALE)
    bound = jnp.maximum(sent[2 * rank_part :], came[2 * rank_part :])

    rank, block = output_upper_factor.shape
    message = jnp.concatenate([output_upper_factor, bound[:, :block]], axis=0)
    upper_o = along_z(along_y(message))
    bound = jnp.max(upper_o[:, :, rank:]).astype(F32)

    weight_q, _ = lax.optimization_barrier((query_base_weight, lower_near))
    query_effective, own, other = query_project(
        t[None], lower_near, lower_far, upper, fetch(weight_q, "fetch_query"), mine, theirs
    )
    other = swap(other)

    inverse = ROPE_BASE ** (-(np.arange(head_dim // 2) * 2.0) / head_dim)
    inverse = jnp.asarray(inverse.astype(np.float32))
    positions = cache_lengths[:, None] - steps + jnp.arange(steps, dtype=jnp.int32)[None, :]
    angles = positions.astype(F32).reshape(tall, 1) * inverse
    cosine, sine = jnp.cos(angles), jnp.sin(angles)
    context = attend(
        cache_lengths,
        own,
        other,
        query_bias[None, :],
        jnp.concatenate([cosine, cosine], axis=1),
        jnp.concatenate([-sine, sine], axis=1),
        cache_keys[:, 0],
        cache_values[:, 0],
        steps,
        width ** (-0.5),
    )

    output_effective, own, other = output_project(
        t[None], lower_o, upper_o, output_base_weight, context, swap(context)
    )

    small = 2.0**-16
    unit = jnp.maximum(bound, 1e-30) * small
    shrink_by = 1.0 / unit

    def shrink(value):
        return (value * shrink_by) * (features ** (-0.5) * small)

    near, far = reduce_blocks(own, other, shrink)

    near = along_z(near)
    near = jnp.stack([near, hop(near, 1)], axis=1)
    far = along_z(along_y(far))
    near = near.reshape((2 * outer,) + near.shape[2:]).astype(F32)
    far = far.reshape((2 * outer,) + far.shape[2:]).astype(F32)

    residual, normed_out = finish(
        place, jnp.maximum(bound, 1e-30)[None], flat, post_gain[None, :], near, far
    )
    return (
        residual.reshape(hidden_in.shape),
        normed_out.reshape(hidden_in.shape),
        query_effective,
        output_effective,
    )


def solution(mesh):
    in_specs = (
        P(("groups", "fsdp"), None, None),
        P(),
        P(),
        P("fsdp", "tp"),
        P("tp"),
        P("tp", "fsdp"),
        P(("fsdp", "tp"), None),
        P("fsdp", "tp"),
        P("tp", "fsdp"),
        P(None, ("fsdp", "tp")),
        P(("groups", "fsdp"), "tp", None, None),
        P(("groups", "fsdp"), "tp", None, None),
        P(("groups", "fsdp")),
    )
    out_specs = (
        P(("groups", "fsdp"), None, None),
        P(("groups", "fsdp"), None, None),
        P(("groups", "fsdp"), "tp"),
        P(("groups", "tp"), "fsdp"),
    )
    return jax.shard_map(local, mesh=mesh, in_specs=in_specs, out_specs=out_specs, check_vma=False)
```

time: 123 us -> 104 us (0.85)
  Pallas kernels: 22.6 us -> 33.1 us
  other arithmetic: 11.2 us -> 2.97 us
  starting transfers between devices: 46.5 us -> 38.7 us
  local copies, waits for them, and re-layouts: 8.84 us -> 1.12 us
  waiting for transfers between devices: 31.6 us -> 25.6 us
    pallas_call x3 -> x5, Pallas kernels: 19.7 us -> 30.2 us  [the longest x1 8.68 us: output_project(): pl.pallas_call(output_kernel, in_specs=[SMEM, VMEM, VMEM, ANY, VMEM, VMEM...]
    ppermute x32 -> x23, waiting for transfers between devices: 31.6 us -> 22.2 us  [hop(): return lax.ppermute(value, 'tp', [(i, i ^ distance) for i in range(total)])]
    ppermute x32 -> x23, starting transfers between devices: 45.7 us -> 37.4 us  [hop(): return lax.ppermute(value, 'tp', [(i, i ^ distance) for i in range(total)])]
    reduce_max x2 -> x1, other arithmetic: 7.48 us -> 0.67 us  [local(): bound = jnp.max(upper_o[:, :, rank:]).astype(F32)]
    unnamed x26 -> x22, local copies, waits for them, and re-layouts: 6.98 us -> 0.7 us
    ppermute x0 -> x1, waiting for transfers between devices: none -> 2.65 us  [cross(): return lax.ppermute(value, ('fsdp', 'tp'), pairs)]
  transfers between devices with their start and end apart: 37 -> 29, of which waited for: 11 -> 11; matrix products, arithmetic and copies ran while one was open for 10% -> 3% of each run, Pallas kernels for 10% -> 21%
where the time goes in v2:
time: 104 us; the launch traced here: 103 us
  starting transfers between devices  38.7 us (37%)
  Pallas kernels  33.1 us (32%)
  waiting for transfers between devices  25.6 us (25%)
  other arithmetic  2.97 us (3%)
  between operations  1.8 us (2%)
  local copies, waits for them, and re-layouts  1.12 us (1%)
    ppermute x23, starting transfers between devices, hop(): return lax.ppermute(value, 'tp', [(i, i ^ distance) for i in range(total)])  37.4 us
    ppermute x23, waiting for transfers between devices, hop(): return lax.ppermute(value, 'tp', [(i, i ^ distance) for i in range(total)])  22.2 us
    pallas_call x1, Pallas kernels, output_project(): pl.pallas_call(output_kernel, in_specs=[SMEM, VMEM, VMEM, ANY, VMEM, VMEM...  8.68 us
    pallas_call x1, Pallas kernels, attend(): pl.pallas_call(functools.partial(attend_kernel, steps, scale), in_specs=[...  7.69 us
    pallas_call x1, Pallas kernels, query_project(): pl.pallas_call(query_kernel, in_specs=[SMEM] + [VMEM] * 6, out_specs=[ANY...  6.46 us
    pallas_call x1, Pallas kernels, largest_in_reach(): pl.pallas_call(reach_kernel, in_specs=[SMEM, ANY], out_specs=VMEM, out_sh...  3.94 us
    pallas_call x1, Pallas kernels, fetch(): pl.pallas_call(fetch_kernel, in_specs=[ANY], out_specs=VMEM, out_shape=pl...  3.39 us
    pallas_call x1, Pallas kernels, finish(): pl.pallas_call(finish_kernel, grid_spec=spec, out_shape=[jax.ShapeDtypeSt...  2.94 us
  transfers between devices with their start and end apart: 29, of which 11 were waited for; matrix products, arithmetic and copies ran while one was open for 3% of the time, Pallas kernels for 21%

profile of v2, /device:TPU:0, one launch (start us, length us, event | category | flops | bytes accessed | tf_op | source)
XLA Modules:
  0.0 103.3 jit_solution(12950938410683894060)
XLA Ops:
  0.6 4.1 %collective-permute-start.6 = (bf16[64,512]{1,0:T(8,128)(2,1)}, bf16[64,512]{1,0:T(8,128)(2,1)S(1)}, u32[]{:S(2)}, u32[]{:S(2)}) collective-permute-start(bf16[64,512]{1,0:T(8,128)(2,1)} %bitcast.94), channel_id=1, source_target_pairs={{0,4},{1,5},{2,6},{3,7},{4,0},{5,1},{6,2},{7,3},{8,12},{9,13},{10,... | collective-permute-start | bytes 196616 | tf_op jit(solution)/shard_map/ppermute | solution.py:31
  4.7 1.6 %collective-permute-start.5 = (bf16[64,512]{1,0:T(8,128)(2,1)}, bf16[64,512]{1,0:T(8,128)(2,1)S(1)}, u32[]{:S(2)}, u32[]{:S(2)}) collective-permute-start(bf16[64,512]{1,0:T(8,128)(2,1)} %bitcast.95), channel_id=1, source_target_pairs={{0,2},{1,3},{2,0},{3,1},{4,6},{5,7},{6,4},{7,5},{8,10},{9,11},{10,... | collective-permute-start | bytes 196616 | tf_op jit(solution)/shard_map/ppermute | solution.py:31
  7.0 3.9 %largest_in_reach.1 = bf16[16,1024]{1,0:T(8,128)(2,1)S(1)} custom-call(s32[8]{0:T(128)S(1)} %copy-done.1, bf16[8,2048,128]{2,1,0:T(8,128)(2,1)} %bitcast.75), custom_call_target="tpu_custom_call" | custom-call | flops 8388608 | bytes 4194304 | tf_op jit(solution)/shard_map/largest_in_reach/pallas_call | solution.py:91
  12.9 1.8 %collective-permute-start.8 = (bf16[4,64,512]{2,1,0:T(8,128)(2,1)S(1)}, bf16[4,64,512]{2,1,0:T(8,128)(2,1)S(1)}, u32[]{:S(2)}, u32[]{:S(2)}) collective-permute-start(bf16[4,64,512]{2,1,0:T(8,128)(2,1)S(1)} %pad_maximum_fusion.2.near), channel_id=1, source_target_pairs={{0,1},{1,0},{2,3},{3,2},{4,5},{5,4},{6,7},{7,6},{8,9},{9,8},{10,11... | collective-permute-start | bytes 786440 | tf_op jit(solution)/shard_map/ppermute | solution.py:31
  14.7 3.4 %fetch_query.1.base = bf16[4096,1024]{1,0:T(8,128)(2,1)S(1)} custom-call(bf16[4096,1024]{1,0:T(8,128)(2,1)} %source), custom_call_target="tpu_custom_call" | custom-call | bytes 8388608 | tf_op jit(solution)/shard_map/fetch_query/pallas_call | solution.py:62
  18.6 3.2 %collective-permute-done.8.far = bf16[4,64,512]{2,1,0:T(8,128)(2,1)S(1)} collective-permute-done((bf16[4,64,512]{2,1,0:T(8,128)(2,1)S(1)}, bf16[4,64,512]{2,1,0:T(8,128)(2,1)S(1)}, u32[]{:S(2)}, u32[]{:S(2)}) %collective-permute-start.8) | collective-permute-done | bytes 262176 | tf_op jit(solution)/shard_map/ppermute | solution.py:31
  21.8 6.5 %query_project.1 = (bf16[4096,1024]{1,0:T(8,128)(2,1)}, f32[64,1024]{1,0:T(8,128)S(1)}, f32[64,1024]{1,0:T(8,128)S(1)}) custom-call(s32[1]{0:T(128)} %bitcast.place, bf16[4,64,512]{2,1,0:T(8,128)(2,1)S(1)} %pad_maximum_fusion.2.near, bf16[4,64,512]{2,1,0:T(8,128)(2,1)S(1)} %collective-permute-done.8.far, bf16[64,1024]{1,0:T(8,128)(2,1)S(1)} %fusion.8.upper, ...), custom_call_target="tpu_custom_call" | custom-call | flops 1610612736 | bytes 8388608 | tf_op jit(solution)/shard_map/query_project/pallas_call | solution.py:141
  28.5 2.2 %collective-permute-start.3 = (bf16[2,80,512]{2,1,0:T(8,128)(2,1)S(1)}, bf16[2,80,512]{2,1,0:T(8,128)(2,1)S(1)}, u32[]{:S(2)}, u32[]{:S(2)}) collective-permute-start(bf16[2,80,512]{2,1,0:T(8,128)(2,1)S(1)} %get-tuple-element.49), channel_id=1, source_target_pairs={{0,4},{1,5},{2,6},{3,7},{4,0},{5,1},{6,2},{7,3},{8,12},{9,13},{10,... | collective-permute-start | bytes 491528 | tf_op jit(solution)/shard_map/ppermute | solution.py:31
  30.7 2.5 %collective-permute-start.2 = (bf16[2,80,512]{2,1,0:T(8,128)(2,1)S(1)}, bf16[2,80,512]{2,1,0:T(8,128)(2,1)S(1)}, u32[]{:S(2)}, u32[]{:S(2)}) collective-permute-start(bf16[2,80,512]{2,1,0:T(8,128)(2,1)S(1)} %get-tuple-element.49), channel_id=1, source_target_pairs={{0,2},{1,3},{2,0},{3,1},{4,6},{5,7},{6,4},{7,5},{8,10},{9,11},{10,... | collective-permute-start | bytes 491528 | tf_op jit(solution)/shard_map/ppermute | solution.py:31
  33.2 7.7 %attend.1.mine = bf16[64,1024]{1,0:T(8,128)(2,1)S(1)} custom-call(s32[8]{0:T(128)S(1)} %copy-done.2, f32[64,1024]{1,0:T(8,128)S(1)} %get-tuple-element.20.own, f32[64,1024]{1,0:T(8,128)S(1)} %collective-permute-done.10.other, bf16[1,1024]{1,0:T(2,128)(2,1)S(1)} %broadcast_in_dim.8.bias, f32[64,128]{1,0:T(8,128)S(1)} %get-tuple-element.59.cosine, ...), custom_call_target="tpu_custom_call" | custom-call | flops 536870912 | bytes 8388608 | tf_op jit(solution)/shard_map/attend/pallas_call | solution.py:218
  41.0 3.6 %collective-permute-done.4 = bf16[2,80,512]{2,1,0:T(8,128)(2,1)S(1)} collective-permute-done((bf16[2,80,512]{2,1,0:T(8,128)(2,1)S(1)}, bf16[2,80,512]{2,1,0:T(8,128)(2,1)S(1)}, u32[]{:S(2)}, u32[]{:S(2)}) %collective-permute-start.4) | collective-permute-done | bytes 163872 | tf_op jit(solution)/shard_map/ppermute | solution.py:31
  46.1 8.7 %output_project.1 = (bf16[1024,4096]{1,0:T(8,128)(2,1)}, f32[2,4,64,512]{3,2,1,0:T(8,128)S(1)}, f32[4,2,64,512]{3,2,1,0:T(8,128)S(1)}) custom-call(s32[1]{0:T(128)} %bitcast.place, bf16[64,1024]{1,0:T(8,128)(2,1)S(1)} %fusion.7.lower, bf16[4,2,80,512]{3,2,1,0:T(8,128)(2,1)S(1)} %pad_maximum_fusion.upper, bf16[1024,4096]{1,0:T(8,128)(2,1)} %base.1, ...), custom_call_target="tpu_custom_call" | custom-call | flops 1610612736 | bytes 16777216 | tf_op jit(solution)/shard_map/output_project/pallas_call | solution.py:283
  54.9 1.7 %collective-permute-start.12 = (f16[4,64,512]{2,1,0:T(8,128)(2,1)S(1)}, f16[4,64,512]{2,1,0:T(8,128)(2,1)S(1)}, u32[]{:S(2)}, u32[]{:S(2)}) collective-permute-start(f16[4,64,512]{2,1,0:T(8,128)(2,1)S(1)} %fusion), channel_id=1, source_target_pairs={{0,1},{1,0},{2,3},{3,2},{4,5},{5,4},{6,7},{7,6},{8,9},{9,8},{10,11... | collective-permute-start | bytes 786440 | tf_op jit(solution)/shard_map/ppermute | solution.py:31
  56.7 1.7 %collective-permute-start.15 = (f16[2,64,512]{2,1,0:T(8,128)(2,1)S(1)}, f16[2,64,512]{2,1,0:T(8,128)(2,1)S(1)}, u32[]{:S(2)}, u32[]{:S(2)}) collective-permute-start(f16[2,64,512]{2,1,0:T(8,128)(2,1)S(1)} %get-tuple-element.36), channel_id=1, source_target_pairs={{0,6},{1,7},{2,4},{3,5},{4,2},{5,3},{6,0},{7,1},{8,14},{9,15},{10,... | collective-permute-start | bytes 393224 | tf_op jit(solution)/shard_map/ppermute | solution.py:31
  58.4 2.8 %collective-permute-start.14 = (f16[2,64,512]{2,1,0:T(8,128)(2,1)S(1)}, f16[2,64,512]{2,1,0:T(8,128)(2,1)S(1)}, u32[]{:S(2)}, u32[]{:S(2)}) collective-permute-start(f16[2,64,512]{2,1,0:T(8,128)(2,1)S(1)} %get-tuple-element.37), channel_id=1, source_target_pairs={{0,4},{1,5},{2,6},{3,7},{4,0},{5,1},{6,2},{7,3},{8,12},{9,13},{10,... | collective-permute-start | bytes 393224 | tf_op jit(solution)/shard_map/ppermute | solution.py:31
  61.4 1.6 %collective-permute-done.12 = f16[4,64,512]{2,1,0:T(8,128)(2,1)S(1)} collective-permute-done((f16[4,64,512]{2,1,0:T(8,128)(2,1)S(1)}, f16[4,64,512]{2,1,0:T(8,128)(2,1)S(1)}, u32[]{:S(2)}, u32[]{:S(2)}) %collective-permute-start.12) | collective-permute-done | bytes 262176 | tf_op jit(solution)/shard_map/ppermute | solution.py:31
  63.2 1.5 %collective-permute-start.18 = (f16[64,512]{1,0:T(8,128)(2,1)S(1)}, f16[64,512]{1,0:T(8,128)(2,1)S(1)}, u32[]{:S(2)}, u32[]{:S(2)}) collective-permute-start(f16[64,512]{1,0:T(8,128)(2,1)S(1)} %get-tuple-element.43), channel_id=1, source_target_pairs={{0,6},{1,7},{2,4},{3,5},{4,2},{5,3},{6,0},{7,1},{8,14},{9,15},{10,... | collective-permute-start | bytes 196616 | tf_op jit(solution)/shard_map/ppermute | solution.py:31
  64.7 3.0 %collective-permute-start.17 = (f16[64,512]{1,0:T(8,128)(2,1)S(1)}, f16[64,512]{1,0:T(8,128)(2,1)S(1)}, u32[]{:S(2)}, u32[]{:S(2)}) collective-permute-start(f16[64,512]{1,0:T(8,128)(2,1)S(1)} %get-tuple-element.44), channel_id=1, source_target_pairs={{0,4},{1,5},{2,6},{3,7},{4,0},{5,1},{6,2},{7,3},{8,12},{9,13},{10,... | collective-permute-start | bytes 196616 | tf_op jit(solution)/shard_map/ppermute | solution.py:31
  67.7 2.8 %collective-permute-start.16 = (f16[64,512]{1,0:T(8,128)(2,1)S(1)}, f16[64,512]{1,0:T(8,128)(2,1)S(1)}, u32[]{:S(2)}, u32[]{:S(2)}) collective-permute-start(f16[64,512]{1,0:T(8,128)(2,1)S(1)} %get-tuple-element.45), channel_id=1, source_target_pairs={{0,2},{1,3},{2,0},{3,1},{4,6},{5,7},{6,4},{7,5},{8,10},{9,11},{10,... | collective-permute-start | bytes 196616 | tf_op jit(solution)/shard_map/ppermute | solution.py:31
  70.5 4.4 %collective-permute-done.14 = f16[2,64,512]{2,1,0:T(8,128)(2,1)S(1)} collective-permute-done((f16[2,64,512]{2,1,0:T(8,128)(2,1)S(1)}, f16[2,64,512]{2,1,0:T(8,128)(2,1)S(1)}, u32[]{:S(2)}, u32[]{:S(2)}) %collective-permute-start.14) | collective-permute-done | bytes 131104 | tf_op jit(solution)/shard_map/ppermute | solution.py:31
  74.9 2.7 %collective-permute-done.17 = f16[64,512]{1,0:T(8,128)(2,1)S(1)} collective-permute-done((f16[64,512]{1,0:T(8,128)(2,1)S(1)}, f16[64,512]{1,0:T(8,128)(2,1)S(1)}, u32[]{:S(2)}, u32[]{:S(2)}) %collective-permute-start.17) | collective-permute-done | bytes 65568 | tf_op jit(solution)/shard_map/ppermute | solution.py:31
  78.3 0.7 collective-permute-done.23
  79.0 2.6 %collective-permute-done.24 = f16[64,512]{1,0:T(8,128)(2,1)S(1)} collective-permute-done((f16[64,512]{1,0:T(8,128)(2,1)S(1)}, f16[64,512]{1,0:T(8,128)(2,1)S(1)}, u32[]{:S(2)}, u32[]{:S(2)}) %collective-permute-start.24) | collective-permute-done | bytes 65568 | tf_op jit(solution)/shard_map/ppermute | solution.py:351
  82.2 1.8 %collective-permute-start.21 = (f16[64,512]{1,0:T(8,128)(2,1)S(1)}, f16[64,512]{1,0:T(8,128)(2,1)S(1)}, u32[]{:S(2)}, u32[]{:S(2)}) collective-permute-start(f16[64,512]{1,0:T(8,128)(2,1)S(1)} %fusion.6), channel_id=1, source_target_pairs={{0,6},{1,7},{2,4},{3,5},{4,2},{5,3},{6,0},{7,1},{8,14},{9,15},{10,... | collective-permute-start | bytes 196616 | tf_op jit(solution)/shard_map/ppermute | solution.py:31
  84.0 2.7 %collective-permute-start.19 = (f16[64,512]{1,0:T(8,128)(2,1)S(1)}, f16[64,512]{1,0:T(8,128)(2,1)S(1)}, u32[]{:S(2)}, u32[]{:S(2)}) collective-permute-start(f16[64,512]{1,0:T(8,128)(2,1)S(1)} %fusion.6), channel_id=1, source_target_pairs={{0,2},{1,3},{2,0},{3,1},{4,6},{5,7},{6,4},{7,5},{8,10},{9,11},{10,... | collective-permute-start | bytes 196616 | tf_op jit(solution)/shard_map/ppermute | solution.py:31
  87.0 2.0 %collective-permute-start.26 = (f16[2,64,512]{2,1,0:T(8,128)(2,1)S(1)}, f16[2,64,512]{2,1,0:T(8,128)(2,1)S(1)}, u32[]{:S(2)}, u32[]{:S(2)}) collective-permute-start(f16[2,64,512]{2,1,0:T(8,128)(2,1)S(1)} %get-tuple-element.51), channel_id=1, source_target_pairs={{0,2},{1,3},{2,0},{3,1},{4,6},{5,7},{6,4},{7,5},{8,10},{9,11},{10,... | collective-permute-start | bytes 393224 | tf_op jit(solution)/shard_map/ppermute | solution.py:31
  89.1 2.1 %collective-permute-start.28 = (f16[2,64,512]{2,1,0:T(8,128)(2,1)S(1)}, f16[2,64,512]{2,1,0:T(8,128)(2,1)S(1)}, u32[]{:S(2)}, u32[]{:S(2)}) collective-permute-start(f16[2,64,512]{2,1,0:T(8,128)(2,1)S(1)} %get-tuple-element.51), channel_id=1, source_target_pairs={{0,6},{1,7},{2,4},{3,5},{4,2},{5,3},{6,0},{7,1},{8,14},{9,15},{10,... | collective-permute-start | bytes 393224 | tf_op jit(solution)/shard_map/ppermute | solution.py:31
  91.3 1.8 %collective-permute-done.20 = f16[64,512]{1,0:T(8,128)(2,1)S(1)} collective-permute-done((f16[64,512]{1,0:T(8,128)(2,1)S(1)}, f16[64,512]{1,0:T(8,128)(2,1)S(1)}, u32[]{:S(2)}, u32[]{:S(2)}) %collective-permute-start.20) | collective-permute-done | bytes 65568 | tf_op jit(solution)/shard_map/ppermute | solution.py:31
  93.2 1.7 %collective-permute-start.22 = (f16[4,64,512]{2,1,0:T(8,128)(2,1)S(1)}, f16[4,64,512]{2,1,0:T(8,128)(2,1)S(1)}, u32[]{:S(2)}, u32[]{:S(2)}) collective-permute-start(f16[4,64,512]{2,1,0:T(8,128)(2,1)S(1)} %get-tuple-element.42), channel_id=1, source_target_pairs={{0,1},{1,0},{2,3},{3,2},{4,5},{5,4},{6,7},{7,6},{8,9},{9,8},{10,11... | collective-permute-start | bytes 786440 | tf_op jit(solution)/shard_map/ppermute | solution.py:31
  94.9 2.7 %collective-permute-done.27 = f16[2,64,512]{2,1,0:T(8,128)(2,1)S(1)} collective-permute-done((f16[2,64,512]{2,1,0:T(8,128)(2,1)S(1)}, f16[2,64,512]{2,1,0:T(8,128)(2,1)S(1)}, u32[]{:S(2)}, u32[]{:S(2)}) %collective-permute-start.27) | collective-permute-done | bytes 131104 | tf_op jit(solution)/shard_map/ppermute | solution.py:31
  97.6 1.9 %collective-permute-done.28 = f16[2,64,512]{2,1,0:T(8,128)(2,1)S(1)} collective-permute-done((f16[2,64,512]{2,1,0:T(8,128)(2,1)S(1)}, f16[2,64,512]{2,1,0:T(8,128)(2,1)S(1)}, u32[]{:S(2)}, u32[]{:S(2)}) %collective-permute-start.28) | collective-permute-done | bytes 131104 | tf_op jit(solution)/shard_map/ppermute | solution.py:31
  100.3 2.9 %finish.1 = (bf16[64,8192]{1,0:T(8,128)(2,1)}, bf16[64,8192]{1,0:T(8,128)(2,1)}) custom-call(s32[2]{0:T(128)S(1)} %pad_add_fusion.place, f32[1]{0:T(128)} %bitcast.10.bound, bf16[64,8192]{1,0:T(8,128)(2,1)S(1)} %bitcast.73, bf16[1,8192]{1,0:T(2,128)(2,1)S(1)} %broadcast_in_dim.7.gain, f32[8,64,512]{2,1,0:T(8,128)S(1)} %bitcast.74, ...), custom_call_target="tpu_custom_call" | custom-call | flops 4194304 | bytes 7340032 | tf_op jit(solution)/shard_map/finish/pallas_call | solution.py:338
  (93 shorter events, 7.2 us)
Async XLA Ops:
  0.6 10.5 %copy-start = (bf16[8,8,8192]{2,1,0:T(8,128)(2,1)S(1)}, bf16[8,8,8192]{2,1,0:T(8,128)(2,1)}, u32[]{:S(2)}) copy-start(bf16[8,8,8192]{2,1,0:T(8,128)(2,1)} %param.14) | copy-start | bytes 3145732
  0.6 12.2 %collective-permute-start.6 = (bf16[64,512]{1,0:T(8,128)(2,1)}, bf16[64,512]{1,0:T(8,128)(2,1)S(1)}, u32[]{:S(2)}, u32[]{:S(2)}) collective-permute-start(bf16[64,512]{1,0:T(8,128)(2,1)} %bitcast.94), channel_id=1, source_target_pairs={{0,4},{1,5},{2,6},{3,7},{4,0},{5,1},{6,2},{7,3},{8,12},{9,13},{10,... | collective-permute-start | bytes 196616 | tf_op jit(solution)/shard_map/ppermute | solution.py:31
  4.7 8.1 %collective-permute-start.5 = (bf16[64,512]{1,0:T(8,128)(2,1)}, bf16[64,512]{1,0:T(8,128)(2,1)S(1)}, u32[]{:S(2)}, u32[]{:S(2)}) collective-permute-start(bf16[64,512]{1,0:T(8,128)(2,1)} %bitcast.95), channel_id=1, source_target_pairs={{0,2},{1,3},{2,0},{3,1},{4,6},{5,7},{6,4},{7,5},{8,10},{9,11},{10,... | collective-permute-start | bytes 196616 | tf_op jit(solution)/shard_map/ppermute | solution.py:31
  6.3 6.5 %collective-permute-start.7 = (bf16[64,512]{1,0:T(8,128)(2,1)}, bf16[64,512]{1,0:T(8,128)(2,1)S(1)}, u32[]{:S(2)}, u32[]{:S(2)}) collective-permute-start(bf16[64,512]{1,0:T(8,128)(2,1)} %bitcast.96), channel_id=1, source_target_pairs={{0,6},{1,7},{2,4},{3,5},{4,2},{5,3},{6,0},{7,1},{8,14},{9,15},{10,... | collective-permute-start | bytes 196616 | tf_op jit(solution)/shard_map/ppermute | solution.py:31
  11.0 7.1 %collective-permute-start = (bf16[80,1024]{1,0:T(8,128)(2,1)S(1)}, bf16[80,1024]{1,0:T(8,128)(2,1)S(1)}, u32[]{:S(2)}, u32[]{:S(2)}) collective-permute-start(bf16[80,1024]{1,0:T(8,128)(2,1)S(1)} %pad_maximum_fusion.4), channel_id=1, source_target_pairs={{0,8},{8,0},{1,9},{9,1},{2,10},{10,2},{3,11},{11,3},{4,12},{12,4},... | collective-permute-start | bytes 491528 | tf_op jit(solution)/shard_map/ppermute | solution.py:35
  11.9 9.9 %collective-permute-start.9 = (bf16[64,4096]{1,0:T(8,128)(2,1)S(1)}, bf16[64,4096]{1,0:T(8,128)(2,1)S(1)}, u32[]{:S(2)}, u32[]{:S(2)}) collective-permute-start(bf16[64,4096]{1,0:T(8,128)(2,1)S(1)} %get-tuple-element.39), channel_id=1, source_target_pairs={{0,8},{8,0},{1,9},{9,1},{2,10},{10,2},{3,11},{11,3},{4,12},{12,4},... | collective-permute-start | bytes 1572872 | tf_op jit(solution)/shard_map/ppermute | solution.py:35
  12.9 8.9 %collective-permute-start.8 = (bf16[4,64,512]{2,1,0:T(8,128)(2,1)S(1)}, bf16[4,64,512]{2,1,0:T(8,128)(2,1)S(1)}, u32[]{:S(2)}, u32[]{:S(2)}) collective-permute-start(bf16[4,64,512]{2,1,0:T(8,128)(2,1)S(1)} %pad_maximum_fusion.2.near), channel_id=1, source_target_pairs={{0,1},{1,0},{2,3},{3,2},{4,5},{5,4},{6,7},{7,6},{8,9},{9,8},{10,11... | collective-permute-start | bytes 786440 | tf_op jit(solution)/shard_map/ppermute | solution.py:31
  18.2 10.3 %collective-permute-start.1 = (bf16[80,512]{1,0:T(8,128)(2,1)S(1)}, bf16[80,512]{1,0:T(8,128)(2,1)S(1)}, u32[]{:S(2)}, u32[]{:S(2)}) collective-permute-start(bf16[80,512]{1,0:T(8,128)(2,1)S(1)} %get-tuple-element.55), channel_id=1, source_target_pairs={{0,1},{1,0},{2,3},{3,2},{4,5},{5,4},{6,7},{7,6},{8,9},{9,8},{10,11... | collective-permute-start | bytes 245768 | tf_op jit(solution)/shard_map/ppermute | solution.py:31
  21.8 6.6 %copy-start.9 = (bf16[1024]{0:T(1024)(128)(2,1)S(1)}, bf16[1024]{0:T(1024)(128)(2,1)}, u32[]{:S(2)}) copy-start(bf16[1024]{0:T(1024)(128)(2,1)} %param.18) | copy-start | bytes 6148
  28.3 4.9 %collective-permute-start.10 = (f32[64,1024]{1,0:T(8,128)S(1)}, f32[64,1024]{1,0:T(8,128)S(1)}, u32[]{:S(2)}, u32[]{:S(2)}) collective-permute-start(f32[64,1024]{1,0:T(8,128)S(1)} %get-tuple-element.21), channel_id=1, source_target_pairs={{0,8},{8,0},{1,9},{9,1},{2,10},{10,2},{3,11},{11,3},{4,12},{12,4},... | collective-permute-start | bytes 786440 | tf_op jit(solution)/shard_map/ppermute | solution.py:35
  28.5 12.5 %collective-permute-start.3 = (bf16[2,80,512]{2,1,0:T(8,128)(2,1)S(1)}, bf16[2,80,512]{2,1,0:T(8,128)(2,1)S(1)}, u32[]{:S(2)}, u32[]{:S(2)}) collective-permute-start(bf16[2,80,512]{2,1,0:T(8,128)(2,1)S(1)} %get-tuple-element.49), channel_id=1, source_target_pairs={{0,4},{1,5},{2,6},{3,7},{4,0},{5,1},{6,2},{7,3},{8,12},{9,13},{10,... | collective-permute-start | bytes 491528 | tf_op jit(solution)/shard_map/ppermute | solution.py:31
  30.7 10.3 %collective-permute-start.2 = (bf16[2,80,512]{2,1,0:T(8,128)(2,1)S(1)}, bf16[2,80,512]{2,1,0:T(8,128)(2,1)S(1)}, u32[]{:S(2)}, u32[]{:S(2)}) collective-permute-start(bf16[2,80,512]{2,1,0:T(8,128)(2,1)S(1)} %get-tuple-element.49), channel_id=1, source_target_pairs={{0,2},{1,3},{2,0},{3,1},{4,6},{5,7},{6,4},{7,5},{8,10},{9,11},{10,... | collective-permute-start | bytes 491528 | tf_op jit(solution)/shard_map/ppermute | solution.py:31
  33.2 11.5 %collective-permute-start.4 = (bf16[2,80,512]{2,1,0:T(8,128)(2,1)S(1)}, bf16[2,80,512]{2,1,0:T(8,128)(2,1)S(1)}, u32[]{:S(2)}, u32[]{:S(2)}) collective-permute-start(bf16[2,80,512]{2,1,0:T(8,128)(2,1)S(1)} %get-tuple-element.49), channel_id=1, source_target_pairs={{0,6},{1,7},{2,4},{3,5},{4,2},{5,3},{6,0},{7,1},{8,14},{9,15},{10,... | collective-permute-start | bytes 491528 | tf_op jit(solution)/shard_map/ppermute | solution.py:31
  40.9 5.2 %collective-permute-start.11 = (bf16[64,1024]{1,0:T(8,128)(2,1)S(1)}, bf16[64,1024]{1,0:T(8,128)(2,1)S(1)}, u32[]{:S(2)}, u32[]{:S(2)}) collective-permute-start(bf16[64,1024]{1,0:T(8,128)(2,1)S(1)} %attend.1.mine), channel_id=1, source_target_pairs={{0,8},{8,0},{1,9},{9,1},{2,10},{10,2},{3,11},{11,3},{4,12},{12,4},... | collective-permute-start | bytes 393224 | tf_op jit(solution)/shard_map/ppermute | solution.py:35
  54.8 36.5 %copy-start.8 = (bf16[8192]{0:T(1024)(128)(2,1)S(1)}, bf16[8192]{0:T(1024)(128)(2,1)}, u32[]{:S(2)}) copy-start(bf16[8192]{0:T(1024)(128)(2,1)} %param.16) | copy-start | bytes 49156
  54.9 8.1 %collective-permute-start.12 = (f16[4,64,512]{2,1,0:T(8,128)(2,1)S(1)}, f16[4,64,512]{2,1,0:T(8,128)(2,1)S(1)}, u32[]{:S(2)}, u32[]{:S(2)}) collective-permute-start(f16[4,64,512]{2,1,0:T(8,128)(2,1)S(1)} %fusion), channel_id=1, source_target_pairs={{0,1},{1,0},{2,3},{3,2},{4,5},{5,4},{6,7},{7,6},{8,9},{9,8},{10,11... | collective-permute-start | bytes 786440 | tf_op jit(solution)/shard_map/ppermute | solution.py:31
  56.7 11.0 %collective-permute-start.15 = (f16[2,64,512]{2,1,0:T(8,128)(2,1)S(1)}, f16[2,64,512]{2,1,0:T(8,128)(2,1)S(1)}, u32[]{:S(2)}, u32[]{:S(2)}) collective-permute-start(f16[2,64,512]{2,1,0:T(8,128)(2,1)S(1)} %get-tuple-element.36), channel_id=1, source_target_pairs={{0,6},{1,7},{2,4},{3,5},{4,2},{5,3},{6,0},{7,1},{8,14},{9,15},{10,... | collective-permute-start | bytes 393224 | tf_op jit(solution)/shard_map/ppermute | solution.py:31
  58.4 16.5 %collective-permute-start.14 = (f16[2,64,512]{2,1,0:T(8,128)(2,1)S(1)}, f16[2,64,512]{2,1,0:T(8,128)(2,1)S(1)}, u32[]{:S(2)}, u32[]{:S(2)}) collective-permute-start(f16[2,64,512]{2,1,0:T(8,128)(2,1)S(1)} %get-tuple-element.37), channel_id=1, source_target_pairs={{0,4},{1,5},{2,6},{3,7},{4,0},{5,1},{6,2},{7,3},{8,12},{9,13},{10,... | collective-permute-start | bytes 393224 | tf_op jit(solution)/shard_map/ppermute | solution.py:31
  61.2 13.6 %collective-permute-start.13 = (f16[2,64,512]{2,1,0:T(8,128)(2,1)S(1)}, f16[2,64,512]{2,1,0:T(8,128)(2,1)S(1)}, u32[]{:S(2)}, u32[]{:S(2)}) collective-permute-start(f16[2,64,512]{2,1,0:T(8,128)(2,1)S(1)} %get-tuple-element.38), channel_id=1, source_target_pairs={{0,2},{1,3},{2,0},{3,1},{4,6},{5,7},{6,4},{7,5},{8,10},{9,11},{10,... | collective-permute-start | bytes 393224 | tf_op jit(solution)/shard_map/ppermute | solution.py:31
  63.2 11.7 %collective-permute-start.18 = (f16[64,512]{1,0:T(8,128)(2,1)S(1)}, f16[64,512]{1,0:T(8,128)(2,1)S(1)}, u32[]{:S(2)}, u32[]{:S(2)}) collective-permute-start(f16[64,512]{1,0:T(8,128)(2,1)S(1)} %get-tuple-element.43), channel_id=1, source_target_pairs={{0,6},{1,7},{2,4},{3,5},{4,2},{5,3},{6,0},{7,1},{8,14},{9,15},{10,... | collective-permute-start | bytes 196616 | tf_op jit(solution)/shard_map/ppermute | solution.py:31
  64.7 12.9 %collective-permute-start.17 = (f16[64,512]{1,0:T(8,128)(2,1)S(1)}, f16[64,512]{1,0:T(8,128)(2,1)S(1)}, u32[]{:S(2)}, u32[]{:S(2)}) collective-permute-start(f16[64,512]{1,0:T(8,128)(2,1)S(1)} %get-tuple-element.44), channel_id=1, source_target_pairs={{0,4},{1,5},{2,6},{3,7},{4,0},{5,1},{6,2},{7,3},{8,12},{9,13},{10,... | collective-permute-start | bytes 196616 | tf_op jit(solution)/shard_map/ppermute | solution.py:31
  67.7 9.9 %collective-permute-start.16 = (f16[64,512]{1,0:T(8,128)(2,1)S(1)}, f16[64,512]{1,0:T(8,128)(2,1)S(1)}, u32[]{:S(2)}, u32[]{:S(2)}) collective-permute-start(f16[64,512]{1,0:T(8,128)(2,1)S(1)} %get-tuple-element.45), channel_id=1, source_target_pairs={{0,2},{1,3},{2,0},{3,1},{4,6},{5,7},{6,4},{7,5},{8,10},{9,11},{10,... | collective-permute-start | bytes 196616 | tf_op jit(solution)/shard_map/ppermute | solution.py:31
  77.7 1.3 %collective-permute-start.23 = (f16[64,512]{1,0:T(8,128)(2,1)S(1)}, f16[64,512]{1,0:T(8,128)(2,1)S(1)}, u32[]{:S(2)}, u32[]{:S(2)}) collective-permute-start(f16[64,512]{1,0:T(8,128)(2,1)S(1)} %get-tuple-element.52), channel_id=1, source_target_pairs={{0,8},{8,0},{1,9},{9,1},{2,10},{10,2},{3,11},{11,3},{4,12},{12,4},... | collective-permute-start | bytes 196616 | tf_op jit(solution)/shard_map/ppermute | solution.py:35
  77.8 3.9 %collective-permute-start.24 = (f16[64,512]{1,0:T(8,128)(2,1)S(1)}, f16[64,512]{1,0:T(8,128)(2,1)S(1)}, u32[]{:S(2)}, u32[]{:S(2)}) collective-permute-start(f16[64,512]{1,0:T(8,128)(2,1)S(1)} %get-tuple-element.53), channel_id=1, source_target_pairs={{0,9},{1,8},{2,11},{3,10},{4,13},{5,12},{6,15},{7,14},{8,1},{9,0},... | collective-permute-start | bytes 196616 | tf_op jit(solution)/shard_map/ppermute | solution.py:351
  81.7 5.0 %collective-permute-start.25 = (f16[64,512]{1,0:T(8,128)(2,1)S(1)}, f16[64,512]{1,0:T(8,128)(2,1)S(1)}, u32[]{:S(2)}, u32[]{:S(2)}) collective-permute-start(f16[64,512]{1,0:T(8,128)(2,1)S(1)} %add_convert_fusion), channel_id=1, source_target_pairs={{0,1},{1,0},{2,3},{3,2},{4,5},{5,4},{6,7},{7,6},{8,9},{9,8},{10,11... | collective-permute-start | bytes 196616 | tf_op jit(solution)/shard_map/ppermute | solution.py:31
  82.2 6.8 %collective-permute-start.21 = (f16[64,512]{1,0:T(8,128)(2,1)S(1)}, f16[64,512]{1,0:T(8,128)(2,1)S(1)}, u32[]{:S(2)}, u32[]{:S(2)}) collective-permute-start(f16[64,512]{1,0:T(8,128)(2,1)S(1)} %fusion.6), channel_id=1, source_target_pairs={{0,6},{1,7},{2,4},{3,5},{4,2},{5,3},{6,0},{7,1},{8,14},{9,15},{10,... | collective-permute-start | bytes 196616 | tf_op jit(solution)/shard_map/ppermute | solution.py:31
  84.0 9.1 %collective-permute-start.20 = (f16[64,512]{1,0:T(8,128)(2,1)S(1)}, f16[64,512]{1,0:T(8,128)(2,1)S(1)}, u32[]{:S(2)}, u32[]{:S(2)}) collective-permute-start(f16[64,512]{1,0:T(8,128)(2,1)S(1)} %fusion.6), channel_id=1, source_target_pairs={{0,4},{1,5},{2,6},{3,7},{4,0},{5,1},{6,2},{7,3},{8,12},{9,13},{10,... | collective-permute-start | bytes 196616 | tf_op jit(solution)/shard_map/ppermute | solution.py:31
  84.0 9.1 %collective-permute-start.19 = (f16[64,512]{1,0:T(8,128)(2,1)S(1)}, f16[64,512]{1,0:T(8,128)(2,1)S(1)}, u32[]{:S(2)}, u32[]{:S(2)}) collective-permute-start(f16[64,512]{1,0:T(8,128)(2,1)S(1)} %fusion.6), channel_id=1, source_target_pairs={{0,2},{1,3},{2,0},{3,1},{4,6},{5,7},{6,4},{7,5},{8,10},{9,11},{10,... | collective-permute-start | bytes 196616 | tf_op jit(solution)/shard_map/ppermute | solution.py:31
  86.7 10.8 %collective-permute-start.27 = (f16[2,64,512]{2,1,0:T(8,128)(2,1)S(1)}, f16[2,64,512]{2,1,0:T(8,128)(2,1)S(1)}, u32[]{:S(2)}, u32[]{:S(2)}) collective-permute-start(f16[2,64,512]{2,1,0:T(8,128)(2,1)S(1)} %get-tuple-element.51), channel_id=1, source_target_pairs={{0,4},{1,5},{2,6},{3,7},{4,0},{5,1},{6,2},{7,3},{8,12},{9,13},{10,... | collective-permute-start | bytes 393224 | tf_op jit(solution)/shard_map/ppermute | solution.py:31
  87.0 10.5 %collective-permute-start.26 = (f16[2,64,512]{2,1,0:T(8,128)(2,1)S(1)}, f16[2,64,512]{2,1,0:T(8,128)(2,1)S(1)}, u32[]{:S(2)}, u32[]{:S(2)}) collective-permute-start(f16[2,64,512]{2,1,0:T(8,128)(2,1)S(1)} %get-tuple-element.51), channel_id=1, source_target_pairs={{0,2},{1,3},{2,0},{3,1},{4,6},{5,7},{6,4},{7,5},{8,10},{9,11},{10,... | collective-permute-start | bytes 393224 | tf_op jit(solution)/shard_map/ppermute | solution.py:31
  89.1 10.4 %collective-permute-start.28 = (f16[2,64,512]{2,1,0:T(8,128)(2,1)S(1)}, f16[2,64,512]{2,1,0:T(8,128)(2,1)S(1)}, u32[]{:S(2)}, u32[]{:S(2)}) collective-permute-start(f16[2,64,512]{2,1,0:T(8,128)(2,1)S(1)} %get-tuple-element.51), channel_id=1, source_target_pairs={{0,6},{1,7},{2,4},{3,5},{4,2},{5,3},{6,0},{7,1},{8,14},{9,15},{10,... | collective-permute-start | bytes 393224 | tf_op jit(solution)/shard_map/ppermute | solution.py:31
  93.2 6.9 %collective-permute-start.22 = (f16[4,64,512]{2,1,0:T(8,128)(2,1)S(1)}, f16[4,64,512]{2,1,0:T(8,128)(2,1)S(1)}, u32[]{:S(2)}, u32[]{:S(2)}) collective-permute-start(f16[4,64,512]{2,1,0:T(8,128)(2,1)S(1)} %get-tuple-element.42), channel_id=1, source_target_pairs={{0,1},{1,0},{2,3},{3,2},{4,5},{5,4},{6,7},{7,6},{8,9},{9,8},{10,11... | collective-permute-start | bytes 786440 | tf_op jit(solution)/shard_map/ppermute | solution.py:31
  (8 other events, 35.4 us)

commit v3 on v2

--- a/solution.py
+++ b/solution.py
@@ -370,10 +370,10 @@
     arrived = [hop(narrow(shrink(other[k])), 2 * k) for k in range(1, outer)]
     summed = shrink(own[0]) + across.astype(F32)
     ended = [hop(narrow(summed[k]), 2 * k) for k in range(1, outer)]
-    arrived, ended = lax.optimization_barrier((arrived, ended))
+    arrived, ended[:1] = lax.optimization_barrier((arrived, ended[:1]))
     total = summed[0] + sum(e.astype(F32) for e in ended)
     pair = narrow(shrink(other[0]) + sum(a.astype(F32) for a in arrived))
-    far = swap(pair[0]).astype(F32) + cross(pair[1]).astype(F32)
+    far = swap(pair).astype(F32) + cross(pair)[::-1].astype(F32)
     return narrow(total), narrow(far)
 
 
@@ -470,7 +470,7 @@
 
     near = along_z(near)
     near = jnp.stack([near, hop(near, 1)], axis=1)
-    far = along_z(along_y(far))
+    far = along_z(far)
     near = near.reshape((2 * outer,) + near.shape[2:]).astype(F32)
     far = far.reshape((2 * outer,) + far.shape[2:]).astype(F32)
 

time: 104 us -> 101 us (0.971)
  starting transfers between devices: 38.7 us -> 36 us
    ppermute x23 -> x22, waiting for transfers between devices: 22.2 us -> 26.1 us  [hop(): return lax.ppermute(value, 'tp', [(i, i ^ distance) for i in range(total)])]
    ppermute x23 -> x22, starting transfers between devices: 37.4 us -> 34.6 us  [hop(): return lax.ppermute(value, 'tp', [(i, i ^ distance) for i in range(total)])]
    ppermute x1, waiting for transfers between devices: 2.65 us -> 0.01 us  [cross(): return lax.ppermute(value, ('fsdp', 'tp'), pairs)]
  transfers between devices with their start and end apart: 29 -> 28, of which waited for: 11 -> 8; matrix products, arithmetic and copies ran while one was open for 3% -> 3% of each run, Pallas kernels for 21% -> 21%
where the time goes in v3:
time: 101 us
  starting transfers between devices  36 us (36%)
  Pallas kernels  33.1 us (33%)
  waiting for transfers between devices  26.1 us (26%)
  other arithmetic  2.96 us (3%)
  between operations  1.8 us (2%)
  local copies, waits for them, and re-layouts  1.09 us (1%)
    ppermute x22, starting transfers between devices, hop(): return lax.ppermute(value, 'tp', [(i, i ^ distance) for i in range(total)])  34.6 us
    ppermute x22, waiting for transfers between devices, hop(): return lax.ppermute(value, 'tp', [(i, i ^ distance) for i in range(total)])  26.1 us
    pallas_call x1, Pallas kernels, output_project(): pl.pallas_call(output_kernel, in_specs=[SMEM, VMEM, VMEM, ANY, VMEM, VMEM...  8.68 us
    pallas_call x1, Pallas kernels, attend(): pl.pallas_call(functools.partial(attend_kernel, steps, scale), in_specs=[...  7.69 us
    pallas_call x1, Pallas kernels, query_project(): pl.pallas_call(query_kernel, in_specs=[SMEM] + [VMEM] * 6, out_specs=[ANY...  6.46 us
    pallas_call x1, Pallas kernels, largest_in_reach(): pl.pallas_call(reach_kernel, in_specs=[SMEM, ANY], out_specs=VMEM, out_sh...  3.94 us
    pallas_call x1, Pallas kernels, fetch(): pl.pallas_call(fetch_kernel, in_specs=[ANY], out_specs=VMEM, out_shape=pl...  3.39 us
    pallas_call x1, Pallas kernels, finish(): pl.pallas_call(finish_kernel, grid_spec=spec, out_shape=[jax.ShapeDtypeSt...  2.94 us
  transfers between devices with their start and end apart: 28, of which 8 were waited for; matrix products, arithmetic and copies ran while one was open for 3% of the time, Pallas kernels for 21%

profile of v3, /device:TPU:0, one launch (start us, length us, event | category | flops | bytes accessed | tf_op | source)
XLA Modules:
  0.0 101.0 jit_solution(18156926185829388485)
XLA Ops:
  0.6 4.1 %collective-permute-start.6 = (bf16[64,512]{1,0:T(8,128)(2,1)}, bf16[64,512]{1,0:T(8,128)(2,1)S(1)}, u32[]{:S(2)}, u32[]{:S(2)}) collective-permute-start(bf16[64,512]{1,0:T(8,128)(2,1)} %bitcast.86), channel_id=1, source_target_pairs={{0,4},{1,5},{2,6},{3,7},{4,0},{5,1},{6,2},{7,3},{8,12},{9,13},{10,... | collective-permute-start | bytes 196616 | tf_op jit(solution)/shard_map/ppermute | solution.py:31
  4.7 1.6 %collective-permute-start.5 = (bf16[64,512]{1,0:T(8,128)(2,1)}, bf16[64,512]{1,0:T(8,128)(2,1)S(1)}, u32[]{:S(2)}, u32[]{:S(2)}) collective-permute-start(bf16[64,512]{1,0:T(8,128)(2,1)} %bitcast.87), channel_id=1, source_target_pairs={{0,2},{1,3},{2,0},{3,1},{4,6},{5,7},{6,4},{7,5},{8,10},{9,11},{10,... | collective-permute-start | bytes 196616 | tf_op jit(solution)/shard_map/ppermute | solution.py:31
  6.3 0.7 copy-done.1
  7.0 3.9 %largest_in_reach.1 = bf16[16,1024]{1,0:T(8,128)(2,1)S(1)} custom-call(s32[8]{0:T(128)S(1)} %copy-done.1, bf16[8,2048,128]{2,1,0:T(8,128)(2,1)} %bitcast.68), custom_call_target="tpu_custom_call" | custom-call | flops 8388608 | bytes 4194304 | tf_op jit(solution)/shard_map/largest_in_reach/pallas_call | solution.py:91
  11.9 0.5 collective-permute-start.9
  12.9 1.8 %collective-permute-start.8 = (bf16[4,64,512]{2,1,0:T(8,128)(2,1)S(1)}, bf16[4,64,512]{2,1,0:T(8,128)(2,1)S(1)}, u32[]{:S(2)}, u32[]{:S(2)}) collective-permute-start(bf16[4,64,512]{2,1,0:T(8,128)(2,1)S(1)} %pad_maximum_fusion.2.near), channel_id=1, source_target_pairs={{0,1},{1,0},{2,3},{3,2},{4,5},{5,4},{6,7},{7,6},{8,9},{9,8},{10,11... | collective-permute-start | bytes 786440 | tf_op jit(solution)/shard_map/ppermute | solution.py:31
  14.7 3.4 %fetch_query.1.base = bf16[4096,1024]{1,0:T(8,128)(2,1)S(1)} custom-call(bf16[4096,1024]{1,0:T(8,128)(2,1)} %source), custom_call_target="tpu_custom_call" | custom-call | bytes 8388608 | tf_op jit(solution)/shard_map/fetch_query/pallas_call | solution.py:62
  18.6 3.2 %collective-permute-done.8.far = bf16[4,64,512]{2,1,0:T(8,128)(2,1)S(1)} collective-permute-done((bf16[4,64,512]{2,1,0:T(8,128)(2,1)S(1)}, bf16[4,64,512]{2,1,0:T(8,128)(2,1)S(1)}, u32[]{:S(2)}, u32[]{:S(2)}) %collective-permute-start.8) | collective-permute-done | bytes 262176 | tf_op jit(solution)/shard_map/ppermute | solution.py:31
  21.8 6.5 %query_project.1 = (bf16[4096,1024]{1,0:T(8,128)(2,1)}, f32[64,1024]{1,0:T(8,128)S(1)}, f32[64,1024]{1,0:T(8,128)S(1)}) custom-call(s32[1]{0:T(128)} %bitcast.place, bf16[4,64,512]{2,1,0:T(8,128)(2,1)S(1)} %pad_maximum_fusion.2.near, bf16[4,64,512]{2,1,0:T(8,128)(2,1)S(1)} %collective-permute-done.8.far, bf16[64,1024]{1,0:T(8,128)(2,1)S(1)} %fusion.8.upper, ...), custom_call_target="tpu_custom_call" | custom-call | flops 1610612736 | bytes 8388608 | tf_op jit(solution)/shard_map/query_project/pallas_call | solution.py:141
  28.5 2.2 %collective-permute-start.3 = (bf16[2,80,512]{2,1,0:T(8,128)(2,1)S(1)}, bf16[2,80,512]{2,1,0:T(8,128)(2,1)S(1)}, u32[]{:S(2)}, u32[]{:S(2)}) collective-permute-start(bf16[2,80,512]{2,1,0:T(8,128)(2,1)S(1)} %get-tuple-element.45), channel_id=1, source_target_pairs={{0,4},{1,5},{2,6},{3,7},{4,0},{5,1},{6,2},{7,3},{8,12},{9,13},{10,... | collective-permute-start | bytes 491528 | tf_op jit(solution)/shard_map/ppermute | solution.py:31
  30.7 2.5 %collective-permute-start.2 = (bf16[2,80,512]{2,1,0:T(8,128)(2,1)S(1)}, bf16[2,80,512]{2,1,0:T(8,128)(2,1)S(1)}, u32[]{:S(2)}, u32[]{:S(2)}) collective-permute-start(bf16[2,80,512]{2,1,0:T(8,128)(2,1)S(1)} %get-tuple-element.45), channel_id=1, source_target_pairs={{0,2},{1,3},{2,0},{3,1},{4,6},{5,7},{6,4},{7,5},{8,10},{9,11},{10,... | collective-permute-start | bytes 491528 | tf_op jit(solution)/shard_map/ppermute | solution.py:31
  33.2 7.7 %attend.1.mine = bf16[64,1024]{1,0:T(8,128)(2,1)S(1)} custom-call(s32[8]{0:T(128)S(1)} %copy-done.2, f32[64,1024]{1,0:T(8,128)S(1)} %get-tuple-element.18.own, f32[64,1024]{1,0:T(8,128)S(1)} %collective-permute-done.10.other, bf16[1,1024]{1,0:T(2,128)(2,1)S(1)} %broadcast_in_dim.8.bias, f32[64,128]{1,0:T(8,128)S(1)} %get-tuple-element.51.cosine, ...), custom_call_target="tpu_custom_call" | custom-call | flops 536870912 | bytes 8388608 | tf_op jit(solution)/shard_map/attend/pallas_call | solution.py:218
  41.0 3.6 %collective-permute-done.4 = bf16[2,80,512]{2,1,0:T(8,128)(2,1)S(1)} collective-permute-done((bf16[2,80,512]{2,1,0:T(8,128)(2,1)S(1)}, bf16[2,80,512]{2,1,0:T(8,128)(2,1)S(1)}, u32[]{:S(2)}, u32[]{:S(2)}) %collective-permute-start.4) | collective-permute-done | bytes 163872 | tf_op jit(solution)/shard_map/ppermute | solution.py:31
  44.7 0.7 slice_reduce_fusion
  46.1 8.7 %output_project.1 = (bf16[1024,4096]{1,0:T(8,128)(2,1)}, f32[2,4,64,512]{3,2,1,0:T(8,128)S(1)}, f32[4,2,64,512]{3,2,1,0:T(8,128)S(1)}) custom-call(s32[1]{0:T(128)} %bitcast.place, bf16[64,1024]{1,0:T(8,128)(2,1)S(1)} %fusion.7.lower, bf16[4,2,80,512]{3,2,1,0:T(8,128)(2,1)S(1)} %pad_maximum_fusion.upper, bf16[1024,4096]{1,0:T(8,128)(2,1)} %base.1, ...), custom_call_target="tpu_custom_call" | custom-call | flops 1610612736 | bytes 16777216 | tf_op jit(solution)/shard_map/output_project/pallas_call | solution.py:283
  54.9 1.7 %collective-permute-start.12 = (f16[4,64,512]{2,1,0:T(8,128)(2,1)S(1)}, f16[4,64,512]{2,1,0:T(8,128)(2,1)S(1)}, u32[]{:S(2)}, u32[]{:S(2)}) collective-permute-start(f16[4,64,512]{2,1,0:T(8,128)(2,1)S(1)} %fusion), channel_id=1, source_target_pairs={{0,1},{1,0},{2,3},{3,2},{4,5},{5,4},{6,7},{7,6},{8,9},{9,8},{10,11... | collective-permute-start | bytes 786440 | tf_op jit(solution)/shard_map/ppermute | solution.py:31
  56.7 1.7 %collective-permute-start.15 = (f16[2,64,512]{2,1,0:T(8,128)(2,1)S(1)}, f16[2,64,512]{2,1,0:T(8,128)(2,1)S(1)}, u32[]{:S(2)}, u32[]{:S(2)}) collective-permute-start(f16[2,64,512]{2,1,0:T(8,128)(2,1)S(1)} %get-tuple-element.32), channel_id=1, source_target_pairs={{0,6},{1,7},{2,4},{3,5},{4,2},{5,3},{6,0},{7,1},{8,14},{9,15},{10,... | collective-permute-start | bytes 393224 | tf_op jit(solution)/shard_map/ppermute | solution.py:31
  58.4 2.8 %collective-permute-start.14 = (f16[2,64,512]{2,1,0:T(8,128)(2,1)S(1)}, f16[2,64,512]{2,1,0:T(8,128)(2,1)S(1)}, u32[]{:S(2)}, u32[]{:S(2)}) collective-permute-start(f16[2,64,512]{2,1,0:T(8,128)(2,1)S(1)} %get-tuple-element.33), channel_id=1, source_target_pairs={{0,4},{1,5},{2,6},{3,7},{4,0},{5,1},{6,2},{7,3},{8,12},{9,13},{10,... | collective-permute-start | bytes 393224 | tf_op jit(solution)/shard_map/ppermute | solution.py:31
  61.4 1.6 %collective-permute-done.12 = f16[4,64,512]{2,1,0:T(8,128)(2,1)S(1)} collective-permute-done((f16[4,64,512]{2,1,0:T(8,128)(2,1)S(1)}, f16[4,64,512]{2,1,0:T(8,128)(2,1)S(1)}, u32[]{:S(2)}, u32[]{:S(2)}) %collective-permute-start.12) | collective-permute-done | bytes 262176 | tf_op jit(solution)/shard_map/ppermute | solution.py:31
  63.2 2.8 %collective-permute-start.16 = (f16[64,512]{1,0:T(8,128)(2,1)S(1)}, f16[64,512]{1,0:T(8,128)(2,1)S(1)}, u32[]{:S(2)}, u32[]{:S(2)}) collective-permute-start(f16[64,512]{1,0:T(8,128)(2,1)S(1)} %get-tuple-element.39), channel_id=1, source_target_pairs={{0,2},{1,3},{2,0},{3,1},{4,6},{5,7},{6,4},{7,5},{8,10},{9,11},{10,... | collective-permute-start | bytes 196616 | tf_op jit(solution)/shard_map/ppermute | solution.py:31
  66.0 3.1 %collective-permute-start.18 = (f16[64,512]{1,0:T(8,128)(2,1)S(1)}, f16[64,512]{1,0:T(8,128)(2,1)S(1)}, u32[]{:S(2)}, u32[]{:S(2)}) collective-permute-start(f16[64,512]{1,0:T(8,128)(2,1)S(1)} %get-tuple-element.40), channel_id=1, source_target_pairs={{0,6},{1,7},{2,4},{3,5},{4,2},{5,3},{6,0},{7,1},{8,14},{9,15},{10,... | collective-permute-start | bytes 196616 | tf_op jit(solution)/shard_map/ppermute | solution.py:31
  69.1 0.9 collective-permute-start.17
  70.0 4.9 %collective-permute-done.14 = f16[2,64,512]{2,1,0:T(8,128)(2,1)S(1)} collective-permute-done((f16[2,64,512]{2,1,0:T(8,128)(2,1)S(1)}, f16[2,64,512]{2,1,0:T(8,128)(2,1)S(1)}, u32[]{:S(2)}, u32[]{:S(2)}) %collective-permute-start.14) | collective-permute-done | bytes 131104 | tf_op jit(solution)/shard_map/ppermute | solution.py:31
  75.6 2.0 %collective-permute-done.17 = f16[64,512]{1,0:T(8,128)(2,1)S(1)} collective-permute-done((f16[64,512]{1,0:T(8,128)(2,1)S(1)}, f16[64,512]{1,0:T(8,128)(2,1)S(1)}, u32[]{:S(2)}, u32[]{:S(2)}) %collective-permute-start.17) | collective-permute-done | bytes 65568 | tf_op jit(solution)/shard_map/ppermute | solution.py:31
  77.6 1.8 %collective-permute-start.21 = (f16[64,512]{1,0:T(8,128)(2,1)S(1)}, f16[64,512]{1,0:T(8,128)(2,1)S(1)}, u32[]{:S(2)}, u32[]{:S(2)}) collective-permute-start(f16[64,512]{1,0:T(8,128)(2,1)S(1)} %fusion.6), channel_id=1, source_target_pairs={{0,6},{1,7},{2,4},{3,5},{4,2},{5,3},{6,0},{7,1},{8,14},{9,15},{10,... | collective-permute-start | bytes 196616 | tf_op jit(solution)/shard_map/ppermute | solution.py:31
  79.4 2.7 %collective-permute-start.19 = (f16[64,512]{1,0:T(8,128)(2,1)S(1)}, f16[64,512]{1,0:T(8,128)(2,1)S(1)}, u32[]{:S(2)}, u32[]{:S(2)}) collective-permute-start(f16[64,512]{1,0:T(8,128)(2,1)S(1)} %fusion.6), channel_id=1, source_target_pairs={{0,2},{1,3},{2,0},{3,1},{4,6},{5,7},{6,4},{7,5},{8,10},{9,11},{10,... | collective-permute-start | bytes 196616 | tf_op jit(solution)/shard_map/ppermute | solution.py:31
  82.1 1.8 %collective-permute-start.27 = (f16[2,64,512]{2,1,0:T(8,128)(2,1)S(1)}, f16[2,64,512]{2,1,0:T(8,128)(2,1)S(1)}, u32[]{:S(2)}, u32[]{:S(2)}) collective-permute-start(f16[2,64,512]{2,1,0:T(8,128)(2,1)S(1)} %add_convert_fusion), channel_id=1, source_target_pairs={{0,6},{1,7},{2,4},{3,5},{4,2},{5,3},{6,0},{7,1},{8,14},{9,15},{10,... | collective-permute-start | bytes 393224 | tf_op jit(solution)/shard_map/ppermute | solution.py:31
  83.9 0.6 collective-permute-done.21
  84.5 2.1 %collective-permute-start.25 = (f16[2,64,512]{2,1,0:T(8,128)(2,1)S(1)}, f16[2,64,512]{2,1,0:T(8,128)(2,1)S(1)}, u32[]{:S(2)}, u32[]{:S(2)}) collective-permute-start(f16[2,64,512]{2,1,0:T(8,128)(2,1)S(1)} %add_convert_fusion), channel_id=1, source_target_pairs={{0,2},{1,3},{2,0},{3,1},{4,6},{5,7},{6,4},{7,5},{8,10},{9,11},{10,... | collective-permute-start | bytes 393224 | tf_op jit(solution)/shard_map/ppermute | solution.py:31
  86.7 4.1 %collective-permute-done.20 = f16[64,512]{1,0:T(8,128)(2,1)S(1)} collective-permute-done((f16[64,512]{1,0:T(8,128)(2,1)S(1)}, f16[64,512]{1,0:T(8,128)(2,1)S(1)}, u32[]{:S(2)}, u32[]{:S(2)}) %collective-permute-start.20) | collective-permute-done | bytes 65568 | tf_op jit(solution)/shard_map/ppermute | solution.py:31
  91.4 6.1 %collective-permute-done.26 = f16[2,64,512]{2,1,0:T(8,128)(2,1)S(1)} collective-permute-done((f16[2,64,512]{2,1,0:T(8,128)(2,1)S(1)}, f16[2,64,512]{2,1,0:T(8,128)(2,1)S(1)}, u32[]{:S(2)}, u32[]{:S(2)}) %collective-permute-start.26) | collective-permute-done | bytes 131104 | tf_op jit(solution)/shard_map/ppermute | solution.py:31
  98.1 2.9 %finish.1 = (bf16[64,8192]{1,0:T(8,128)(2,1)}, bf16[64,8192]{1,0:T(8,128)(2,1)}) custom-call(s32[2]{0:T(128)S(1)} %pad_add_fusion.place, f32[1]{0:T(128)} %bitcast.10.bound, bf16[64,8192]{1,0:T(8,128)(2,1)S(1)} %bitcast.66, bf16[1,8192]{1,0:T(2,128)(2,1)S(1)} %broadcast_in_dim.7.gain, f32[8,64,512]{2,1,0:T(8,128)S(1)} %bitcast.67, ...), custom_call_target="tpu_custom_call" | custom-call | flops 4194304 | bytes 7340032 | tf_op jit(solution)/shard_map/finish/pallas_call | solution.py:338
  (89 shorter events, 4.7 us)
Async XLA Ops:
  0.6 10.5 %copy-start = (bf16[8,8,8192]{2,1,0:T(8,128)(2,1)S(1)}, bf16[8,8,8192]{2,1,0:T(8,128)(2,1)}, u32[]{:S(2)}) copy-start(bf16[8,8,8192]{2,1,0:T(8,128)(2,1)} %param.14) | copy-start | bytes 3145732
  0.6 12.2 %collective-permute-start.6 = (bf16[64,512]{1,0:T(8,128)(2,1)}, bf16[64,512]{1,0:T(8,128)(2,1)S(1)}, u32[]{:S(2)}, u32[]{:S(2)}) collective-permute-start(bf16[64,512]{1,0:T(8,128)(2,1)} %bitcast.86), channel_id=1, source_target_pairs={{0,4},{1,5},{2,6},{3,7},{4,0},{5,1},{6,2},{7,3},{8,12},{9,13},{10,... | collective-permute-start | bytes 196616 | tf_op jit(solution)/shard_map/ppermute | solution.py:31
  4.7 8.1 %collective-permute-start.5 = (bf16[64,512]{1,0:T(8,128)(2,1)}, bf16[64,512]{1,0:T(8,128)(2,1)S(1)}, u32[]{:S(2)}, u32[]{:S(2)}) collective-permute-start(bf16[64,512]{1,0:T(8,128)(2,1)} %bitcast.87), channel_id=1, source_target_pairs={{0,2},{1,3},{2,0},{3,1},{4,6},{5,7},{6,4},{7,5},{8,10},{9,11},{10,... | collective-permute-start | bytes 196616 | tf_op jit(solution)/shard_map/ppermute | solution.py:31
  6.3 6.5 %collective-permute-start.7 = (bf16[64,512]{1,0:T(8,128)(2,1)}, bf16[64,512]{1,0:T(8,128)(2,1)S(1)}, u32[]{:S(2)}, u32[]{:S(2)}) collective-permute-start(bf16[64,512]{1,0:T(8,128)(2,1)} %bitcast.88), channel_id=1, source_target_pairs={{0,6},{1,7},{2,4},{3,5},{4,2},{5,3},{6,0},{7,1},{8,14},{9,15},{10,... | collective-permute-start | bytes 196616 | tf_op jit(solution)/shard_map/ppermute | solution.py:31
  7.0 5.9 %copy-start.6 = (bf16[512,64]{0,1:T(8,128)(2,1)S(1)}, bf16[512,64]{0,1:T(8,128)(2,1)}, u32[]{:S(2)}) copy-start(bf16[512,64]{0,1:T(8,128)(2,1)} %param.20) | copy-start | bytes 196612
  11.0 7.1 %collective-permute-start = (bf16[80,1024]{1,0:T(8,128)(2,1)S(1)}, bf16[80,1024]{1,0:T(8,128)(2,1)S(1)}, u32[]{:S(2)}, u32[]{:S(2)}) collective-permute-start(bf16[80,1024]{1,0:T(8,128)(2,1)S(1)} %pad_maximum_fusion.4), channel_id=1, source_target_pairs={{0,8},{8,0},{1,9},{9,1},{2,10},{10,2},{3,11},{11,3},{4,12},{12,4},... | collective-permute-start | bytes 491528 | tf_op jit(solution)/shard_map/ppermute | solution.py:35
  11.9 9.9 %collective-permute-start.9 = (bf16[64,4096]{1,0:T(8,128)(2,1)S(1)}, bf16[64,4096]{1,0:T(8,128)(2,1)S(1)}, u32[]{:S(2)}, u32[]{:S(2)}) collective-permute-start(bf16[64,4096]{1,0:T(8,128)(2,1)S(1)} %get-tuple-element.35), channel_id=1, source_target_pairs={{0,8},{8,0},{1,9},{9,1},{2,10},{10,2},{3,11},{11,3},{4,12},{12,4},... | collective-permute-start | bytes 1572872 | tf_op jit(solution)/shard_map/ppermute | solution.py:35
  12.9 8.9 %collective-permute-start.8 = (bf16[4,64,512]{2,1,0:T(8,128)(2,1)S(1)}, bf16[4,64,512]{2,1,0:T(8,128)(2,1)S(1)}, u32[]{:S(2)}, u32[]{:S(2)}) collective-permute-start(bf16[4,64,512]{2,1,0:T(8,128)(2,1)S(1)} %pad_maximum_fusion.2.near), channel_id=1, source_target_pairs={{0,1},{1,0},{2,3},{3,2},{4,5},{5,4},{6,7},{7,6},{8,9},{9,8},{10,11... | collective-permute-start | bytes 786440 | tf_op jit(solution)/shard_map/ppermute | solution.py:31
  18.2 10.3 %collective-permute-start.1 = (bf16[80,512]{1,0:T(8,128)(2,1)S(1)}, bf16[80,512]{1,0:T(8,128)(2,1)S(1)}, u32[]{:S(2)}, u32[]{:S(2)}) collective-permute-start(bf16[80,512]{1,0:T(8,128)(2,1)S(1)} %get-tuple-element.47), channel_id=1, source_target_pairs={{0,1},{1,0},{2,3},{3,2},{4,5},{5,4},{6,7},{7,6},{8,9},{9,8},{10,11... | collective-permute-start | bytes 245768 | tf_op jit(solution)/shard_map/ppermute | solution.py:31
  21.8 6.6 %copy-start.9 = (bf16[1024]{0:T(1024)(128)(2,1)S(1)}, bf16[1024]{0:T(1024)(128)(2,1)}, u32[]{:S(2)}) copy-start(bf16[1024]{0:T(1024)(128)(2,1)} %param.18) | copy-start | bytes 6148
  28.3 4.9 %collective-permute-start.10 = (f32[64,1024]{1,0:T(8,128)S(1)}, f32[64,1024]{1,0:T(8,128)S(1)}, u32[]{:S(2)}, u32[]{:S(2)}) collective-permute-start(f32[64,1024]{1,0:T(8,128)S(1)} %get-tuple-element.19), channel_id=1, source_target_pairs={{0,8},{8,0},{1,9},{9,1},{2,10},{10,2},{3,11},{11,3},{4,12},{12,4},... | collective-permute-start | bytes 786440 | tf_op jit(solution)/shard_map/ppermute | solution.py:35
  28.5 12.5 %collective-permute-start.3 = (bf16[2,80,512]{2,1,0:T(8,128)(2,1)S(1)}, bf16[2,80,512]{2,1,0:T(8,128)(2,1)S(1)}, u32[]{:S(2)}, u32[]{:S(2)}) collective-permute-start(bf16[2,80,512]{2,1,0:T(8,128)(2,1)S(1)} %get-tuple-element.45), channel_id=1, source_target_pairs={{0,4},{1,5},{2,6},{3,7},{4,0},{5,1},{6,2},{7,3},{8,12},{9,13},{10,... | collective-permute-start | bytes 491528 | tf_op jit(solution)/shard_map/ppermute | solution.py:31
  30.7 10.3 %collective-permute-start.2 = (bf16[2,80,512]{2,1,0:T(8,128)(2,1)S(1)}, bf16[2,80,512]{2,1,0:T(8,128)(2,1)S(1)}, u32[]{:S(2)}, u32[]{:S(2)}) collective-permute-start(bf16[2,80,512]{2,1,0:T(8,128)(2,1)S(1)} %get-tuple-element.45), channel_id=1, source_target_pairs={{0,2},{1,3},{2,0},{3,1},{4,6},{5,7},{6,4},{7,5},{8,10},{9,11},{10,... | collective-permute-start | bytes 491528 | tf_op jit(solution)/shard_map/ppermute | solution.py:31
  33.2 11.5 %collective-permute-start.4 = (bf16[2,80,512]{2,1,0:T(8,128)(2,1)S(1)}, bf16[2,80,512]{2,1,0:T(8,128)(2,1)S(1)}, u32[]{:S(2)}, u32[]{:S(2)}) collective-permute-start(bf16[2,80,512]{2,1,0:T(8,128)(2,1)S(1)} %get-tuple-element.45), channel_id=1, source_target_pairs={{0,6},{1,7},{2,4},{3,5},{4,2},{5,3},{6,0},{7,1},{8,14},{9,15},{10,... | collective-permute-start | bytes 491528 | tf_op jit(solution)/shard_map/ppermute | solution.py:31
  40.9 5.2 %collective-permute-start.11 = (bf16[64,1024]{1,0:T(8,128)(2,1)S(1)}, bf16[64,1024]{1,0:T(8,128)(2,1)S(1)}, u32[]{:S(2)}, u32[]{:S(2)}) collective-permute-start(bf16[64,1024]{1,0:T(8,128)(2,1)S(1)} %attend.1.mine), channel_id=1, source_target_pairs={{0,8},{8,0},{1,9},{9,1},{2,10},{10,2},{3,11},{11,3},{4,12},{12,4},... | collective-permute-start | bytes 393224 | tf_op jit(solution)/shard_map/ppermute | solution.py:35
  54.8 31.9 %copy-start.8 = (bf16[8192]{0:T(1024)(128)(2,1)S(1)}, bf16[8192]{0:T(1024)(128)(2,1)}, u32[]{:S(2)}) copy-start(bf16[8192]{0:T(1024)(128)(2,1)} %param.16) | copy-start | bytes 49156
  54.9 8.1 %collective-permute-start.12 = (f16[4,64,512]{2,1,0:T(8,128)(2,1)S(1)}, f16[4,64,512]{2,1,0:T(8,128)(2,1)S(1)}, u32[]{:S(2)}, u32[]{:S(2)}) collective-permute-start(f16[4,64,512]{2,1,0:T(8,128)(2,1)S(1)} %fusion), channel_id=1, source_target_pairs={{0,1},{1,0},{2,3},{3,2},{4,5},{5,4},{6,7},{7,6},{8,9},{9,8},{10,11... | collective-permute-start | bytes 786440 | tf_op jit(solution)/shard_map/ppermute | solution.py:31
  56.7 12.4 %collective-permute-start.15 = (f16[2,64,512]{2,1,0:T(8,128)(2,1)S(1)}, f16[2,64,512]{2,1,0:T(8,128)(2,1)S(1)}, u32[]{:S(2)}, u32[]{:S(2)}) collective-permute-start(f16[2,64,512]{2,1,0:T(8,128)(2,1)S(1)} %get-tuple-element.32), channel_id=1, source_target_pairs={{0,6},{1,7},{2,4},{3,5},{4,2},{5,3},{6,0},{7,1},{8,14},{9,15},{10,... | collective-permute-start | bytes 393224 | tf_op jit(solution)/shard_map/ppermute | solution.py:31
  58.4 16.4 %collective-permute-start.14 = (f16[2,64,512]{2,1,0:T(8,128)(2,1)S(1)}, f16[2,64,512]{2,1,0:T(8,128)(2,1)S(1)}, u32[]{:S(2)}, u32[]{:S(2)}) collective-permute-start(f16[2,64,512]{2,1,0:T(8,128)(2,1)S(1)} %get-tuple-element.33), channel_id=1, source_target_pairs={{0,4},{1,5},{2,6},{3,7},{4,0},{5,1},{6,2},{7,3},{8,12},{9,13},{10,... | collective-permute-start | bytes 393224 | tf_op jit(solution)/shard_map/ppermute | solution.py:31
  61.2 13.6 %collective-permute-start.13 = (f16[2,64,512]{2,1,0:T(8,128)(2,1)S(1)}, f16[2,64,512]{2,1,0:T(8,128)(2,1)S(1)}, u32[]{:S(2)}, u32[]{:S(2)}) collective-permute-start(f16[2,64,512]{2,1,0:T(8,128)(2,1)S(1)} %get-tuple-element.34), channel_id=1, source_target_pairs={{0,2},{1,3},{2,0},{3,1},{4,6},{5,7},{6,4},{7,5},{8,10},{9,11},{10,... | collective-permute-start | bytes 393224 | tf_op jit(solution)/shard_map/ppermute | solution.py:31
  63.2 11.7 %collective-permute-start.16 = (f16[64,512]{1,0:T(8,128)(2,1)S(1)}, f16[64,512]{1,0:T(8,128)(2,1)S(1)}, u32[]{:S(2)}, u32[]{:S(2)}) collective-permute-start(f16[64,512]{1,0:T(8,128)(2,1)S(1)} %get-tuple-element.39), channel_id=1, source_target_pairs={{0,2},{1,3},{2,0},{3,1},{4,6},{5,7},{6,4},{7,5},{8,10},{9,11},{10,... | collective-permute-start | bytes 196616 | tf_op jit(solution)/shard_map/ppermute | solution.py:31
  66.0 9.6 %collective-permute-start.18 = (f16[64,512]{1,0:T(8,128)(2,1)S(1)}, f16[64,512]{1,0:T(8,128)(2,1)S(1)}, u32[]{:S(2)}, u32[]{:S(2)}) collective-permute-start(f16[64,512]{1,0:T(8,128)(2,1)S(1)} %get-tuple-element.40), channel_id=1, source_target_pairs={{0,6},{1,7},{2,4},{3,5},{4,2},{5,3},{6,0},{7,1},{8,14},{9,15},{10,... | collective-permute-start | bytes 196616 | tf_op jit(solution)/shard_map/ppermute | solution.py:31
  69.1 8.5 %collective-permute-start.17 = (f16[64,512]{1,0:T(8,128)(2,1)S(1)}, f16[64,512]{1,0:T(8,128)(2,1)S(1)}, u32[]{:S(2)}, u32[]{:S(2)}) collective-permute-start(f16[64,512]{1,0:T(8,128)(2,1)S(1)} %get-tuple-element.41), channel_id=1, source_target_pairs={{0,4},{1,5},{2,6},{3,7},{4,0},{5,1},{6,2},{7,3},{8,12},{9,13},{10,... | collective-permute-start | bytes 196616 | tf_op jit(solution)/shard_map/ppermute | solution.py:31
  74.9 7.1 %collective-permute-start.24 = (f16[2,64,512]{2,1,0:T(8,128)(2,1)S(1)}, f16[2,64,512]{2,1,0:T(8,128)(2,1)S(1)}, u32[]{:S(2)}, u32[]{:S(2)}) collective-permute-start(f16[2,64,512]{2,1,0:T(8,128)(2,1)S(1)} %fusion.1), channel_id=1, source_target_pairs={{0,9},{1,8},{2,11},{3,10},{4,13},{5,12},{6,15},{7,14},{8,1},{9,0},... | collective-permute-start | bytes 393224 | tf_op jit(solution)/shard_map/ppermute | solution.py:351
  75.0 7.0 %collective-permute-start.23 = (f16[2,64,512]{2,1,0:T(8,128)(2,1)S(1)}, f16[2,64,512]{2,1,0:T(8,128)(2,1)S(1)}, u32[]{:S(2)}, u32[]{:S(2)}) collective-permute-start(f16[2,64,512]{2,1,0:T(8,128)(2,1)S(1)} %fusion.1), channel_id=1, source_target_pairs={{0,8},{8,0},{1,9},{9,1},{2,10},{10,2},{3,11},{11,3},{4,12},{12,4},... | collective-permute-start | bytes 393224 | tf_op jit(solution)/shard_map/ppermute | solution.py:35
  77.6 6.9 %collective-permute-start.21 = (f16[64,512]{1,0:T(8,128)(2,1)S(1)}, f16[64,512]{1,0:T(8,128)(2,1)S(1)}, u32[]{:S(2)}, u32[]{:S(2)}) collective-permute-start(f16[64,512]{1,0:T(8,128)(2,1)S(1)} %fusion.6), channel_id=1, source_target_pairs={{0,6},{1,7},{2,4},{3,5},{4,2},{5,3},{6,0},{7,1},{8,14},{9,15},{10,... | collective-permute-start | bytes 196616 | tf_op jit(solution)/shard_map/ppermute | solution.py:31
  79.4 11.4 %collective-permute-start.20 = (f16[64,512]{1,0:T(8,128)(2,1)S(1)}, f16[64,512]{1,0:T(8,128)(2,1)S(1)}, u32[]{:S(2)}, u32[]{:S(2)}) collective-permute-start(f16[64,512]{1,0:T(8,128)(2,1)S(1)} %fusion.6), channel_id=1, source_target_pairs={{0,4},{1,5},{2,6},{3,7},{4,0},{5,1},{6,2},{7,3},{8,12},{9,13},{10,... | collective-permute-start | bytes 196616 | tf_op jit(solution)/shard_map/ppermute | solution.py:31
  79.4 11.4 %collective-permute-start.19 = (f16[64,512]{1,0:T(8,128)(2,1)S(1)}, f16[64,512]{1,0:T(8,128)(2,1)S(1)}, u32[]{:S(2)}, u32[]{:S(2)}) collective-permute-start(f16[64,512]{1,0:T(8,128)(2,1)S(1)} %fusion.6), channel_id=1, source_target_pairs={{0,2},{1,3},{2,0},{3,1},{4,6},{5,7},{6,4},{7,5},{8,10},{9,11},{10,... | collective-permute-start | bytes 196616 | tf_op jit(solution)/shard_map/ppermute | solution.py:31
  82.1 9.3 %collective-permute-start.27 = (f16[2,64,512]{2,1,0:T(8,128)(2,1)S(1)}, f16[2,64,512]{2,1,0:T(8,128)(2,1)S(1)}, u32[]{:S(2)}, u32[]{:S(2)}) collective-permute-start(f16[2,64,512]{2,1,0:T(8,128)(2,1)S(1)} %add_convert_fusion), channel_id=1, source_target_pairs={{0,6},{1,7},{2,4},{3,5},{4,2},{5,3},{6,0},{7,1},{8,14},{9,15},{10,... | collective-permute-start | bytes 393224 | tf_op jit(solution)/shard_map/ppermute | solution.py:31
  83.9 13.7 %collective-permute-start.26 = (f16[2,64,512]{2,1,0:T(8,128)(2,1)S(1)}, f16[2,64,512]{2,1,0:T(8,128)(2,1)S(1)}, u32[]{:S(2)}, u32[]{:S(2)}) collective-permute-start(f16[2,64,512]{2,1,0:T(8,128)(2,1)S(1)} %add_convert_fusion), channel_id=1, source_target_pairs={{0,4},{1,5},{2,6},{3,7},{4,0},{5,1},{6,2},{7,3},{8,12},{9,13},{10,... | collective-permute-start | bytes 393224 | tf_op jit(solution)/shard_map/ppermute | solution.py:31
  84.5 13.1 %collective-permute-start.25 = (f16[2,64,512]{2,1,0:T(8,128)(2,1)S(1)}, f16[2,64,512]{2,1,0:T(8,128)(2,1)S(1)}, u32[]{:S(2)}, u32[]{:S(2)}) collective-permute-start(f16[2,64,512]{2,1,0:T(8,128)(2,1)S(1)} %add_convert_fusion), channel_id=1, source_target_pairs={{0,2},{1,3},{2,0},{3,1},{4,6},{5,7},{6,4},{7,5},{8,10},{9,11},{10,... | collective-permute-start | bytes 393224 | tf_op jit(solution)/shard_map/ppermute | solution.py:31
  90.9 7.0 %collective-permute-start.22 = (f16[4,64,512]{2,1,0:T(8,128)(2,1)S(1)}, f16[4,64,512]{2,1,0:T(8,128)(2,1)S(1)}, u32[]{:S(2)}, u32[]{:S(2)}) collective-permute-start(f16[4,64,512]{2,1,0:T(8,128)(2,1)S(1)} %get-tuple-element.38), channel_id=1, source_target_pairs={{0,1},{1,0},{2,3},{3,2},{4,5},{5,4},{6,7},{7,6},{8,9},{9,8},{10,11... | collective-permute-start | bytes 786440 | tf_op jit(solution)/shard_map/ppermute | solution.py:31
  (7 other events, 29.5 us)

commit v4 on v3

--- a/solution.py
+++ b/solution.py
@@ -71,11 +71,14 @@
     )(in_hbm(value))
 
 
-def reach_kernel(lengths, values, bound, held, arrived):
+def reach_kernel(lengths, values, upper, message, held, arrived, factor, factor_arrived):
     rows, slots, head_dim = values.shape
+    rank, width = upper.shape
     copies = [
         pltpu.make_async_copy(values.at[row], held.at[row], arrived.at[row]) for row in range(rows)
     ]
+    columns = pltpu.make_async_copy(upper, factor, factor_arrived)
+    columns.start()
     for copy in copies:
         copy.start()
     slot = lax.broadcasted_iota(jnp.int32, (slots, head_dim), 0)
@@ -84,23 +87,29 @@
         copies[row].wait()
         size = jnp.where(slot < lengths[row], jnp.abs(held[row].astype(F32)), 0.0)
         top = jnp.maximum(top, jnp.max(size.reshape(-1, 8, head_dim), axis=0))
-    bound[...] = jnp.broadcast_to(jnp.max(top), bound.shape).astype(BF16)
-
-
-def largest_in_reach(lengths, values, columns):
+    columns.wait()
+    for first in range(0, width, 128):
+        message[first // 128 * rank : (first // 128 + 1) * rank] = factor[:, first : first + 128]
+    message[width // 128 * rank :] = jnp.broadcast_to(jnp.max(top), (16, 128)).astype(BF16)
+
+
+def with_largest_in_reach(lengths, values, upper):
+    rank, width = upper.shape
     return pl.pallas_call(
         reach_kernel,
-        in_specs=[SMEM, ANY],
+        in_specs=[SMEM, ANY, ANY],
         out_specs=VMEM,
-        out_shape=jax.ShapeDtypeStruct((16, columns), BF16),
+        out_shape=jax.ShapeDtypeStruct((width // 128 * rank + 16, 128), BF16),
         scratch_shapes=[
             pltpu.VMEM(values.shape, BF16),
             pltpu.SemaphoreType.DMA((values.shape[0],)),
+            pltpu.VMEM(upper.shape, BF16),
+            pltpu.SemaphoreType.DMA,
         ],
         compiler_params=params(8),
         cost_estimate=cost(4 * values.size, 2 * values.size),
-        name="largest_in_reach",
-    )(lengths, in_hbm(values))
+        name="with_largest_in_reach",
+    )(lengths, in_hbm(values), in_hbm(upper))
 
 
 def query_kernel(
@@ -164,7 +173,6 @@
 ):
     rows, slots, head_dim = keys.shape
     heads = own.shape[1] // head_dim
-    group = 2
     copies = []
     for row in range(rows):
         copies.append(
@@ -178,34 +186,52 @@
     slot = lax.broadcasted_iota(jnp.int32, (heads * steps, slots), 1)
     step = lax.broadcasted_iota(jnp.int32, (heads * steps, slots), 0) % steps
     behind = slot - step
-    for first in range(0, rows, group):
-        span = slice(first * steps, (first + group) * steps)
+    many = heads * steps
+    nothing = jnp.zeros((many, head_dim), F32)
+    for first in range(0, rows, 2):
+        pair = (first, first + 1)
+        span = slice(first * steps, (first + 2) * steps)
         query = (own[span] + other[span]) * scale + bias[...].astype(F32)
         turned = []
         for head in range(heads):
             part = query[:, head * head_dim : (head + 1) * head_dim]
             part = part * cosine[span] + pltpu.roll(part, head_dim // 2, 1) * sine[span]
             turned.append(part * head_dim ** (-0.5))
-        gathered = []
-        for row in range(group):
-            for copy in copies[first + row]:
-                copy.wait()
-            queries = jnp.concatenate(
-                [q[row * steps : (row + 1) * steps] for q in turned], axis=0
-            ).astype(BF16)
-            scores = lax.dot_general(
-                queries,
-                keys_held[first + row],
-                (((1,), (1,)), ((), ())),
-                preferred_element_type=F32,
-            )
-            scores = jnp.where(behind <= lengths[first + row] - steps, scores, F32(-1e30))
-            top = jnp.max(scores, axis=-1, keepdims=True)
-            weights = jnp.exp(scores - top)
-            probs = (weights / jnp.sum(weights, axis=-1, keepdims=True)).astype(BF16)
-            gathered.append(
-                jnp.dot(probs, values_held[first + row], preferred_element_type=F32)
-            )
+        upper, lower = [
+            jnp.concatenate([q[i * steps : (i + 1) * steps] for q in turned], axis=0) for i in (0, 1)
+        ]
+        queries = jnp.concatenate(
+            [
+                jnp.concatenate([upper, nothing], axis=1),
+                jnp.concatenate([nothing, lower], axis=1),
+            ],
+            axis=0,
+        ).astype(BF16)
+        for row in pair:
+            copies[row][0].wait()
+        both = jnp.concatenate([keys_held[row] for row in pair], axis=1)
+        scores = lax.dot_general(
+            queries, both, (((1,), (1,)), ((), ())), preferred_element_type=F32
+        )
+        scores = jnp.concatenate(
+            [
+                jnp.where(
+                    behind <= lengths[first + i] - steps,
+                    scores[i * many : (i + 1) * many],
+                    F32(-1e30),
+                )
+                for i in (0, 1)
+            ],
+            axis=0,
+        )
+        top = jnp.max(scores, axis=-1, keepdims=True)
+        weights = jnp.exp(scores - top)
+        probs = (weights / jnp.sum(weights, axis=-1, keepdims=True)).astype(BF16)
+        for row in pair:
+            copies[row][1].wait()
+        both = jnp.concatenate([values_held[row] for row in pair], axis=1)
+        mixed = jnp.dot(probs, both, preferred_element_type=F32)
+        gathered = (mixed[:many, :head_dim], mixed[many:, head_dim:])
         for head in range(heads):
             context[span, head * head_dim : (head + 1) * head_dim] = jnp.concatenate(
                 [g[head * steps : (head + 1) * steps] for g in gathered], axis=0
@@ -236,7 +262,7 @@
 ):
     outer = upper.shape[0]
     rank = lower.shape[0]
-    width = upper.shape[3]
+    width = fresh.shape[2]
     rows = mine.shape[0]
 
     def columns(k):
@@ -261,7 +287,8 @@
             def _():
                 out.wait()
 
-            update = contract_first(lower[...], upper[z, y, :rank])
+            factor = [upper[z, y, n * rank : (n + 1) * rank] for n in range(width // 128)]
+            update = contract_first(lower[...], jnp.concatenate(factor, axis=1))
             fetch(k).wait()
             fresh[y] = (held[k].astype(F32) + update).astype(BF16)
             out.start()
@@ -277,7 +304,7 @@
 
 def output_project(place, lower, upper, base, mine, theirs):
     outer = upper.shape[0]
-    width = upper.shape[3]
+    width = base.shape[1] // (2 * outer)
     depth = base.shape[0]
     rows = mine.shape[0]
     return pl.pallas_call(
@@ -301,44 +328,55 @@
     )(place, lower, upper, in_hbm(base), mine, theirs)
 
 
-def finish_kernel(place, bound, hidden, gain, near, far, residual, normed, combined):
+def finish_kernel(place, bound, hidden, gain, near, far, residual, normed, combined, held, left):
     blocks, rows, width = near.shape
     half = blocks * width
-    squares = jnp.zeros((rows, 1), F32)
-    for pieces, which in ((near, place[1]), (far, 1 - place[1])):
-        for k in range(blocks):
-            start = pl.multiple_of(which * half + (place[0] ^ k) * width, width)
-            total = hidden[:, pl.ds(start, width)].astype(F32) + pieces[k] * bound[0]
-            combined[:, pl.ds(start, width)] = total
-            residual[:, pl.ds(start, width)] = total.astype(BF16)
-            squares += jnp.sum(total * total, axis=-1, keepdims=True)
-    inverse = lax.rsqrt(squares / (2 * half) + NORM_EPS)
-    normed[...] = (combined[...] * inverse * gain[...].astype(F32)).astype(BF16)
+    tall = combined.shape[0]
+
+    def put(which, out, first):
+        slot = first // tall % 2
+        return pltpu.make_async_copy(
+            held.at[which, slot], out.at[pl.ds(first, tall)], left.at[which, slot]
+        )
+
+    for first in range(0, rows, tall):
+        slot = first // tall % 2
+        if first >= 2 * tall:
+            put(0, residual, first - 2 * tall).wait()
+            put(1, normed, first - 2 * tall).wait()
+        squares = jnp.zeros((tall, 128), F32)
+        for pieces, which in ((near, place[1]), (far, 1 - place[1])):
+            for k in range(blocks):
+                start = pl.multiple_of(which * half + (place[0] ^ k) * width, width)
+                total = hidden[first : first + tall, pl.ds(start, width)].astype(F32)
+                total += pieces[k, first : first + tall] * bound[0]
+                combined[:, pl.ds(start, width)] = total
+                held[0, slot, :, pl.ds(start, width)] = total.astype(BF16)
+                for lane in range(0, width, 128):
+                    squares += total[:, lane : lane + 128] * total[:, lane : lane + 128]
+        put(0, residual, first).start()
+        mean = jnp.sum(squares, axis=-1, keepdims=True) / (2 * half)
+        inverse = lax.rsqrt(mean + NORM_EPS)
+        held[1, slot] = (combined[...] * inverse * gain[...].astype(F32)).astype(BF16)
+        put(1, normed, first).start()
+    for first in range(max(rows - 2 * tall, 0), rows, tall):
+        put(0, residual, first).wait()
+        put(1, normed, first).wait()
 
 
 def finish(place, bound, hidden, gain, near, far):
     rows, whole = hidden.shape
-    blocks, _, width = near.shape
     tall = 16
-    spec = pltpu.PrefetchScalarGridSpec(
-        num_scalar_prefetch=2,
-        grid=(rows // tall,),
-        in_specs=[
-            pl.BlockSpec((tall, whole), lambda r, p, b: (r, 0)),
-            pl.BlockSpec((1, whole), lambda r, p, b: (0, 0)),
-            pl.BlockSpec((blocks, tall, width), lambda r, p, b: (0, r, 0)),
-            pl.BlockSpec((blocks, tall, width), lambda r, p, b: (0, r, 0)),
-        ],
-        out_specs=[
-            pl.BlockSpec((tall, whole), lambda r, p, b: (r, 0)),
-            pl.BlockSpec((tall, whole), lambda r, p, b: (r, 0)),
-        ],
-        scratch_shapes=[pltpu.VMEM((tall, whole), F32)],
-    )
     return pl.pallas_call(
         finish_kernel,
-        grid_spec=spec,
+        in_specs=[SMEM, SMEM] + [VMEM] * 4,
+        out_specs=[ANY, ANY],
         out_shape=[jax.ShapeDtypeStruct((rows, whole), BF16)] * 2,
+        scratch_shapes=[
+            pltpu.VMEM((tall, whole), F32),
+            pltpu.VMEM((2, 2, tall, whole), BF16),
+            pltpu.SemaphoreType.DMA((2, 2)),
+        ],
         compiler_params=params(14),
         cost_estimate=cost(8 * hidden.size, 14 * hidden.size),
         name="finish",
@@ -405,31 +443,31 @@
     lower_near = along_z(query_lower_factor.T)
     lower_far = hop(lower_near, 1)
 
-    flat = hidden_in.reshape(tall, width)
+    rank_part = query_upper_factor.shape[0]
+    sent = jnp.concatenate([query_upper_factor, output_lower_factor.T], axis=0)
+    came = swap(sent)
+
+    def in_order(a, b):
+        return jnp.where(f == 0, jnp.concatenate([a, b]), jnp.concatenate([b, a]))
+
+    upper = in_order(sent[:rank_part], came[:rank_part]) * BF16(ADAPTER_SCALE)
+    lower_o = in_order(sent[rank_part:], came[rank_part:]) * BF16(ADAPTER_SCALE)
+
+    message = with_largest_in_reach(cache_lengths, cache_values[:, 0], output_upper_factor)
+    bound = jnp.maximum(message[-16:], swap(message[-16:]))
+
+    hidden, message = lax.optimization_barrier((hidden_in, message))
+    flat = hidden.reshape(tall, width)
     inputs32 = flat.astype(F32)
     mean_square = jnp.mean(inputs32 * inputs32, axis=-1, keepdims=True)
     normed = (inputs32 * lax.rsqrt(mean_square + NORM_EPS) * input_gain.astype(F32)).astype(BF16)
     mine = lax.dynamic_slice_in_dim(normed, f * half, half, 1)
     theirs = swap(lax.dynamic_slice_in_dim(normed, (1 - f) * half, half, 1))
 
-    columns = query_upper_factor.shape[1]
-    bound = largest_in_reach(cache_lengths, cache_values[:, 0], columns)
-    rank_part = query_upper_factor.shape[0]
-    sent = jnp.concatenate([query_upper_factor, output_lower_factor.T, bound], axis=0)
-    came = swap(sent)
-
-    def in_order(a, b):
-        return jnp.where(f == 0, jnp.concatenate([a, b]), jnp.concatenate([b, a]))
-
-    upper = in_order(sent[:rank_part], came[:rank_part]) * BF16(ADAPTER_SCALE)
-    lower_o = in_order(sent[rank_part : 2 * rank_part], came[rank_part : 2 * rank_part])
-    lower_o = lower_o * BF16(ADAPTER_SCALE)
-    bound = jnp.maximum(sent[2 * rank_part :], came[2 * rank_part :])
-
-    rank, block = output_upper_factor.shape
-    message = jnp.concatenate([output_upper_factor, bound[:, :block]], axis=0)
+    message = jnp.concatenate([message[:-16], bound], axis=0)
+    message, lower_near = lax.optimization_barrier((message, lower_near))
     upper_o = along_z(along_y(message))
-    bound = jnp.max(upper_o[:, :, rank:]).astype(F32)
+    bound = jnp.max(upper_o[:, :, -16:]).astype(F32)
 
     weight_q, _ = lax.optimization_barrier((query_base_weight, lower_near))
     query_effective, own, other = query_project(

time: 101 us -> 99.8 us (0.988)
  transfers between devices with their start and end apart: 28 -> 29, of which waited for: 8 -> 8; matrix products, arithmetic and copies ran while one was open for 3% -> 3% of each run, Pallas kernels for 21% -> 21%
where the time goes in v4:
time: 99.8 us; the launch traced here: 99.6 us
  starting transfers between devices  35.9 us (36%)
  Pallas kernels  32.7 us (33%)
  waiting for transfers between devices  25.1 us (25%)
  other arithmetic  2.88 us (3%)
  between operations  1.96 us (2%)
  local copies, waits for them, and re-layouts  1.09 us (1%)
    ppermute x22, starting transfers between devices, hop(): return lax.ppermute(value, 'tp', [(i, i ^ distance) for i in range(total)])  34.3 us
    ppermute x22, waiting for transfers between devices, hop(): return lax.ppermute(value, 'tp', [(i, i ^ distance) for i in range(total)])  25.1 us
    pallas_call x1, Pallas kernels, output_project(): pl.pallas_call(output_kernel, in_specs=[SMEM, VMEM, VMEM, ANY, VMEM, VMEM...  8.69 us
    pallas_call x1, Pallas kernels, attend(): pl.pallas_call(functools.partial(attend_kernel, steps, scale), in_specs=[...  7.33 us
    pallas_call x1, Pallas kernels, query_project(): pl.pallas_call(query_kernel, in_specs=[SMEM] + [VMEM] * 6, out_specs=[ANY...  6.46 us
    pallas_call x1, Pallas kernels, with_largest_in_reach(): pl.pallas_call(reach_kernel, in_specs=[SMEM, ANY, ANY], out_specs=VMEM, o...  3.94 us
    pallas_call x1, Pallas kernels, fetch(): pl.pallas_call(fetch_kernel, in_specs=[ANY], out_specs=VMEM, out_shape=pl...  3.39 us
    pallas_call x1, Pallas kernels, finish(): pl.pallas_call(finish_kernel, in_specs=[SMEM, SMEM] + [VMEM] * 4, out_spe...  2.86 us
  transfers between devices with their start and end apart: 29, of which 8 were waited for; matrix products, arithmetic and copies ran while one was open for 3% of the time, Pallas kernels for 21%

profile of v4, /device:TPU:0, one launch (start us, length us, event | category | flops | bytes accessed | tf_op | source)
XLA Modules:
  0.0 99.6 jit_solution(1296082137488021706)
XLA Ops:
  0.6 4.1 %collective-permute-start.2 = (bf16[64,512]{1,0:T(8,128)(2,1)}, bf16[64,512]{1,0:T(8,128)(2,1)S(1)}, u32[]{:S(2)}, u32[]{:S(2)}) collective-permute-start(bf16[64,512]{1,0:T(8,128)(2,1)} %bitcast.86), channel_id=1, source_target_pairs={{0,4},{1,5},{2,6},{3,7},{4,0},{5,1},{6,2},{7,3},{8,12},{9,13},{10,... | collective-permute-start | bytes 196616 | tf_op jit(solution)/shard_map/ppermute | solution.py:31
  4.7 1.6 %collective-permute-start.1 = (bf16[64,512]{1,0:T(8,128)(2,1)}, bf16[64,512]{1,0:T(8,128)(2,1)S(1)}, u32[]{:S(2)}, u32[]{:S(2)}) collective-permute-start(bf16[64,512]{1,0:T(8,128)(2,1)} %bitcast.87), channel_id=1, source_target_pairs={{0,2},{1,3},{2,0},{3,1},{4,6},{5,7},{6,4},{7,5},{8,10},{9,11},{10,... | collective-permute-start | bytes 196616 | tf_op jit(solution)/shard_map/ppermute | solution.py:31
  6.3 0.7 copy-done.1
  7.0 3.9 %with_largest_in_reach.1 = bf16[272,128]{1,0:T(8,128)(2,1)S(1)} custom-call(s32[8]{0:T(128)S(1)} %copy-done.1, bf16[8,2048,128]{2,1,0:T(8,128)(2,1)} %bitcast.67, bf16[64,512]{1,0:T(8,128)(2,1)} %upper.1), custom_call_target="tpu_custom_call" | custom-call | flops 8388608 | bytes 4194304 | tf_op jit(solution)/shard_map/with_largest_in_reach/pallas_call | solution.py:98
  11.1 0.5 collective-permute-start.8
  13.1 1.8 %collective-permute-start.9 = (bf16[4,64,512]{2,1,0:T(8,128)(2,1)S(1)}, bf16[4,64,512]{2,1,0:T(8,128)(2,1)S(1)}, u32[]{:S(2)}, u32[]{:S(2)}) collective-permute-start(bf16[4,64,512]{2,1,0:T(8,128)(2,1)S(1)} %pad_maximum_fusion.2.near), channel_id=1, source_target_pairs={{0,1},{1,0},{2,3},{3,2},{4,5},{5,4},{6,7},{7,6},{8,9},{9,8},{10,11... | collective-permute-start | bytes 786440 | tf_op jit(solution)/shard_map/ppermute | solution.py:31
  15.1 3.4 %fetch_query.1.base = bf16[4096,1024]{1,0:T(8,128)(2,1)S(1)} custom-call(bf16[4096,1024]{1,0:T(8,128)(2,1)} %source), custom_call_target="tpu_custom_call" | custom-call | bytes 8388608 | tf_op jit(solution)/shard_map/fetch_query/pallas_call | solution.py:62
  18.6 3.6 %collective-permute-done.9.far = bf16[4,64,512]{2,1,0:T(8,128)(2,1)S(1)} collective-permute-done((bf16[4,64,512]{2,1,0:T(8,128)(2,1)S(1)}, bf16[4,64,512]{2,1,0:T(8,128)(2,1)S(1)}, u32[]{:S(2)}, u32[]{:S(2)}) %collective-permute-start.9) | collective-permute-done | bytes 262176 | tf_op jit(solution)/shard_map/ppermute | solution.py:31
  22.2 6.5 %query_project.1 = (bf16[4096,1024]{1,0:T(8,128)(2,1)}, f32[64,1024]{1,0:T(8,128)S(1)}, f32[64,1024]{1,0:T(8,128)S(1)}) custom-call(s32[1]{0:T(128)} %bitcast.place, bf16[4,64,512]{2,1,0:T(8,128)(2,1)S(1)} %pad_maximum_fusion.2.near, bf16[4,64,512]{2,1,0:T(8,128)(2,1)S(1)} %collective-permute-done.9.far, bf16[64,1024]{1,0:T(8,128)(2,1)S(1)} %fusion.3.upper, ...), custom_call_target="tpu_custom_call" | custom-call | flops 1610612736 | bytes 8388608 | tf_op jit(solution)/shard_map/query_project/pallas_call | solution.py:150
  28.9 2.0 %collective-permute-start.6 = (bf16[2,272,128]{2,1,0:T(8,128)(2,1)S(1)}, bf16[2,272,128]{2,1,0:T(8,128)(2,1)S(1)}, u32[]{:S(2)}, u32[]{:S(2)}) collective-permute-start(bf16[2,272,128]{2,1,0:T(8,128)(2,1)S(1)} %get-tuple-element.51), channel_id=1, source_target_pairs={{0,4},{1,5},{2,6},{3,7},{4,0},{5,1},{6,2},{7,3},{8,12},{9,13},{10,... | collective-permute-start | bytes 417800 | tf_op jit(solution)/shard_map/ppermute | solution.py:31
  30.9 2.5 %collective-permute-start.5 = (bf16[2,272,128]{2,1,0:T(8,128)(2,1)S(1)}, bf16[2,272,128]{2,1,0:T(8,128)(2,1)S(1)}, u32[]{:S(2)}, u32[]{:S(2)}) collective-permute-start(bf16[2,272,128]{2,1,0:T(8,128)(2,1)S(1)} %get-tuple-element.51), channel_id=1, source_target_pairs={{0,2},{1,3},{2,0},{3,1},{4,6},{5,7},{6,4},{7,5},{8,10},{9,11},{10,... | collective-permute-start | bytes 417800 | tf_op jit(solution)/shard_map/ppermute | solution.py:31
  33.5 7.3 %attend.1.mine = bf16[64,1024]{1,0:T(8,128)(2,1)S(1)} custom-call(s32[8]{0:T(128)S(1)} %copy-done.2, f32[64,1024]{1,0:T(8,128)S(1)} %get-tuple-element.26.own, f32[64,1024]{1,0:T(8,128)S(1)} %collective-permute-done.11.other, bf16[1,1024]{1,0:T(2,128)(2,1)S(1)} %broadcast_in_dim.8.bias, f32[64,128]{1,0:T(8,128)S(1)} %get-tuple-element.57.cosine, ...), custom_call_target="tpu_custom_call" | custom-call | flops 536870912 | bytes 8388608 | tf_op jit(solution)/shard_map/attend/pallas_call | solution.py:244
  40.9 2.4 %collective-permute-done.7 = bf16[2,272,128]{2,1,0:T(8,128)(2,1)S(1)} collective-permute-done((bf16[2,272,128]{2,1,0:T(8,128)(2,1)S(1)}, bf16[2,272,128]{2,1,0:T(8,128)(2,1)S(1)}, u32[]{:S(2)}, u32[]{:S(2)}) %collective-permute-start.7) | collective-permute-done | bytes 139296 | tf_op jit(solution)/shard_map/ppermute | solution.py:31
  43.4 0.6 slice_reduce_fusion
  44.7 8.7 %output_project.1 = (bf16[1024,4096]{1,0:T(8,128)(2,1)}, f32[2,4,64,512]{3,2,1,0:T(8,128)S(1)}, f32[4,2,64,512]{3,2,1,0:T(8,128)S(1)}) custom-call(s32[1]{0:T(128)} %bitcast.place, bf16[64,1024]{1,0:T(8,128)(2,1)S(1)} %fusion.5.lower, bf16[4,2,272,128]{3,2,1,0:T(8,128)(2,1)S(1)} %pad_maximum_fusion.upper, bf16[1024,4096]{1,0:T(8,128)(2,1)} %base.1, ...), custom_call_target="tpu_custom_call" | custom-call | flops 1610612736 | bytes 16777216 | tf_op jit(solution)/shard_map/output_project/pallas_call | solution.py:310
  53.5 1.6 %collective-permute-start.13 = (f16[4,64,512]{2,1,0:T(8,128)(2,1)S(1)}, f16[4,64,512]{2,1,0:T(8,128)(2,1)S(1)}, u32[]{:S(2)}, u32[]{:S(2)}) collective-permute-start(f16[4,64,512]{2,1,0:T(8,128)(2,1)S(1)} %fusion), channel_id=1, source_target_pairs={{0,1},{1,0},{2,3},{3,2},{4,5},{5,4},{6,7},{7,6},{8,9},{9,8},{10,11... | collective-permute-start | bytes 786440 | tf_op jit(solution)/shard_map/ppermute | solution.py:31
  55.2 1.7 %collective-permute-start.16 = (f16[2,64,512]{2,1,0:T(8,128)(2,1)S(1)}, f16[2,64,512]{2,1,0:T(8,128)(2,1)S(1)}, u32[]{:S(2)}, u32[]{:S(2)}) collective-permute-start(f16[2,64,512]{2,1,0:T(8,128)(2,1)S(1)} %get-tuple-element.40), channel_id=1, source_target_pairs={{0,6},{1,7},{2,4},{3,5},{4,2},{5,3},{6,0},{7,1},{8,14},{9,15},{10,... | collective-permute-start | bytes 393224 | tf_op jit(solution)/shard_map/ppermute | solution.py:31
  56.9 2.3 %collective-permute-start.15 = (f16[2,64,512]{2,1,0:T(8,128)(2,1)S(1)}, f16[2,64,512]{2,1,0:T(8,128)(2,1)S(1)}, u32[]{:S(2)}, u32[]{:S(2)}) collective-permute-start(f16[2,64,512]{2,1,0:T(8,128)(2,1)S(1)} %get-tuple-element.41), channel_id=1, source_target_pairs={{0,4},{1,5},{2,6},{3,7},{4,0},{5,1},{6,2},{7,3},{8,12},{9,13},{10,... | collective-permute-start | bytes 393224 | tf_op jit(solution)/shard_map/ppermute | solution.py:31
  59.6 2.0 %collective-permute-done.13 = f16[4,64,512]{2,1,0:T(8,128)(2,1)S(1)} collective-permute-done((f16[4,64,512]{2,1,0:T(8,128)(2,1)S(1)}, f16[4,64,512]{2,1,0:T(8,128)(2,1)S(1)}, u32[]{:S(2)}, u32[]{:S(2)}) %collective-permute-start.13) | collective-permute-done | bytes 262176 | tf_op jit(solution)/shard_map/ppermute | solution.py:31
  61.8 2.2 %collective-permute-start.17 = (f16[64,512]{1,0:T(8,128)(2,1)S(1)}, f16[64,512]{1,0:T(8,128)(2,1)S(1)}, u32[]{:S(2)}, u32[]{:S(2)}) collective-permute-start(f16[64,512]{1,0:T(8,128)(2,1)S(1)} %get-tuple-element.47), channel_id=1, source_target_pairs={{0,2},{1,3},{2,0},{3,1},{4,6},{5,7},{6,4},{7,5},{8,10},{9,11},{10,... | collective-permute-start | bytes 196616 | tf_op jit(solution)/shard_map/ppermute | solution.py:31
  63.9 3.2 %collective-permute-start.19 = (f16[64,512]{1,0:T(8,128)(2,1)S(1)}, f16[64,512]{1,0:T(8,128)(2,1)S(1)}, u32[]{:S(2)}, u32[]{:S(2)}) collective-permute-start(f16[64,512]{1,0:T(8,128)(2,1)S(1)} %get-tuple-element.48), channel_id=1, source_target_pairs={{0,6},{1,7},{2,4},{3,5},{4,2},{5,3},{6,0},{7,1},{8,14},{9,15},{10,... | collective-permute-start | bytes 196616 | tf_op jit(solution)/shard_map/ppermute | solution.py:31
  67.1 1.8 %collective-permute-start.18 = (f16[64,512]{1,0:T(8,128)(2,1)S(1)}, f16[64,512]{1,0:T(8,128)(2,1)S(1)}, u32[]{:S(2)}, u32[]{:S(2)}) collective-permute-start(f16[64,512]{1,0:T(8,128)(2,1)S(1)} %get-tuple-element.49), channel_id=1, source_target_pairs={{0,4},{1,5},{2,6},{3,7},{4,0},{5,1},{6,2},{7,3},{8,12},{9,13},{10,... | collective-permute-start | bytes 196616 | tf_op jit(solution)/shard_map/ppermute | solution.py:31
  68.9 4.4 %collective-permute-done.15 = f16[2,64,512]{2,1,0:T(8,128)(2,1)S(1)} collective-permute-done((f16[2,64,512]{2,1,0:T(8,128)(2,1)S(1)}, f16[2,64,512]{2,1,0:T(8,128)(2,1)S(1)}, u32[]{:S(2)}, u32[]{:S(2)}) %collective-permute-start.15) | collective-permute-done | bytes 131104 | tf_op jit(solution)/shard_map/ppermute | solution.py:31
  73.5 0.6 collective-permute-start.24
  74.1 1.9 %collective-permute-done.18 = f16[64,512]{1,0:T(8,128)(2,1)S(1)} collective-permute-done((f16[64,512]{1,0:T(8,128)(2,1)S(1)}, f16[64,512]{1,0:T(8,128)(2,1)S(1)}, u32[]{:S(2)}, u32[]{:S(2)}) %collective-permute-start.18) | collective-permute-done | bytes 65568 | tf_op jit(solution)/shard_map/ppermute | solution.py:31
  76.1 2.1 %collective-permute-start.22 = (f16[64,512]{1,0:T(8,128)(2,1)S(1)}, f16[64,512]{1,0:T(8,128)(2,1)S(1)}, u32[]{:S(2)}, u32[]{:S(2)}) collective-permute-start(f16[64,512]{1,0:T(8,128)(2,1)S(1)} %fusion.10), channel_id=1, source_target_pairs={{0,6},{1,7},{2,4},{3,5},{4,2},{5,3},{6,0},{7,1},{8,14},{9,15},{10,... | collective-permute-start | bytes 196616 | tf_op jit(solution)/shard_map/ppermute | solution.py:31
  78.2 2.3 %collective-permute-start.20 = (f16[64,512]{1,0:T(8,128)(2,1)S(1)}, f16[64,512]{1,0:T(8,128)(2,1)S(1)}, u32[]{:S(2)}, u32[]{:S(2)}) collective-permute-start(f16[64,512]{1,0:T(8,128)(2,1)S(1)} %fusion.10), channel_id=1, source_target_pairs={{0,2},{1,3},{2,0},{3,1},{4,6},{5,7},{6,4},{7,5},{8,10},{9,11},{10,... | collective-permute-start | bytes 196616 | tf_op jit(solution)/shard_map/ppermute | solution.py:31
  80.6 2.1 %collective-permute-start.28 = (f16[2,64,512]{2,1,0:T(8,128)(2,1)S(1)}, f16[2,64,512]{2,1,0:T(8,128)(2,1)S(1)}, u32[]{:S(2)}, u32[]{:S(2)}) collective-permute-start(f16[2,64,512]{2,1,0:T(8,128)(2,1)S(1)} %add_convert_fusion), channel_id=1, source_target_pairs={{0,6},{1,7},{2,4},{3,5},{4,2},{5,3},{6,0},{7,1},{8,14},{9,15},{10,... | collective-permute-start | bytes 393224 | tf_op jit(solution)/shard_map/ppermute | solution.py:31
  82.8 2.3 %collective-permute-start.26 = (f16[2,64,512]{2,1,0:T(8,128)(2,1)S(1)}, f16[2,64,512]{2,1,0:T(8,128)(2,1)S(1)}, u32[]{:S(2)}, u32[]{:S(2)}) collective-permute-start(f16[2,64,512]{2,1,0:T(8,128)(2,1)S(1)} %add_convert_fusion), channel_id=1, source_target_pairs={{0,2},{1,3},{2,0},{3,1},{4,6},{5,7},{6,4},{7,5},{8,10},{9,11},{10,... | collective-permute-start | bytes 393224 | tf_op jit(solution)/shard_map/ppermute | solution.py:31
  85.2 4.1 %collective-permute-done.21 = f16[64,512]{1,0:T(8,128)(2,1)S(1)} collective-permute-done((f16[64,512]{1,0:T(8,128)(2,1)S(1)}, f16[64,512]{1,0:T(8,128)(2,1)S(1)}, u32[]{:S(2)}, u32[]{:S(2)}) %collective-permute-start.21) | collective-permute-done | bytes 65568 | tf_op jit(solution)/shard_map/ppermute | solution.py:31
  89.4 6.6 %collective-permute-done.27 = f16[2,64,512]{2,1,0:T(8,128)(2,1)S(1)} collective-permute-done((f16[2,64,512]{2,1,0:T(8,128)(2,1)S(1)}, f16[2,64,512]{2,1,0:T(8,128)(2,1)S(1)}, u32[]{:S(2)}, u32[]{:S(2)}) %collective-permute-start.27) | collective-permute-done | bytes 131104 | tf_op jit(solution)/shard_map/ppermute | solution.py:31
  96.6 2.9 %finish.1 = (bf16[64,8192]{1,0:T(8,128)(2,1)}, bf16[64,8192]{1,0:T(8,128)(2,1)}) custom-call(s32[2]{0:T(128)S(1)} %pad_add_fusion.place, f32[1]{0:T(128)} %bitcast.14.bound, bf16[64,8192]{1,0:T(8,128)(2,1)S(1)} %bitcast.65, bf16[1,8192]{1,0:T(2,128)(2,1)S(1)} %broadcast_in_dim.7.gain, f32[8,64,512]{2,1,0:T(8,128)S(1)} %bitcast.66, ...), custom_call_target="tpu_custom_call" | custom-call | flops 4194304 | bytes 7340032 | tf_op jit(solution)/shard_map/finish/pallas_call | solution.py:370
  (90 shorter events, 4.0 us)
Async XLA Ops:
  0.6 11.2 %copy-start = (bf16[8,8,8192]{2,1,0:T(8,128)(2,1)S(1)}, bf16[8,8,8192]{2,1,0:T(8,128)(2,1)}, u32[]{:S(2)}) copy-start(bf16[8,8,8192]{2,1,0:T(8,128)(2,1)} %param.14) | copy-start | bytes 3145732
  0.6 12.3 %collective-permute-start.2 = (bf16[64,512]{1,0:T(8,128)(2,1)}, bf16[64,512]{1,0:T(8,128)(2,1)S(1)}, u32[]{:S(2)}, u32[]{:S(2)}) collective-permute-start(bf16[64,512]{1,0:T(8,128)(2,1)} %bitcast.86), channel_id=1, source_target_pairs={{0,4},{1,5},{2,6},{3,7},{4,0},{5,1},{6,2},{7,3},{8,12},{9,13},{10,... | collective-permute-start | bytes 196616 | tf_op jit(solution)/shard_map/ppermute | solution.py:31
  4.7 8.2 %collective-permute-start.1 = (bf16[64,512]{1,0:T(8,128)(2,1)}, bf16[64,512]{1,0:T(8,128)(2,1)S(1)}, u32[]{:S(2)}, u32[]{:S(2)}) collective-permute-start(bf16[64,512]{1,0:T(8,128)(2,1)} %bitcast.87), channel_id=1, source_target_pairs={{0,2},{1,3},{2,0},{3,1},{4,6},{5,7},{6,4},{7,5},{8,10},{9,11},{10,... | collective-permute-start | bytes 196616 | tf_op jit(solution)/shard_map/ppermute | solution.py:31
  6.3 6.7 %collective-permute-start.3 = (bf16[64,512]{1,0:T(8,128)(2,1)}, bf16[64,512]{1,0:T(8,128)(2,1)S(1)}, u32[]{:S(2)}, u32[]{:S(2)}) collective-permute-start(bf16[64,512]{1,0:T(8,128)(2,1)} %bitcast.88), channel_id=1, source_target_pairs={{0,6},{1,7},{2,4},{3,5},{4,2},{5,3},{6,0},{7,1},{8,14},{9,15},{10,... | collective-permute-start | bytes 196616 | tf_op jit(solution)/shard_map/ppermute | solution.py:31
  11.0 1.9 %collective-permute-start = (bf16[16,128]{1,0:T(8,128)(2,1)S(1)}, bf16[16,128]{1,0:T(8,128)(2,1)S(1)}, u32[]{:S(2)}, u32[]{:S(2)}) collective-permute-start(bf16[16,128]{1,0:T(8,128)(2,1)S(1)} %slice.64), channel_id=1, source_target_pairs={{0,8},{8,0},{1,9},{9,1},{2,10},{10,2},{3,11},{11,3},{4,12},{12,4},... | collective-permute-start | bytes 12296 | tf_op jit(solution)/shard_map/ppermute | solution.py:35
  11.1 7.5 %collective-permute-start.8 = (bf16[64,1024]{1,0:T(8,128)(2,1)S(1)}, bf16[64,1024]{1,0:T(8,128)(2,1)S(1)}, u32[]{:S(2)}, u32[]{:S(2)}) collective-permute-start(bf16[64,1024]{1,0:T(8,128)(2,1)S(1)} %pad_maximum_fusion.5), channel_id=1, source_target_pairs={{0,8},{8,0},{1,9},{9,1},{2,10},{10,2},{3,11},{11,3},{4,12},{12,4},... | collective-permute-start | bytes 393224 | tf_op jit(solution)/shard_map/ppermute | solution.py:35
  12.9 9.4 %collective-permute-start.10 = (bf16[64,4096]{1,0:T(8,128)(2,1)S(1)}, bf16[64,4096]{1,0:T(8,128)(2,1)S(1)}, u32[]{:S(2)}, u32[]{:S(2)}) collective-permute-start(bf16[64,4096]{1,0:T(8,128)(2,1)S(1)} %get-tuple-element.43), channel_id=1, source_target_pairs={{0,8},{8,0},{1,9},{9,1},{2,10},{10,2},{3,11},{11,3},{4,12},{12,4},... | collective-permute-start | bytes 1572872 | tf_op jit(solution)/shard_map/ppermute | solution.py:35
  13.1 9.2 %collective-permute-start.9 = (bf16[4,64,512]{2,1,0:T(8,128)(2,1)S(1)}, bf16[4,64,512]{2,1,0:T(8,128)(2,1)S(1)}, u32[]{:S(2)}, u32[]{:S(2)}) collective-permute-start(bf16[4,64,512]{2,1,0:T(8,128)(2,1)S(1)} %pad_maximum_fusion.2.near), channel_id=1, source_target_pairs={{0,1},{1,0},{2,3},{3,2},{4,5},{5,4},{6,7},{7,6},{8,9},{9,8},{10,11... | collective-permute-start | bytes 786440 | tf_op jit(solution)/shard_map/ppermute | solution.py:31
  14.9 14.0 %collective-permute-start.4 = (bf16[272,128]{1,0:T(8,128)(2,1)S(1)}, bf16[272,128]{1,0:T(8,128)(2,1)S(1)}, u32[]{:S(2)}, u32[]{:S(2)}) collective-permute-start(bf16[272,128]{1,0:T(8,128)(2,1)S(1)} %pad_maximum_fusion.8), channel_id=1, source_target_pairs={{0,1},{1,0},{2,3},{3,2},{4,5},{5,4},{6,7},{7,6},{8,9},{9,8},{10,11... | collective-permute-start | bytes 208904 | tf_op jit(solution)/shard_map/ppermute | solution.py:31
  22.2 11.2 %copy-start.2 = (s32[8]{0:T(128)S(1)}, s32[8]{0:T(128)}, u32[]{:S(2)}) copy-start(s32[8]{0:T(128)} %lengths.3) | copy-start | bytes 100
  28.7 4.7 %collective-permute-start.11 = (f32[64,1024]{1,0:T(8,128)S(1)}, f32[64,1024]{1,0:T(8,128)S(1)}, u32[]{:S(2)}, u32[]{:S(2)}) collective-permute-start(f32[64,1024]{1,0:T(8,128)S(1)} %get-tuple-element.27), channel_id=1, source_target_pairs={{0,8},{8,0},{1,9},{9,1},{2,10},{10,2},{3,11},{11,3},{4,12},{12,4},... | collective-permute-start | bytes 786440 | tf_op jit(solution)/shard_map/ppermute | solution.py:35
  28.9 11.9 %collective-permute-start.6 = (bf16[2,272,128]{2,1,0:T(8,128)(2,1)S(1)}, bf16[2,272,128]{2,1,0:T(8,128)(2,1)S(1)}, u32[]{:S(2)}, u32[]{:S(2)}) collective-permute-start(bf16[2,272,128]{2,1,0:T(8,128)(2,1)S(1)} %get-tuple-element.51), channel_id=1, source_target_pairs={{0,4},{1,5},{2,6},{3,7},{4,0},{5,1},{6,2},{7,3},{8,12},{9,13},{10,... | collective-permute-start | bytes 417800 | tf_op jit(solution)/shard_map/ppermute | solution.py:31
  30.9 10.0 %collective-permute-start.5 = (bf16[2,272,128]{2,1,0:T(8,128)(2,1)S(1)}, bf16[2,272,128]{2,1,0:T(8,128)(2,1)S(1)}, u32[]{:S(2)}, u32[]{:S(2)}) collective-permute-start(bf16[2,272,128]{2,1,0:T(8,128)(2,1)S(1)} %get-tuple-element.51), channel_id=1, source_target_pairs={{0,2},{1,3},{2,0},{3,1},{4,6},{5,7},{6,4},{7,5},{8,10},{9,11},{10,... | collective-permute-start | bytes 417800 | tf_op jit(solution)/shard_map/ppermute | solution.py:31
  33.4 9.9 %collective-permute-start.7 = (bf16[2,272,128]{2,1,0:T(8,128)(2,1)S(1)}, bf16[2,272,128]{2,1,0:T(8,128)(2,1)S(1)}, u32[]{:S(2)}, u32[]{:S(2)}) collective-permute-start(bf16[2,272,128]{2,1,0:T(8,128)(2,1)S(1)} %get-tuple-element.51), channel_id=1, source_target_pairs={{0,6},{1,7},{2,4},{3,5},{4,2},{5,3},{6,0},{7,1},{8,14},{9,15},{10,... | collective-permute-start | bytes 417800 | tf_op jit(solution)/shard_map/ppermute | solution.py:31
  40.8 3.9 %collective-permute-start.12 = (bf16[64,1024]{1,0:T(8,128)(2,1)S(1)}, bf16[64,1024]{1,0:T(8,128)(2,1)S(1)}, u32[]{:S(2)}, u32[]{:S(2)}) collective-permute-start(bf16[64,1024]{1,0:T(8,128)(2,1)S(1)} %attend.1.mine), channel_id=1, source_target_pairs={{0,8},{8,0},{1,9},{9,1},{2,10},{10,2},{3,11},{11,3},{4,12},{12,4},... | collective-permute-start | bytes 393224 | tf_op jit(solution)/shard_map/ppermute | solution.py:35
  53.4 31.8 %copy-start.7 = (bf16[8192]{0:T(1024)(128)(2,1)S(1)}, bf16[8192]{0:T(1024)(128)(2,1)}, u32[]{:S(2)}) copy-start(bf16[8192]{0:T(1024)(128)(2,1)} %param.16) | copy-start | bytes 49156
  53.5 8.1 %collective-permute-start.13 = (f16[4,64,512]{2,1,0:T(8,128)(2,1)S(1)}, f16[4,64,512]{2,1,0:T(8,128)(2,1)S(1)}, u32[]{:S(2)}, u32[]{:S(2)}) collective-permute-start(f16[4,64,512]{2,1,0:T(8,128)(2,1)S(1)} %fusion), channel_id=1, source_target_pairs={{0,1},{1,0},{2,3},{3,2},{4,5},{5,4},{6,7},{7,6},{8,9},{9,8},{10,11... | collective-permute-start | bytes 786440 | tf_op jit(solution)/shard_map/ppermute | solution.py:31
  55.2 11.9 %collective-permute-start.16 = (f16[2,64,512]{2,1,0:T(8,128)(2,1)S(1)}, f16[2,64,512]{2,1,0:T(8,128)(2,1)S(1)}, u32[]{:S(2)}, u32[]{:S(2)}) collective-permute-start(f16[2,64,512]{2,1,0:T(8,128)(2,1)S(1)} %get-tuple-element.40), channel_id=1, source_target_pairs={{0,6},{1,7},{2,4},{3,5},{4,2},{5,3},{6,0},{7,1},{8,14},{9,15},{10,... | collective-permute-start | bytes 393224 | tf_op jit(solution)/shard_map/ppermute | solution.py:31
  56.9 16.4 %collective-permute-start.15 = (f16[2,64,512]{2,1,0:T(8,128)(2,1)S(1)}, f16[2,64,512]{2,1,0:T(8,128)(2,1)S(1)}, u32[]{:S(2)}, u32[]{:S(2)}) collective-permute-start(f16[2,64,512]{2,1,0:T(8,128)(2,1)S(1)} %get-tuple-element.41), channel_id=1, source_target_pairs={{0,4},{1,5},{2,6},{3,7},{4,0},{5,1},{6,2},{7,3},{8,12},{9,13},{10,... | collective-permute-start | bytes 393224 | tf_op jit(solution)/shard_map/ppermute | solution.py:31
  59.2 14.2 %collective-permute-start.14 = (f16[2,64,512]{2,1,0:T(8,128)(2,1)S(1)}, f16[2,64,512]{2,1,0:T(8,128)(2,1)S(1)}, u32[]{:S(2)}, u32[]{:S(2)}) collective-permute-start(f16[2,64,512]{2,1,0:T(8,128)(2,1)S(1)} %get-tuple-element.42), channel_id=1, source_target_pairs={{0,2},{1,3},{2,0},{3,1},{4,6},{5,7},{6,4},{7,5},{8,10},{9,11},{10,... | collective-permute-start | bytes 393224 | tf_op jit(solution)/shard_map/ppermute | solution.py:31
  61.8 11.6 %collective-permute-start.17 = (f16[64,512]{1,0:T(8,128)(2,1)S(1)}, f16[64,512]{1,0:T(8,128)(2,1)S(1)}, u32[]{:S(2)}, u32[]{:S(2)}) collective-permute-start(f16[64,512]{1,0:T(8,128)(2,1)S(1)} %get-tuple-element.47), channel_id=1, source_target_pairs={{0,2},{1,3},{2,0},{3,1},{4,6},{5,7},{6,4},{7,5},{8,10},{9,11},{10,... | collective-permute-start | bytes 196616 | tf_op jit(solution)/shard_map/ppermute | solution.py:31
  63.9 10.2 %collective-permute-start.19 = (f16[64,512]{1,0:T(8,128)(2,1)S(1)}, f16[64,512]{1,0:T(8,128)(2,1)S(1)}, u32[]{:S(2)}, u32[]{:S(2)}) collective-permute-start(f16[64,512]{1,0:T(8,128)(2,1)S(1)} %get-tuple-element.48), channel_id=1, source_target_pairs={{0,6},{1,7},{2,4},{3,5},{4,2},{5,3},{6,0},{7,1},{8,14},{9,15},{10,... | collective-permute-start | bytes 196616 | tf_op jit(solution)/shard_map/ppermute | solution.py:31
  67.1 8.9 %collective-permute-start.18 = (f16[64,512]{1,0:T(8,128)(2,1)S(1)}, f16[64,512]{1,0:T(8,128)(2,1)S(1)}, u32[]{:S(2)}, u32[]{:S(2)}) collective-permute-start(f16[64,512]{1,0:T(8,128)(2,1)S(1)} %get-tuple-element.49), channel_id=1, source_target_pairs={{0,4},{1,5},{2,6},{3,7},{4,0},{5,1},{6,2},{7,3},{8,12},{9,13},{10,... | collective-permute-start | bytes 196616 | tf_op jit(solution)/shard_map/ppermute | solution.py:31
  73.4 7.1 %collective-permute-start.25 = (f16[2,64,512]{2,1,0:T(8,128)(2,1)S(1)}, f16[2,64,512]{2,1,0:T(8,128)(2,1)S(1)}, u32[]{:S(2)}, u32[]{:S(2)}) collective-permute-start(f16[2,64,512]{2,1,0:T(8,128)(2,1)S(1)} %fusion.1), channel_id=1, source_target_pairs={{0,9},{1,8},{2,11},{3,10},{4,13},{5,12},{6,15},{7,14},{8,1},{9,0},... | collective-permute-start | bytes 393224 | tf_op jit(solution)/shard_map/ppermute | solution.py:389
  73.5 7.0 %collective-permute-start.24 = (f16[2,64,512]{2,1,0:T(8,128)(2,1)S(1)}, f16[2,64,512]{2,1,0:T(8,128)(2,1)S(1)}, u32[]{:S(2)}, u32[]{:S(2)}) collective-permute-start(f16[2,64,512]{2,1,0:T(8,128)(2,1)S(1)} %fusion.1), channel_id=1, source_target_pairs={{0,8},{8,0},{1,9},{9,1},{2,10},{10,2},{3,11},{11,3},{4,12},{12,4},... | collective-permute-start | bytes 393224 | tf_op jit(solution)/shard_map/ppermute | solution.py:35
  76.1 6.7 %collective-permute-start.22 = (f16[64,512]{1,0:T(8,128)(2,1)S(1)}, f16[64,512]{1,0:T(8,128)(2,1)S(1)}, u32[]{:S(2)}, u32[]{:S(2)}) collective-permute-start(f16[64,512]{1,0:T(8,128)(2,1)S(1)} %fusion.10), channel_id=1, source_target_pairs={{0,6},{1,7},{2,4},{3,5},{4,2},{5,3},{6,0},{7,1},{8,14},{9,15},{10,... | collective-permute-start | bytes 196616 | tf_op jit(solution)/shard_map/ppermute | solution.py:31
  78.2 11.0 %collective-permute-start.21 = (f16[64,512]{1,0:T(8,128)(2,1)S(1)}, f16[64,512]{1,0:T(8,128)(2,1)S(1)}, u32[]{:S(2)}, u32[]{:S(2)}) collective-permute-start(f16[64,512]{1,0:T(8,128)(2,1)S(1)} %fusion.10), channel_id=1, source_target_pairs={{0,4},{1,5},{2,6},{3,7},{4,0},{5,1},{6,2},{7,3},{8,12},{9,13},{10,... | collective-permute-start | bytes 196616 | tf_op jit(solution)/shard_map/ppermute | solution.py:31
  78.2 11.0 %collective-permute-start.20 = (f16[64,512]{1,0:T(8,128)(2,1)S(1)}, f16[64,512]{1,0:T(8,128)(2,1)S(1)}, u32[]{:S(2)}, u32[]{:S(2)}) collective-permute-start(f16[64,512]{1,0:T(8,128)(2,1)S(1)} %fusion.10), channel_id=1, source_target_pairs={{0,2},{1,3},{2,0},{3,1},{4,6},{5,7},{6,4},{7,5},{8,10},{9,11},{10,... | collective-permute-start | bytes 196616 | tf_op jit(solution)/shard_map/ppermute | solution.py:31
  80.6 8.8 %collective-permute-start.28 = (f16[2,64,512]{2,1,0:T(8,128)(2,1)S(1)}, f16[2,64,512]{2,1,0:T(8,128)(2,1)S(1)}, u32[]{:S(2)}, u32[]{:S(2)}) collective-permute-start(f16[2,64,512]{2,1,0:T(8,128)(2,1)S(1)} %add_convert_fusion), channel_id=1, source_target_pairs={{0,6},{1,7},{2,4},{3,5},{4,2},{5,3},{6,0},{7,1},{8,14},{9,15},{10,... | collective-permute-start | bytes 393224 | tf_op jit(solution)/shard_map/ppermute | solution.py:31
  82.7 13.3 %collective-permute-start.27 = (f16[2,64,512]{2,1,0:T(8,128)(2,1)S(1)}, f16[2,64,512]{2,1,0:T(8,128)(2,1)S(1)}, u32[]{:S(2)}, u32[]{:S(2)}) collective-permute-start(f16[2,64,512]{2,1,0:T(8,128)(2,1)S(1)} %add_convert_fusion), channel_id=1, source_target_pairs={{0,4},{1,5},{2,6},{3,7},{4,0},{5,1},{6,2},{7,3},{8,12},{9,13},{10,... | collective-permute-start | bytes 393224 | tf_op jit(solution)/shard_map/ppermute | solution.py:31
  82.8 13.2 %collective-permute-start.26 = (f16[2,64,512]{2,1,0:T(8,128)(2,1)S(1)}, f16[2,64,512]{2,1,0:T(8,128)(2,1)S(1)}, u32[]{:S(2)}, u32[]{:S(2)}) collective-permute-start(f16[2,64,512]{2,1,0:T(8,128)(2,1)S(1)} %add_convert_fusion), channel_id=1, source_target_pairs={{0,2},{1,3},{2,0},{3,1},{4,6},{5,7},{6,4},{7,5},{8,10},{9,11},{10,... | collective-permute-start | bytes 393224 | tf_op jit(solution)/shard_map/ppermute | solution.py:31
  89.4 7.0 %collective-permute-start.23 = (f16[4,64,512]{2,1,0:T(8,128)(2,1)S(1)}, f16[4,64,512]{2,1,0:T(8,128)(2,1)S(1)}, u32[]{:S(2)}, u32[]{:S(2)}) collective-permute-start(f16[4,64,512]{2,1,0:T(8,128)(2,1)S(1)} %get-tuple-element.46), channel_id=1, source_target_pairs={{0,1},{1,0},{2,3},{3,2},{4,5},{5,4},{6,7},{7,6},{8,9},{9,8},{10,11... | collective-permute-start | bytes 786440 | tf_op jit(solution)/shard_map/ppermute | solution.py:31
  (7 other events, 31.9 us)

commit v5 on v4

--- a/solution.py
+++ b/solution.py
@@ -81,16 +81,28 @@
     columns.start()
     for copy in copies:
         copy.start()
-    slot = lax.broadcasted_iota(jnp.int32, (slots, head_dim), 0)
-    top = jnp.zeros((8, head_dim), F32)
+    part = 256
+    slot = lax.broadcasted_iota(jnp.int32, (part, head_dim), 0)
+    top = jnp.zeros((16, head_dim), BF16)
+    edge = jnp.zeros((8, head_dim), F32)
     for row in range(rows):
         copies[row].wait()
-        size = jnp.where(slot < lengths[row], jnp.abs(held[row].astype(F32)), 0.0)
-        top = jnp.maximum(top, jnp.max(size.reshape(-1, 8, head_dim), axis=0))
+        whole = lengths[row] // part
+
+        def full(n, top, row=row):
+            size = jnp.abs(held[row, pl.ds(pl.multiple_of(n * part, part), part)])
+            return jnp.maximum(top, jnp.max(size.reshape(-1, 16, head_dim), axis=0))
+
+        top = lax.fori_loop(0, whole, full, top)
+        last = pl.multiple_of(jnp.minimum(whole, slots // part - 1) * part, part)
+        size = jnp.abs(held[row, pl.ds(last, part)].astype(F32))
+        size = jnp.where(slot < lengths[row] - last, size, 0.0)
+        edge = jnp.maximum(edge, jnp.max(size.reshape(-1, 8, head_dim), axis=0))
+    most = jnp.maximum(jnp.max(top.astype(F32)), jnp.max(edge))
     columns.wait()
     for first in range(0, width, 128):
         message[first // 128 * rank : (first // 128 + 1) * rank] = factor[:, first : first + 128]
-    message[width // 128 * rank :] = jnp.broadcast_to(jnp.max(top), (16, 128)).astype(BF16)
+    message[width // 128 * rank :] = jnp.broadcast_to(most, (16, 128)).astype(BF16)
 
 
 def with_largest_in_reach(lengths, values, upper):
@@ -112,44 +124,50 @@
     )(lengths, in_hbm(values), in_hbm(upper))
 
 
-def query_kernel(
-    place, near, far, upper, base, mine, theirs, effective, own, other, fresh, total, left
-):
-    outer, _, depth = near.shape
+def query_kernel(y, place, lower, upper, base, mine, theirs, *refs):
+    before, (effective, own, other, fresh, total, left) = refs[: 3 * y], refs[3 * y :]
+    outer, _, depth = lower.shape
     rows = mine.shape[0]
-    total[...] = jnp.zeros_like(total)
-
-    def pair(z, _):
-        for y, lower in ((0, near), (1, far)):
+    if y:
+        total[:rows] = before[1][...]
+        total[rows:] = before[2][...]
+    else:
+        total[...] = jnp.zeros_like(total)
+
+    def pair(half, _):
+        for slot in range(2):
+            z = 2 * half + slot
             start = pl.multiple_of(((2 * z + y) ^ place[0]) * depth, depth)
             block = pl.ds(start, depth)
-            out = pltpu.make_async_copy(fresh.at[y], effective.at[block], left.at[y])
-
-            @pl.when(z > 0)
+            out = pltpu.make_async_copy(fresh.at[slot], effective.at[block], left.at[slot])
+
+            @pl.when(half > 0)
             def _():
                 out.wait()
 
             update = contract_first(lower[z], upper[...])
-            fresh[y] = (base[block, :].astype(F32) + update).astype(BF16)
+            fresh[slot] = (base[block, :].astype(F32) + update).astype(BF16)
             out.start()
             both = jnp.concatenate([mine[:, block], theirs[:, block]], axis=0)
-            total[...] += jnp.dot(both, fresh[y], preferred_element_type=F32)
+            total[...] += jnp.dot(both, fresh[slot], preferred_element_type=F32)
         return 0
 
-    lax.fori_loop(0, outer, pair, 0)
+    lax.fori_loop(0, outer // 2, pair, 0)
     own[...] = total[:rows]
     other[...] = total[rows:]
-    for y in range(2):
-        pltpu.make_async_copy(fresh.at[y], effective.at[pl.ds(0, depth)], left.at[y]).wait()
-
-
-def query_project(place, near, far, upper, base, mine, theirs):
-    depth = near.shape[2]
+    for slot in range(2):
+        pltpu.make_async_copy(
+            fresh.at[slot], effective.at[pl.ds(0, depth)], left.at[slot]
+        ).wait()
+
+
+def query_project(y, place, lower, upper, base, mine, theirs, before=()):
+    depth = lower.shape[2]
     width = base.shape[1]
     rows = mine.shape[0]
     return pl.pallas_call(
-        query_kernel,
-        in_specs=[SMEM] + [VMEM] * 6,
+        functools.partial(query_kernel, y),
+        in_specs=[SMEM] + [VMEM] * 5 + [ANY, VMEM, VMEM][: len(before)],
         out_specs=[ANY, VMEM, VMEM],
         out_shape=[
             jax.ShapeDtypeStruct(base.shape, BF16),
@@ -161,10 +179,11 @@
             pltpu.VMEM((2 * rows, width), F32),
             pltpu.SemaphoreType.DMA((2,)),
         ],
+        input_output_aliases={6: 0} if before else {},
         compiler_params=params(14),
-        cost_estimate=cost(2 * base.size * (near.shape[1] + 2 * rows), 2 * base.size),
+        cost_estimate=cost(base.size * (lower.shape[1] + 2 * rows), base.size),
         name="query_project",
-    )(place, near, far, upper, in_vmem(base), mine, theirs)
+    )(place, lower, upper, in_vmem(base), mine, theirs, *before)
 
 
 def attend_kernel(
@@ -470,8 +489,10 @@
     bound = jnp.max(upper_o[:, :, -16:]).astype(F32)
 
     weight_q, _ = lax.optimization_barrier((query_base_weight, lower_near))
+    weight_q = fetch(weight_q, "fetch_query")
+    half_done = query_project(0, t[None], lower_near, upper, weight_q, mine, theirs)
     query_effective, own, other = query_project(
-        t[None], lower_near, lower_far, upper, fetch(weight_q, "fetch_query"), mine, theirs
+        1, t[None], lower_far, upper, weight_q, mine, theirs, half_done
     )
     other = swap(other)
 

time: 99.8 us -> 97.3 us (0.975)
  waiting for transfers between devices: 25.1 us -> 21.7 us
    ppermute x22, waiting for transfers between devices: 25.1 us -> 20.7 us  [hop(): return lax.ppermute(value, 'tp', [(i, i ^ distance) for i in range(total)])]
    pallas_call x1 -> x2, Pallas kernels: 6.46 us -> 7.09 us  [query_project(): pl.pallas_call(functools.partial(query_kernel, y), in_specs=[SMEM] + [VME...]
  transfers between devices with their start and end apart: 29 -> 29, of which waited for: 8 -> 8; matrix products, arithmetic and copies ran while one was open for 3% -> 3% of each run, Pallas kernels for 21% -> 22%
where the time goes in v5:
time: 97.3 us; the launch traced here: 97 us
  starting transfers between devices  36.8 us (38%)
  Pallas kernels  32.5 us (33%)
  waiting for transfers between devices  21.7 us (22%)
  other arithmetic  2.88 us (3%)
  between operations  1.96 us (2%)
  local copies, waits for them, and re-layouts  1.09 us (1%)
    ppermute x22, starting transfers between devices, hop(): return lax.ppermute(value, 'tp', [(i, i ^ distance) for i in range(total)])  35.3 us
    ppermute x22, waiting for transfers between devices, hop(): return lax.ppermute(value, 'tp', [(i, i ^ distance) for i in range(total)])  20.7 us
    pallas_call x1, Pallas kernels, output_project(): pl.pallas_call(output_kernel, in_specs=[SMEM, VMEM, VMEM, ANY, VMEM, VMEM...  8.7 us
    pallas_call x1, Pallas kernels, attend(): pl.pallas_call(functools.partial(attend_kernel, steps, scale), in_specs=[...  7.34 us
    pallas_call x2, Pallas kernels, query_project(): pl.pallas_call(functools.partial(query_kernel, y), in_specs=[SMEM] + [VME...  7.09 us
    pallas_call x1, Pallas kernels, fetch(): pl.pallas_call(fetch_kernel, in_specs=[ANY], out_specs=VMEM, out_shape=pl...  3.39 us
    pallas_call x1, Pallas kernels, with_largest_in_reach(): pl.pallas_call(reach_kernel, in_specs=[SMEM, ANY, ANY], out_specs=VMEM, o...  3.17 us
    pallas_call x1, Pallas kernels, finish(): pl.pallas_call(finish_kernel, in_specs=[SMEM, SMEM] + [VMEM] * 4, out_spe...  2.86 us
  transfers between devices with their start and end apart: 29, of which 8 were waited for; matrix products, arithmetic and copies ran while one was open for 3% of the time, Pallas kernels for 22%

profile of v5, /device:TPU:0, one launch (start us, length us, event | category | flops | bytes accessed | tf_op | source)
XLA Modules:
  0.0 97.0 jit_solution(18007359085484680299)
XLA Ops:
  0.6 3.1 %collective-permute-start.1 = (bf16[64,512]{1,0:T(8,128)(2,1)}, bf16[64,512]{1,0:T(8,128)(2,1)S(1)}, u32[]{:S(2)}, u32[]{:S(2)}) collective-permute-start(bf16[64,512]{1,0:T(8,128)(2,1)} %bitcast.86), channel_id=1, source_target_pairs={{0,2},{1,3},{2,0},{3,1},{4,6},{5,7},{6,4},{7,5},{8,10},{9,11},{10,... | collective-permute-start | bytes 196616 | tf_op jit(solution)/shard_map/ppermute | solution.py:31
  3.7 2.6 %collective-permute-start.2 = (bf16[64,512]{1,0:T(8,128)(2,1)}, bf16[64,512]{1,0:T(8,128)(2,1)S(1)}, u32[]{:S(2)}, u32[]{:S(2)}) collective-permute-start(bf16[64,512]{1,0:T(8,128)(2,1)} %bitcast.87), channel_id=1, source_target_pairs={{0,4},{1,5},{2,6},{3,7},{4,0},{5,1},{6,2},{7,3},{8,12},{9,13},{10,... | collective-permute-start | bytes 196616 | tf_op jit(solution)/shard_map/ppermute | solution.py:31
  7.0 3.2 %with_largest_in_reach.1 = bf16[272,128]{1,0:T(8,128)(2,1)S(1)} custom-call(s32[8]{0:T(128)S(1)} %copy-done.1, bf16[8,2048,128]{2,1,0:T(8,128)(2,1)} %bitcast.67, bf16[64,512]{1,0:T(8,128)(2,1)} %upper.1), custom_call_target="tpu_custom_call" | custom-call | flops 8388608 | bytes 4194304 | tf_op jit(solution)/shard_map/with_largest_in_reach/pallas_call | solution.py:110
  12.0 1.0 %collective-permute-done = bf16[16,128]{1,0:T(8,128)(2,1)S(1)} collective-permute-done((bf16[16,128]{1,0:T(8,128)(2,1)S(1)}, bf16[16,128]{1,0:T(8,128)(2,1)S(1)}, u32[]{:S(2)}, u32[]{:S(2)}) %collective-permute-start) | collective-permute-done | bytes 4128 | tf_op jit(solution)/shard_map/ppermute | solution.py:35
  13.2 1.8 %collective-permute-start.9 = (bf16[4,64,512]{2,1,0:T(8,128)(2,1)S(1)}, bf16[4,64,512]{2,1,0:T(8,128)(2,1)S(1)}, u32[]{:S(2)}, u32[]{:S(2)}) collective-permute-start(bf16[4,64,512]{2,1,0:T(8,128)(2,1)S(1)} %pad_maximum_fusion.2.lower), channel_id=1, source_target_pairs={{0,1},{1,0},{2,3},{3,2},{4,5},{5,4},{6,7},{7,6},{8,9},{9,8},{10,11... | collective-permute-start | bytes 786440 | tf_op jit(solution)/shard_map/ppermute | solution.py:31
  15.0 3.4 %fetch_query.1.base = bf16[4096,1024]{1,0:T(8,128)(2,1)S(1)} custom-call(bf16[4096,1024]{1,0:T(8,128)(2,1)} %source), custom_call_target="tpu_custom_call" | custom-call | bytes 8388608 | tf_op jit(solution)/shard_map/fetch_query/pallas_call | solution.py:62
  18.9 3.6 %query_project.2 = (bf16[4096,1024]{1,0:T(8,128)(2,1)}, f32[64,1024]{1,0:T(8,128)S(1)}, f32[64,1024]{1,0:T(8,128)S(1)}) custom-call(s32[1]{0:T(128)} %bitcast.place, bf16[4,64,512]{2,1,0:T(8,128)(2,1)S(1)} %pad_maximum_fusion.2.lower, bf16[64,1024]{1,0:T(8,128)(2,1)S(1)} %fusion.3.upper, bf16[4096,1024]{1,0:T(8,128)(2,1)S(1)} %fetch_query.1.base, ...), custom_call_target="tpu_custom_call" | custom-call | flops 805306368 | bytes 4194304 | tf_op jit(solution)/shard_map/query_project/pallas_call | solution.py:168
  22.5 3.5 %query_project.3 = (bf16[4096,1024]{1,0:T(8,128)(2,1)}, f32[64,1024]{1,0:T(8,128)S(1)}, f32[64,1024]{1,0:T(8,128)S(1)}) custom-call(s32[1]{0:T(128)} %bitcast.place, bf16[4,64,512]{2,1,0:T(8,128)(2,1)S(1)} %collective-permute-done.9.lower, bf16[64,1024]{1,0:T(8,128)(2,1)S(1)} %fusion.3.upper, ...), custom_call_target="tpu_custom_call", output_to_operand_aliasing={{0}: (6, {})} | custom-call | flops 805306368 | bytes 4194304 | tf_op jit(solution)/shard_map/query_project/pallas_call | solution.py:168
  26.2 1.0 collective-permute-start.5
  27.2 3.5 %collective-permute-start.6 = (bf16[2,272,128]{2,1,0:T(8,128)(2,1)S(1)}, bf16[2,272,128]{2,1,0:T(8,128)(2,1)S(1)}, u32[]{:S(2)}, u32[]{:S(2)}) collective-permute-start(bf16[2,272,128]{2,1,0:T(8,128)(2,1)S(1)} %get-tuple-element.57), channel_id=1, source_target_pairs={{0,4},{1,5},{2,6},{3,7},{4,0},{5,1},{6,2},{7,3},{8,12},{9,13},{10,... | collective-permute-start | bytes 417800 | tf_op jit(solution)/shard_map/ppermute | solution.py:31
  30.7 7.3 %attend.1.mine = bf16[64,1024]{1,0:T(8,128)(2,1)S(1)} custom-call(s32[8]{0:T(128)S(1)} %copy-done.2, f32[64,1024]{1,0:T(8,128)S(1)} %get-tuple-element.32.own, f32[64,1024]{1,0:T(8,128)S(1)} %collective-permute-done.11.other, bf16[1,1024]{1,0:T(2,128)(2,1)S(1)} %broadcast_in_dim.8.bias, f32[64,128]{1,0:T(8,128)S(1)} %get-tuple-element.63.cosine, ...), custom_call_target="tpu_custom_call" | custom-call | flops 536870912 | bytes 8388608 | tf_op jit(solution)/shard_map/attend/pallas_call | solution.py:263
  38.2 3.0 %collective-permute-done.6 = bf16[2,272,128]{2,1,0:T(8,128)(2,1)S(1)} collective-permute-done((bf16[2,272,128]{2,1,0:T(8,128)(2,1)S(1)}, bf16[2,272,128]{2,1,0:T(8,128)(2,1)S(1)}, u32[]{:S(2)}, u32[]{:S(2)}) %collective-permute-start.6) | collective-permute-done | bytes 139296 | tf_op jit(solution)/shard_map/ppermute | solution.py:31
  42.5 8.7 %output_project.1 = (bf16[1024,4096]{1,0:T(8,128)(2,1)}, f32[2,4,64,512]{3,2,1,0:T(8,128)S(1)}, f32[4,2,64,512]{3,2,1,0:T(8,128)S(1)}) custom-call(s32[1]{0:T(128)} %bitcast.place, bf16[64,1024]{1,0:T(8,128)(2,1)S(1)} %fusion.5.lower, bf16[4,2,272,128]{3,2,1,0:T(8,128)(2,1)S(1)} %pad_maximum_fusion.upper, bf16[1024,4096]{1,0:T(8,128)(2,1)} %base.1, ...), custom_call_target="tpu_custom_call" | custom-call | flops 1610612736 | bytes 16777216 | tf_op jit(solution)/shard_map/output_project/pallas_call | solution.py:329
  51.3 1.6 %collective-permute-start.13 = (f16[4,64,512]{2,1,0:T(8,128)(2,1)S(1)}, f16[4,64,512]{2,1,0:T(8,128)(2,1)S(1)}, u32[]{:S(2)}, u32[]{:S(2)}) collective-permute-start(f16[4,64,512]{2,1,0:T(8,128)(2,1)S(1)} %fusion), channel_id=1, source_target_pairs={{0,1},{1,0},{2,3},{3,2},{4,5},{5,4},{6,7},{7,6},{8,9},{9,8},{10,11... | collective-permute-start | bytes 786440 | tf_op jit(solution)/shard_map/ppermute | solution.py:31
  53.0 3.2 %collective-permute-start.14 = (f16[2,64,512]{2,1,0:T(8,128)(2,1)S(1)}, f16[2,64,512]{2,1,0:T(8,128)(2,1)S(1)}, u32[]{:S(2)}, u32[]{:S(2)}) collective-permute-start(f16[2,64,512]{2,1,0:T(8,128)(2,1)S(1)} %get-tuple-element.48), channel_id=1, source_target_pairs={{0,2},{1,3},{2,0},{3,1},{4,6},{5,7},{6,4},{7,5},{8,10},{9,11},{10,... | collective-permute-start | bytes 393224 | tf_op jit(solution)/shard_map/ppermute | solution.py:31
  56.2 1.1 %collective-permute-start.15 = (f16[2,64,512]{2,1,0:T(8,128)(2,1)S(1)}, f16[2,64,512]{2,1,0:T(8,128)(2,1)S(1)}, u32[]{:S(2)}, u32[]{:S(2)}) collective-permute-start(f16[2,64,512]{2,1,0:T(8,128)(2,1)S(1)} %get-tuple-element.47), channel_id=1, source_target_pairs={{0,4},{1,5},{2,6},{3,7},{4,0},{5,1},{6,2},{7,3},{8,12},{9,13},{10,... | collective-permute-start | bytes 393224 | tf_op jit(solution)/shard_map/ppermute | solution.py:31
  57.3 1.4 %collective-permute-start.16 = (f16[2,64,512]{2,1,0:T(8,128)(2,1)S(1)}, f16[2,64,512]{2,1,0:T(8,128)(2,1)S(1)}, u32[]{:S(2)}, u32[]{:S(2)}) collective-permute-start(f16[2,64,512]{2,1,0:T(8,128)(2,1)S(1)} %get-tuple-element.46), channel_id=1, source_target_pairs={{0,6},{1,7},{2,4},{3,5},{4,2},{5,3},{6,0},{7,1},{8,14},{9,15},{10,... | collective-permute-start | bytes 393224 | tf_op jit(solution)/shard_map/ppermute | solution.py:31
  59.0 3.7 %collective-permute-start.17 = (f16[64,512]{1,0:T(8,128)(2,1)S(1)}, f16[64,512]{1,0:T(8,128)(2,1)S(1)}, u32[]{:S(2)}, u32[]{:S(2)}) collective-permute-start(f16[64,512]{1,0:T(8,128)(2,1)S(1)} %get-tuple-element.53), channel_id=1, source_target_pairs={{0,2},{1,3},{2,0},{3,1},{4,6},{5,7},{6,4},{7,5},{8,10},{9,11},{10,... | collective-permute-start | bytes 196616 | tf_op jit(solution)/shard_map/ppermute | solution.py:31
  62.7 1.1 %collective-permute-start.18 = (f16[64,512]{1,0:T(8,128)(2,1)S(1)}, f16[64,512]{1,0:T(8,128)(2,1)S(1)}, u32[]{:S(2)}, u32[]{:S(2)}) collective-permute-start(f16[64,512]{1,0:T(8,128)(2,1)S(1)} %get-tuple-element.55), channel_id=1, source_target_pairs={{0,4},{1,5},{2,6},{3,7},{4,0},{5,1},{6,2},{7,3},{8,12},{9,13},{10,... | collective-permute-start | bytes 196616 | tf_op jit(solution)/shard_map/ppermute | solution.py:31
  63.8 1.4 %collective-permute-start.19 = (f16[64,512]{1,0:T(8,128)(2,1)S(1)}, f16[64,512]{1,0:T(8,128)(2,1)S(1)}, u32[]{:S(2)}, u32[]{:S(2)}) collective-permute-start(f16[64,512]{1,0:T(8,128)(2,1)S(1)} %get-tuple-element.54), channel_id=1, source_target_pairs={{0,6},{1,7},{2,4},{3,5},{4,2},{5,3},{6,0},{7,1},{8,14},{9,15},{10,... | collective-permute-start | bytes 196616 | tf_op jit(solution)/shard_map/ppermute | solution.py:31
  65.2 6.4 %collective-permute-done.15 = f16[2,64,512]{2,1,0:T(8,128)(2,1)S(1)} collective-permute-done((f16[2,64,512]{2,1,0:T(8,128)(2,1)S(1)}, f16[2,64,512]{2,1,0:T(8,128)(2,1)S(1)}, u32[]{:S(2)}, u32[]{:S(2)}) %collective-permute-start.15) | collective-permute-done | bytes 131104 | tf_op jit(solution)/shard_map/ppermute | solution.py:31
  72.4 2.7 %collective-permute-done.18 = f16[64,512]{1,0:T(8,128)(2,1)S(1)} collective-permute-done((f16[64,512]{1,0:T(8,128)(2,1)S(1)}, f16[64,512]{1,0:T(8,128)(2,1)S(1)}, u32[]{:S(2)}, u32[]{:S(2)}) %collective-permute-start.18) | collective-permute-done | bytes 65568 | tf_op jit(solution)/shard_map/ppermute | solution.py:31
  75.1 1.3 %collective-permute-start.20 = (f16[64,512]{1,0:T(8,128)(2,1)S(1)}, f16[64,512]{1,0:T(8,128)(2,1)S(1)}, u32[]{:S(2)}, u32[]{:S(2)}) collective-permute-start(f16[64,512]{1,0:T(8,128)(2,1)S(1)} %fusion.10), channel_id=1, source_target_pairs={{0,2},{1,3},{2,0},{3,1},{4,6},{5,7},{6,4},{7,5},{8,10},{9,11},{10,... | collective-permute-start | bytes 196616 | tf_op jit(solution)/shard_map/ppermute | solution.py:31
  76.5 1.7 %collective-permute-start.21 = (f16[64,512]{1,0:T(8,128)(2,1)S(1)}, f16[64,512]{1,0:T(8,128)(2,1)S(1)}, u32[]{:S(2)}, u32[]{:S(2)}) collective-permute-start(f16[64,512]{1,0:T(8,128)(2,1)S(1)} %fusion.10), channel_id=1, source_target_pairs={{0,4},{1,5},{2,6},{3,7},{4,0},{5,1},{6,2},{7,3},{8,12},{9,13},{10,... | collective-permute-start | bytes 196616 | tf_op jit(solution)/shard_map/ppermute | solution.py:31
  78.2 1.4 %collective-permute-start.22 = (f16[64,512]{1,0:T(8,128)(2,1)S(1)}, f16[64,512]{1,0:T(8,128)(2,1)S(1)}, u32[]{:S(2)}, u32[]{:S(2)}) collective-permute-start(f16[64,512]{1,0:T(8,128)(2,1)S(1)} %fusion.10), channel_id=1, source_target_pairs={{0,6},{1,7},{2,4},{3,5},{4,2},{5,3},{6,0},{7,1},{8,14},{9,15},{10,... | collective-permute-start | bytes 196616 | tf_op jit(solution)/shard_map/ppermute | solution.py:31
  79.6 0.9 collective-permute-start.26
  80.5 2.1 %collective-permute-start.27 = (f16[2,64,512]{2,1,0:T(8,128)(2,1)S(1)}, f16[2,64,512]{2,1,0:T(8,128)(2,1)S(1)}, u32[]{:S(2)}, u32[]{:S(2)}) collective-permute-start(f16[2,64,512]{2,1,0:T(8,128)(2,1)S(1)} %add_convert_fusion), channel_id=1, source_target_pairs={{0,4},{1,5},{2,6},{3,7},{4,0},{5,1},{6,2},{7,3},{8,12},{9,13},{10,... | collective-permute-start | bytes 393224 | tf_op jit(solution)/shard_map/ppermute | solution.py:31
  82.7 1.4 %collective-permute-start.28 = (f16[2,64,512]{2,1,0:T(8,128)(2,1)S(1)}, f16[2,64,512]{2,1,0:T(8,128)(2,1)S(1)}, u32[]{:S(2)}, u32[]{:S(2)}) collective-permute-start(f16[2,64,512]{2,1,0:T(8,128)(2,1)S(1)} %add_convert_fusion), channel_id=1, source_target_pairs={{0,6},{1,7},{2,4},{3,5},{4,2},{5,3},{6,0},{7,1},{8,14},{9,15},{10,... | collective-permute-start | bytes 393224 | tf_op jit(solution)/shard_map/ppermute | solution.py:31
  84.8 0.7 collective-permute-start.23
  85.5 2.9 %collective-permute-done.26 = f16[2,64,512]{2,1,0:T(8,128)(2,1)S(1)} collective-permute-done((f16[2,64,512]{2,1,0:T(8,128)(2,1)S(1)}, f16[2,64,512]{2,1,0:T(8,128)(2,1)S(1)}, u32[]{:S(2)}, u32[]{:S(2)}) %collective-permute-start.26) | collective-permute-done | bytes 131104 | tf_op jit(solution)/shard_map/ppermute | solution.py:31
  88.4 5.0 %collective-permute-done.27 = f16[2,64,512]{2,1,0:T(8,128)(2,1)S(1)} collective-permute-done((f16[2,64,512]{2,1,0:T(8,128)(2,1)S(1)}, f16[2,64,512]{2,1,0:T(8,128)(2,1)S(1)}, u32[]{:S(2)}, u32[]{:S(2)}) %collective-permute-start.27) | collective-permute-done | bytes 131104 | tf_op jit(solution)/shard_map/ppermute | solution.py:31
  94.0 2.9 %finish.1 = (bf16[64,8192]{1,0:T(8,128)(2,1)}, bf16[64,8192]{1,0:T(8,128)(2,1)}) custom-call(s32[2]{0:T(128)S(1)} %pad_add_fusion.place, f32[1]{0:T(128)} %bitcast.14.bound, bf16[64,8192]{1,0:T(8,128)(2,1)S(1)} %bitcast.65, bf16[1,8192]{1,0:T(2,128)(2,1)S(1)} %broadcast_in_dim.7.gain, f32[8,64,512]{2,1,0:T(8,128)S(1)} %bitcast.66, ...), custom_call_target="tpu_custom_call" | custom-call | flops 4194304 | bytes 7340032 | tf_op jit(solution)/shard_map/finish/pallas_call | solution.py:389
  (91 shorter events, 6.6 us)
Async XLA Ops:
  0.6 9.6 %copy-start = (bf16[8,8,8192]{2,1,0:T(8,128)(2,1)S(1)}, bf16[8,8,8192]{2,1,0:T(8,128)(2,1)}, u32[]{:S(2)}) copy-start(bf16[8,8,8192]{2,1,0:T(8,128)(2,1)} %param.14) | copy-start | bytes 3145732
  0.6 12.5 %collective-permute-start.1 = (bf16[64,512]{1,0:T(8,128)(2,1)}, bf16[64,512]{1,0:T(8,128)(2,1)S(1)}, u32[]{:S(2)}, u32[]{:S(2)}) collective-permute-start(bf16[64,512]{1,0:T(8,128)(2,1)} %bitcast.86), channel_id=1, source_target_pairs={{0,2},{1,3},{2,0},{3,1},{4,6},{5,7},{6,4},{7,5},{8,10},{9,11},{10,... | collective-permute-start | bytes 196616 | tf_op jit(solution)/shard_map/ppermute | solution.py:31
  3.7 9.4 %collective-permute-start.2 = (bf16[64,512]{1,0:T(8,128)(2,1)}, bf16[64,512]{1,0:T(8,128)(2,1)S(1)}, u32[]{:S(2)}, u32[]{:S(2)}) collective-permute-start(bf16[64,512]{1,0:T(8,128)(2,1)} %bitcast.87), channel_id=1, source_target_pairs={{0,4},{1,5},{2,6},{3,7},{4,0},{5,1},{6,2},{7,3},{8,12},{9,13},{10,... | collective-permute-start | bytes 196616 | tf_op jit(solution)/shard_map/ppermute | solution.py:31
  6.3 6.8 %collective-permute-start.3 = (bf16[64,512]{1,0:T(8,128)(2,1)}, bf16[64,512]{1,0:T(8,128)(2,1)S(1)}, u32[]{:S(2)}, u32[]{:S(2)}) collective-permute-start(bf16[64,512]{1,0:T(8,128)(2,1)} %bitcast.88), channel_id=1, source_target_pairs={{0,6},{1,7},{2,4},{3,5},{4,2},{5,3},{6,0},{7,1},{8,14},{9,15},{10,... | collective-permute-start | bytes 196616 | tf_op jit(solution)/shard_map/ppermute | solution.py:31
  7.0 6.2 %copy-start.5 = (bf16[512,64]{0,1:T(8,128)(2,1)S(1)}, bf16[512,64]{0,1:T(8,128)(2,1)}, u32[]{:S(2)}) copy-start(bf16[512,64]{0,1:T(8,128)(2,1)} %param.20) | copy-start | bytes 196612
  11.0 7.8 %collective-permute-start.10 = (bf16[64,4096]{1,0:T(8,128)(2,1)S(1)}, bf16[64,4096]{1,0:T(8,128)(2,1)S(1)}, u32[]{:S(2)}, u32[]{:S(2)}) collective-permute-start(bf16[64,4096]{1,0:T(8,128)(2,1)S(1)} %get-tuple-element.49), channel_id=1, source_target_pairs={{0,8},{8,0},{1,9},{9,1},{2,10},{10,2},{3,11},{11,3},{4,12},{12,4},... | collective-permute-start | bytes 1572872 | tf_op jit(solution)/shard_map/ppermute | solution.py:35
  11.1 1.9 %collective-permute-start = (bf16[16,128]{1,0:T(8,128)(2,1)S(1)}, bf16[16,128]{1,0:T(8,128)(2,1)S(1)}, u32[]{:S(2)}, u32[]{:S(2)}) collective-permute-start(bf16[16,128]{1,0:T(8,128)(2,1)S(1)} %slice.64), channel_id=1, source_target_pairs={{0,8},{8,0},{1,9},{9,1},{2,10},{10,2},{3,11},{11,3},{4,12},{12,4},... | collective-permute-start | bytes 12296 | tf_op jit(solution)/shard_map/ppermute | solution.py:35
  13.0 5.8 %collective-permute-start.8 = (bf16[64,1024]{1,0:T(8,128)(2,1)S(1)}, bf16[64,1024]{1,0:T(8,128)(2,1)S(1)}, u32[]{:S(2)}, u32[]{:S(2)}) collective-permute-start(bf16[64,1024]{1,0:T(8,128)(2,1)S(1)} %pad_maximum_fusion.5), channel_id=1, source_target_pairs={{0,8},{8,0},{1,9},{9,1},{2,10},{10,2},{3,11},{11,3},{4,12},{12,4},... | collective-permute-start | bytes 393224 | tf_op jit(solution)/shard_map/ppermute | solution.py:35
  13.2 9.3 %collective-permute-start.9 = (bf16[4,64,512]{2,1,0:T(8,128)(2,1)S(1)}, bf16[4,64,512]{2,1,0:T(8,128)(2,1)S(1)}, u32[]{:S(2)}, u32[]{:S(2)}) collective-permute-start(bf16[4,64,512]{2,1,0:T(8,128)(2,1)S(1)} %pad_maximum_fusion.2.lower), channel_id=1, source_target_pairs={{0,1},{1,0},{2,3},{3,2},{4,5},{5,4},{6,7},{7,6},{8,9},{9,8},{10,11... | collective-permute-start | bytes 786440 | tf_op jit(solution)/shard_map/ppermute | solution.py:31
  18.4 7.7 %collective-permute-start.4 = (bf16[272,128]{1,0:T(8,128)(2,1)S(1)}, bf16[272,128]{1,0:T(8,128)(2,1)S(1)}, u32[]{:S(2)}, u32[]{:S(2)}) collective-permute-start(bf16[272,128]{1,0:T(8,128)(2,1)S(1)} %pad_maximum_fusion.8), channel_id=1, source_target_pairs={{0,1},{1,0},{2,3},{3,2},{4,5},{5,4},{6,7},{7,6},{8,9},{9,8},{10,11... | collective-permute-start | bytes 208904 | tf_op jit(solution)/shard_map/ppermute | solution.py:31
  26.0 4.7 %collective-permute-start.11 = (f32[64,1024]{1,0:T(8,128)S(1)}, f32[64,1024]{1,0:T(8,128)S(1)}, u32[]{:S(2)}, u32[]{:S(2)}) collective-permute-start(f32[64,1024]{1,0:T(8,128)S(1)} %get-tuple-element.33), channel_id=1, source_target_pairs={{0,8},{8,0},{1,9},{9,1},{2,10},{10,2},{3,11},{11,3},{4,12},{12,4},... | collective-permute-start | bytes 786440 | tf_op jit(solution)/shard_map/ppermute | solution.py:35
  26.2 11.9 %collective-permute-start.5 = (bf16[2,272,128]{2,1,0:T(8,128)(2,1)S(1)}, bf16[2,272,128]{2,1,0:T(8,128)(2,1)S(1)}, u32[]{:S(2)}, u32[]{:S(2)}) collective-permute-start(bf16[2,272,128]{2,1,0:T(8,128)(2,1)S(1)} %get-tuple-element.57), channel_id=1, source_target_pairs={{0,2},{1,3},{2,0},{3,1},{4,6},{5,7},{6,4},{7,5},{8,10},{9,11},{10,... | collective-permute-start | bytes 417800 | tf_op jit(solution)/shard_map/ppermute | solution.py:31
  27.2 14.0 %collective-permute-start.6 = (bf16[2,272,128]{2,1,0:T(8,128)(2,1)S(1)}, bf16[2,272,128]{2,1,0:T(8,128)(2,1)S(1)}, u32[]{:S(2)}, u32[]{:S(2)}) collective-permute-start(bf16[2,272,128]{2,1,0:T(8,128)(2,1)S(1)} %get-tuple-element.57), channel_id=1, source_target_pairs={{0,4},{1,5},{2,6},{3,7},{4,0},{5,1},{6,2},{7,3},{8,12},{9,13},{10,... | collective-permute-start | bytes 417800 | tf_op jit(solution)/shard_map/ppermute | solution.py:31
  30.7 10.5 %collective-permute-start.7 = (bf16[2,272,128]{2,1,0:T(8,128)(2,1)S(1)}, bf16[2,272,128]{2,1,0:T(8,128)(2,1)S(1)}, u32[]{:S(2)}, u32[]{:S(2)}) collective-permute-start(bf16[2,272,128]{2,1,0:T(8,128)(2,1)S(1)} %get-tuple-element.57), channel_id=1, source_target_pairs={{0,6},{1,7},{2,4},{3,5},{4,2},{5,3},{6,0},{7,1},{8,14},{9,15},{10,... | collective-permute-start | bytes 417800 | tf_op jit(solution)/shard_map/ppermute | solution.py:31
  38.1 4.5 %collective-permute-start.12 = (bf16[64,1024]{1,0:T(8,128)(2,1)S(1)}, bf16[64,1024]{1,0:T(8,128)(2,1)S(1)}, u32[]{:S(2)}, u32[]{:S(2)}) collective-permute-start(bf16[64,1024]{1,0:T(8,128)(2,1)S(1)} %attend.1.mine), channel_id=1, source_target_pairs={{0,8},{8,0},{1,9},{9,1},{2,10},{10,2},{3,11},{11,3},{4,12},{12,4},... | collective-permute-start | bytes 393224 | tf_op jit(solution)/shard_map/ppermute | solution.py:35
  51.3 32.9 %copy-start.7 = (bf16[8192]{0:T(1024)(128)(2,1)S(1)}, bf16[8192]{0:T(1024)(128)(2,1)}, u32[]{:S(2)}) copy-start(bf16[8192]{0:T(1024)(128)(2,1)} %param.16) | copy-start | bytes 49156
  51.3 7.5 %collective-permute-start.13 = (f16[4,64,512]{2,1,0:T(8,128)(2,1)S(1)}, f16[4,64,512]{2,1,0:T(8,128)(2,1)S(1)}, u32[]{:S(2)}, u32[]{:S(2)}) collective-permute-start(f16[4,64,512]{2,1,0:T(8,128)(2,1)S(1)} %fusion), channel_id=1, source_target_pairs={{0,1},{1,0},{2,3},{3,2},{4,5},{5,4},{6,7},{7,6},{8,9},{9,8},{10,11... | collective-permute-start | bytes 786440 | tf_op jit(solution)/shard_map/ppermute | solution.py:31
  53.0 10.7 %collective-permute-start.14 = (f16[2,64,512]{2,1,0:T(8,128)(2,1)S(1)}, f16[2,64,512]{2,1,0:T(8,128)(2,1)S(1)}, u32[]{:S(2)}, u32[]{:S(2)}) collective-permute-start(f16[2,64,512]{2,1,0:T(8,128)(2,1)S(1)} %get-tuple-element.48), channel_id=1, source_target_pairs={{0,2},{1,3},{2,0},{3,1},{4,6},{5,7},{6,4},{7,5},{8,10},{9,11},{10,... | collective-permute-start | bytes 393224 | tf_op jit(solution)/shard_map/ppermute | solution.py:31
  56.2 15.4 %collective-permute-start.15 = (f16[2,64,512]{2,1,0:T(8,128)(2,1)S(1)}, f16[2,64,512]{2,1,0:T(8,128)(2,1)S(1)}, u32[]{:S(2)}, u32[]{:S(2)}) collective-permute-start(f16[2,64,512]{2,1,0:T(8,128)(2,1)S(1)} %get-tuple-element.47), channel_id=1, source_target_pairs={{0,4},{1,5},{2,6},{3,7},{4,0},{5,1},{6,2},{7,3},{8,12},{9,13},{10,... | collective-permute-start | bytes 393224 | tf_op jit(solution)/shard_map/ppermute | solution.py:31
  57.3 14.3 %collective-permute-start.16 = (f16[2,64,512]{2,1,0:T(8,128)(2,1)S(1)}, f16[2,64,512]{2,1,0:T(8,128)(2,1)S(1)}, u32[]{:S(2)}, u32[]{:S(2)}) collective-permute-start(f16[2,64,512]{2,1,0:T(8,128)(2,1)S(1)} %get-tuple-element.46), channel_id=1, source_target_pairs={{0,6},{1,7},{2,4},{3,5},{4,2},{5,3},{6,0},{7,1},{8,14},{9,15},{10,... | collective-permute-start | bytes 393224 | tf_op jit(solution)/shard_map/ppermute | solution.py:31
  59.0 12.6 %collective-permute-start.17 = (f16[64,512]{1,0:T(8,128)(2,1)S(1)}, f16[64,512]{1,0:T(8,128)(2,1)S(1)}, u32[]{:S(2)}, u32[]{:S(2)}) collective-permute-start(f16[64,512]{1,0:T(8,128)(2,1)S(1)} %get-tuple-element.53), channel_id=1, source_target_pairs={{0,2},{1,3},{2,0},{3,1},{4,6},{5,7},{6,4},{7,5},{8,10},{9,11},{10,... | collective-permute-start | bytes 196616 | tf_op jit(solution)/shard_map/ppermute | solution.py:31
  62.7 12.4 %collective-permute-start.18 = (f16[64,512]{1,0:T(8,128)(2,1)S(1)}, f16[64,512]{1,0:T(8,128)(2,1)S(1)}, u32[]{:S(2)}, u32[]{:S(2)}) collective-permute-start(f16[64,512]{1,0:T(8,128)(2,1)S(1)} %get-tuple-element.55), channel_id=1, source_target_pairs={{0,4},{1,5},{2,6},{3,7},{4,0},{5,1},{6,2},{7,3},{8,12},{9,13},{10,... | collective-permute-start | bytes 196616 | tf_op jit(solution)/shard_map/ppermute | solution.py:31
  63.8 11.3 %collective-permute-start.19 = (f16[64,512]{1,0:T(8,128)(2,1)S(1)}, f16[64,512]{1,0:T(8,128)(2,1)S(1)}, u32[]{:S(2)}, u32[]{:S(2)}) collective-permute-start(f16[64,512]{1,0:T(8,128)(2,1)S(1)} %get-tuple-element.54), channel_id=1, source_target_pairs={{0,6},{1,7},{2,4},{3,5},{4,2},{5,3},{6,0},{7,1},{8,14},{9,15},{10,... | collective-permute-start | bytes 196616 | tf_op jit(solution)/shard_map/ppermute | solution.py:31
  71.7 7.9 %collective-permute-start.24 = (f16[2,64,512]{2,1,0:T(8,128)(2,1)S(1)}, f16[2,64,512]{2,1,0:T(8,128)(2,1)S(1)}, u32[]{:S(2)}, u32[]{:S(2)}) collective-permute-start(f16[2,64,512]{2,1,0:T(8,128)(2,1)S(1)} %fusion.1), channel_id=1, source_target_pairs={{0,8},{8,0},{1,9},{9,1},{2,10},{10,2},{3,11},{11,3},{4,12},{12,4},... | collective-permute-start | bytes 393224 | tf_op jit(solution)/shard_map/ppermute | solution.py:35
  71.8 7.8 %collective-permute-start.25 = (f16[2,64,512]{2,1,0:T(8,128)(2,1)S(1)}, f16[2,64,512]{2,1,0:T(8,128)(2,1)S(1)}, u32[]{:S(2)}, u32[]{:S(2)}) collective-permute-start(f16[2,64,512]{2,1,0:T(8,128)(2,1)S(1)} %fusion.1), channel_id=1, source_target_pairs={{0,9},{1,8},{2,11},{3,10},{4,13},{5,12},{6,15},{7,14},{8,1},{9,0},... | collective-permute-start | bytes 393224 | tf_op jit(solution)/shard_map/ppermute | solution.py:408
  75.1 7.5 %collective-permute-start.20 = (f16[64,512]{1,0:T(8,128)(2,1)S(1)}, f16[64,512]{1,0:T(8,128)(2,1)S(1)}, u32[]{:S(2)}, u32[]{:S(2)}) collective-permute-start(f16[64,512]{1,0:T(8,128)(2,1)S(1)} %fusion.10), channel_id=1, source_target_pairs={{0,2},{1,3},{2,0},{3,1},{4,6},{5,7},{6,4},{7,5},{8,10},{9,11},{10,... | collective-permute-start | bytes 196616 | tf_op jit(solution)/shard_map/ppermute | solution.py:31
  76.5 7.7 %collective-permute-start.21 = (f16[64,512]{1,0:T(8,128)(2,1)S(1)}, f16[64,512]{1,0:T(8,128)(2,1)S(1)}, u32[]{:S(2)}, u32[]{:S(2)}) collective-permute-start(f16[64,512]{1,0:T(8,128)(2,1)S(1)} %fusion.10), channel_id=1, source_target_pairs={{0,4},{1,5},{2,6},{3,7},{4,0},{5,1},{6,2},{7,3},{8,12},{9,13},{10,... | collective-permute-start | bytes 196616 | tf_op jit(solution)/shard_map/ppermute | solution.py:31
  78.2 6.6 %collective-permute-start.22 = (f16[64,512]{1,0:T(8,128)(2,1)S(1)}, f16[64,512]{1,0:T(8,128)(2,1)S(1)}, u32[]{:S(2)}, u32[]{:S(2)}) collective-permute-start(f16[64,512]{1,0:T(8,128)(2,1)S(1)} %fusion.10), channel_id=1, source_target_pairs={{0,6},{1,7},{2,4},{3,5},{4,2},{5,3},{6,0},{7,1},{8,14},{9,15},{10,... | collective-permute-start | bytes 196616 | tf_op jit(solution)/shard_map/ppermute | solution.py:31
  79.6 8.8 %collective-permute-start.26 = (f16[2,64,512]{2,1,0:T(8,128)(2,1)S(1)}, f16[2,64,512]{2,1,0:T(8,128)(2,1)S(1)}, u32[]{:S(2)}, u32[]{:S(2)}) collective-permute-start(f16[2,64,512]{2,1,0:T(8,128)(2,1)S(1)} %add_convert_fusion), channel_id=1, source_target_pairs={{0,2},{1,3},{2,0},{3,1},{4,6},{5,7},{6,4},{7,5},{8,10},{9,11},{10,... | collective-permute-start | bytes 393224 | tf_op jit(solution)/shard_map/ppermute | solution.py:31
  80.5 12.9 %collective-permute-start.27 = (f16[2,64,512]{2,1,0:T(8,128)(2,1)S(1)}, f16[2,64,512]{2,1,0:T(8,128)(2,1)S(1)}, u32[]{:S(2)}, u32[]{:S(2)}) collective-permute-start(f16[2,64,512]{2,1,0:T(8,128)(2,1)S(1)} %add_convert_fusion), channel_id=1, source_target_pairs={{0,4},{1,5},{2,6},{3,7},{4,0},{5,1},{6,2},{7,3},{8,12},{9,13},{10,... | collective-permute-start | bytes 393224 | tf_op jit(solution)/shard_map/ppermute | solution.py:31
  82.7 10.7 %collective-permute-start.28 = (f16[2,64,512]{2,1,0:T(8,128)(2,1)S(1)}, f16[2,64,512]{2,1,0:T(8,128)(2,1)S(1)}, u32[]{:S(2)}, u32[]{:S(2)}) collective-permute-start(f16[2,64,512]{2,1,0:T(8,128)(2,1)S(1)} %add_convert_fusion), channel_id=1, source_target_pairs={{0,6},{1,7},{2,4},{3,5},{4,2},{5,3},{6,0},{7,1},{8,14},{9,15},{10,... | collective-permute-start | bytes 393224 | tf_op jit(solution)/shard_map/ppermute | solution.py:31
  84.8 8.9 %collective-permute-start.23 = (f16[4,64,512]{2,1,0:T(8,128)(2,1)S(1)}, f16[4,64,512]{2,1,0:T(8,128)(2,1)S(1)}, u32[]{:S(2)}, u32[]{:S(2)}) collective-permute-start(f16[4,64,512]{2,1,0:T(8,128)(2,1)S(1)} %get-tuple-element.52), channel_id=1, source_target_pairs={{0,1},{1,0},{2,3},{3,2},{4,5},{5,4},{6,7},{7,6},{8,9},{9,8},{10,11... | collective-permute-start | bytes 786440 | tf_op jit(solution)/shard_map/ppermute | solution.py:31
  (7 other events, 27.3 us)

commit v6 on v5

--- a/solution.py
+++ b/solution.py
@@ -306,7 +306,7 @@
             def _():
                 out.wait()
 
-            factor = [upper[z, y, n * rank : (n + 1) * rank] for n in range(width // 128)]
+            factor = [upper[lax.rem(outer - z, outer), y, n * rank : (n + 1) * rank] for n in range(width // 128)]
             update = contract_first(lower[...], jnp.concatenate(factor, axis=1))
             fetch(k).wait()
             fresh[y] = (held[k].astype(F32) + update).astype(BF16)
@@ -413,6 +413,11 @@
     return jnp.stack([value] + [hop(value, 2 * k) for k in range(1, outer)])
 
 
+def along_z_far_first(value):
+    outer = lax.axis_size("tp") // 2
+    return jnp.stack([value] + [hop(value, 2 * k) for k in range(outer - 1, 0, -1)])
+
+
 def along_y(value):
     return jnp.stack([value, hop(value, 1)])
 
@@ -424,7 +429,7 @@
         return value.astype(F16)
 
     across = hop(narrow(shrink(own[1])), 1)
-    arrived = [hop(narrow(shrink(other[k])), 2 * k) for k in range(1, outer)]
+    arrived = [hop(narrow(shrink(other[k])), 2 * k) for k in range(outer - 1, 0, -1)]
     summed = shrink(own[0]) + across.astype(F32)
     ended = [hop(narrow(summed[k]), 2 * k) for k in range(1, outer)]
     arrived, ended[:1] = lax.optimization_barrier((arrived, ended[:1]))
@@ -485,7 +490,7 @@
 
     message = jnp.concatenate([message[:-16], bound], axis=0)
     message, lower_near = lax.optimization_barrier((message, lower_near))
-    upper_o = along_z(along_y(message))
+    upper_o = along_z_far_first(along_y(message))
     bound = jnp.max(upper_o[:, :, -16:]).astype(F32)
 
     weight_q, _ = lax.optimization_barrier((query_base_weight, lower_near))

time: 97.3 us -> 94.3 us (0.969)
  starting transfers between devices: 36.8 us -> 34.7 us
    ppermute x22, starting transfers between devices: 35.3 us -> 33.1 us  [hop(): return lax.ppermute(value, 'tp', [(i, i ^ distance) for i in range(total)])]
  transfers between devices with their start and end apart: 29 -> 29, of which waited for: 8 -> 7; matrix products, arithmetic and copies ran while one was open for 3% -> 3% of each run, Pallas kernels for 22% -> 22%
where the time goes in v6:
time: 94.3 us; the launch traced here: 94.2 us
  starting transfers between devices  34.7 us (37%)
  Pallas kernels  32.5 us (34%)
  waiting for transfers between devices  21.1 us (22%)
  other arithmetic  2.88 us (3%)
  between operations  1.97 us (2%)
  local copies, waits for them, and re-layouts  1.09 us (1%)
    ppermute x22, starting transfers between devices, hop(): return lax.ppermute(value, 'tp', [(i, i ^ distance) for i in range(total)])  33.1 us
    ppermute x22, waiting for transfers between devices, hop(): return lax.ppermute(value, 'tp', [(i, i ^ distance) for i in range(total)])  20.1 us
    pallas_call x1, Pallas kernels, output_project(): pl.pallas_call(output_kernel, in_specs=[SMEM, VMEM, VMEM, ANY, VMEM, VMEM...  8.68 us
    pallas_call x1, Pallas kernels, attend(): pl.pallas_call(functools.partial(attend_kernel, steps, scale), in_specs=[...  7.34 us
    pallas_call x2, Pallas kernels, query_project(): pl.pallas_call(functools.partial(query_kernel, y), in_specs=[SMEM] + [VME...  7.08 us
    pallas_call x1, Pallas kernels, fetch(): pl.pallas_call(fetch_kernel, in_specs=[ANY], out_specs=VMEM, out_shape=pl...  3.39 us
    pallas_call x1, Pallas kernels, with_largest_in_reach(): pl.pallas_call(reach_kernel, in_specs=[SMEM, ANY, ANY], out_specs=VMEM, o...  3.14 us
    pallas_call x1, Pallas kernels, finish(): pl.pallas_call(finish_kernel, in_specs=[SMEM, SMEM] + [VMEM] * 4, out_spe...  2.86 us
  transfers between devices with their start and end apart: 29, of which 7 were waited for; matrix products, arithmetic and copies ran while one was open for 3% of the time, Pallas kernels for 22%

profile of v6, /device:TPU:0, one launch (start us, length us, event | category | flops | bytes accessed | tf_op | source)
XLA Modules:
  0.0 94.2 jit_solution(16917724519630308564)
XLA Ops:
  0.6 3.1 %collective-permute-start.1 = (bf16[64,512]{1,0:T(8,128)(2,1)}, bf16[64,512]{1,0:T(8,128)(2,1)S(1)}, u32[]{:S(2)}, u32[]{:S(2)}) collective-permute-start(bf16[64,512]{1,0:T(8,128)(2,1)} %bitcast.86), channel_id=1, source_target_pairs={{0,2},{1,3},{2,0},{3,1},{4,6},{5,7},{6,4},{7,5},{8,10},{9,11},{10,... | collective-permute-start | bytes 196616 | tf_op jit(solution)/shard_map/ppermute | solution.py:31
  3.7 2.6 %collective-permute-start.2 = (bf16[64,512]{1,0:T(8,128)(2,1)}, bf16[64,512]{1,0:T(8,128)(2,1)S(1)}, u32[]{:S(2)}, u32[]{:S(2)}) collective-permute-start(bf16[64,512]{1,0:T(8,128)(2,1)} %bitcast.87), channel_id=1, source_target_pairs={{0,4},{1,5},{2,6},{3,7},{4,0},{5,1},{6,2},{7,3},{8,12},{9,13},{10,... | collective-permute-start | bytes 196616 | tf_op jit(solution)/shard_map/ppermute | solution.py:31
  6.3 0.7 copy-done.1
  7.0 3.1 %with_largest_in_reach.1 = bf16[272,128]{1,0:T(8,128)(2,1)S(1)} custom-call(s32[8]{0:T(128)S(1)} %copy-done.1, bf16[8,2048,128]{2,1,0:T(8,128)(2,1)} %bitcast.67, bf16[64,512]{1,0:T(8,128)(2,1)} %upper.1), custom_call_target="tpu_custom_call" | custom-call | flops 8388608 | bytes 4194304 | tf_op jit(solution)/shard_map/with_largest_in_reach/pallas_call | solution.py:110
  12.0 1.0 %collective-permute-done = bf16[16,128]{1,0:T(8,128)(2,1)S(1)} collective-permute-done((bf16[16,128]{1,0:T(8,128)(2,1)S(1)}, bf16[16,128]{1,0:T(8,128)(2,1)S(1)}, u32[]{:S(2)}, u32[]{:S(2)}) %collective-permute-start) | collective-permute-done | bytes 4128 | tf_op jit(solution)/shard_map/ppermute | solution.py:35
  13.2 1.8 %collective-permute-start.9 = (bf16[4,64,512]{2,1,0:T(8,128)(2,1)S(1)}, bf16[4,64,512]{2,1,0:T(8,128)(2,1)S(1)}, u32[]{:S(2)}, u32[]{:S(2)}) collective-permute-start(bf16[4,64,512]{2,1,0:T(8,128)(2,1)S(1)} %pad_maximum_fusion.2.lower), channel_id=1, source_target_pairs={{0,1},{1,0},{2,3},{3,2},{4,5},{5,4},{6,7},{7,6},{8,9},{9,8},{10,11... | collective-permute-start | bytes 786440 | tf_op jit(solution)/shard_map/ppermute | solution.py:31
  15.0 3.4 %fetch_query.1.base = bf16[4096,1024]{1,0:T(8,128)(2,1)S(1)} custom-call(bf16[4096,1024]{1,0:T(8,128)(2,1)} %source), custom_call_target="tpu_custom_call" | custom-call | bytes 8388608 | tf_op jit(solution)/shard_map/fetch_query/pallas_call | solution.py:62
  18.8 3.6 %query_project.2 = (bf16[4096,1024]{1,0:T(8,128)(2,1)}, f32[64,1024]{1,0:T(8,128)S(1)}, f32[64,1024]{1,0:T(8,128)S(1)}) custom-call(s32[1]{0:T(128)} %bitcast.place, bf16[4,64,512]{2,1,0:T(8,128)(2,1)S(1)} %pad_maximum_fusion.2.lower, bf16[64,1024]{1,0:T(8,128)(2,1)S(1)} %fusion.3.upper, bf16[4096,1024]{1,0:T(8,128)(2,1)S(1)} %fetch_query.1.base, ...), custom_call_target="tpu_custom_call" | custom-call | flops 805306368 | bytes 4194304 | tf_op jit(solution)/shard_map/query_project/pallas_call | solution.py:168
  22.5 3.5 %query_project.3 = (bf16[4096,1024]{1,0:T(8,128)(2,1)}, f32[64,1024]{1,0:T(8,128)S(1)}, f32[64,1024]{1,0:T(8,128)S(1)}) custom-call(s32[1]{0:T(128)} %bitcast.place, bf16[4,64,512]{2,1,0:T(8,128)(2,1)S(1)} %collective-permute-done.9.lower, bf16[64,1024]{1,0:T(8,128)(2,1)S(1)} %fusion.3.upper, ...), custom_call_target="tpu_custom_call", output_to_operand_aliasing={{0}: (6, {})} | custom-call | flops 805306368 | bytes 4194304 | tf_op jit(solution)/shard_map/query_project/pallas_call | solution.py:168
  26.2 3.9 %collective-permute-start.5 = (bf16[2,272,128]{2,1,0:T(8,128)(2,1)S(1)}, bf16[2,272,128]{2,1,0:T(8,128)(2,1)S(1)}, u32[]{:S(2)}, u32[]{:S(2)}) collective-permute-start(bf16[2,272,128]{2,1,0:T(8,128)(2,1)S(1)} %get-tuple-element.57), channel_id=1, source_target_pairs={{0,6},{1,7},{2,4},{3,5},{4,2},{5,3},{6,0},{7,1},{8,14},{9,15},{10,... | collective-permute-start | bytes 417800 | tf_op jit(solution)/shard_map/ppermute | solution.py:31
  30.1 0.6 collective-permute-start.7
  30.8 7.3 %attend.1.mine = bf16[64,1024]{1,0:T(8,128)(2,1)S(1)} custom-call(s32[8]{0:T(128)S(1)} %copy-done.2, f32[64,1024]{1,0:T(8,128)S(1)} %get-tuple-element.32.own, f32[64,1024]{1,0:T(8,128)S(1)} %collective-permute-done.11.other, bf16[1,1024]{1,0:T(2,128)(2,1)S(1)} %broadcast_in_dim.8.bias, f32[64,128]{1,0:T(8,128)S(1)} %get-tuple-element.63.cosine, ...), custom_call_target="tpu_custom_call" | custom-call | flops 536870912 | bytes 8388608 | tf_op jit(solution)/shard_map/attend/pallas_call | solution.py:263
  38.2 3.4 %collective-permute-done.6 = bf16[2,272,128]{2,1,0:T(8,128)(2,1)S(1)} collective-permute-done((bf16[2,272,128]{2,1,0:T(8,128)(2,1)S(1)}, bf16[2,272,128]{2,1,0:T(8,128)(2,1)S(1)}, u32[]{:S(2)}, u32[]{:S(2)}) %collective-permute-start.6) | collective-permute-done | bytes 139296 | tf_op jit(solution)/shard_map/ppermute | solution.py:31
  41.7 0.6 slice_reduce_fusion
  43.0 8.7 %output_project.1 = (bf16[1024,4096]{1,0:T(8,128)(2,1)}, f32[2,4,64,512]{3,2,1,0:T(8,128)S(1)}, f32[4,2,64,512]{3,2,1,0:T(8,128)S(1)}) custom-call(s32[1]{0:T(128)} %bitcast.place, bf16[64,1024]{1,0:T(8,128)(2,1)S(1)} %fusion.5.lower, bf16[4,2,272,128]{3,2,1,0:T(8,128)(2,1)S(1)} %pad_maximum_fusion.upper, bf16[1024,4096]{1,0:T(8,128)(2,1)} %base.1, ...), custom_call_target="tpu_custom_call" | custom-call | flops 1610612736 | bytes 16777216 | tf_op jit(solution)/shard_map/output_project/pallas_call | solution.py:329
  51.8 1.6 %collective-permute-start.13 = (f16[4,64,512]{2,1,0:T(8,128)(2,1)S(1)}, f16[4,64,512]{2,1,0:T(8,128)(2,1)S(1)}, u32[]{:S(2)}, u32[]{:S(2)}) collective-permute-start(f16[4,64,512]{2,1,0:T(8,128)(2,1)S(1)} %fusion), channel_id=1, source_target_pairs={{0,1},{1,0},{2,3},{3,2},{4,5},{5,4},{6,7},{7,6},{8,9},{9,8},{10,11... | collective-permute-start | bytes 786440 | tf_op jit(solution)/shard_map/ppermute | solution.py:31
  53.5 2.6 %collective-permute-start.14 = (f16[2,64,512]{2,1,0:T(8,128)(2,1)S(1)}, f16[2,64,512]{2,1,0:T(8,128)(2,1)S(1)}, u32[]{:S(2)}, u32[]{:S(2)}) collective-permute-start(f16[2,64,512]{2,1,0:T(8,128)(2,1)S(1)} %get-tuple-element.48), channel_id=1, source_target_pairs={{0,6},{1,7},{2,4},{3,5},{4,2},{5,3},{6,0},{7,1},{8,14},{9,15},{10,... | collective-permute-start | bytes 393224 | tf_op jit(solution)/shard_map/ppermute | solution.py:31
  56.1 1.9 %collective-permute-start.16 = (f16[2,64,512]{2,1,0:T(8,128)(2,1)S(1)}, f16[2,64,512]{2,1,0:T(8,128)(2,1)S(1)}, u32[]{:S(2)}, u32[]{:S(2)}) collective-permute-start(f16[2,64,512]{2,1,0:T(8,128)(2,1)S(1)} %get-tuple-element.46), channel_id=1, source_target_pairs={{0,2},{1,3},{2,0},{3,1},{4,6},{5,7},{6,4},{7,5},{8,10},{9,11},{10,... | collective-permute-start | bytes 393224 | tf_op jit(solution)/shard_map/ppermute | solution.py:31
  57.9 1.9 %collective-permute-done.13 = f16[4,64,512]{2,1,0:T(8,128)(2,1)S(1)} collective-permute-done((f16[4,64,512]{2,1,0:T(8,128)(2,1)S(1)}, f16[4,64,512]{2,1,0:T(8,128)(2,1)S(1)}, u32[]{:S(2)}, u32[]{:S(2)}) %collective-permute-start.13) | collective-permute-done | bytes 262176 | tf_op jit(solution)/shard_map/ppermute | solution.py:31
  60.0 0.7 collective-permute-start.17
  60.6 2.5 %collective-permute-start.18 = (f16[64,512]{1,0:T(8,128)(2,1)S(1)}, f16[64,512]{1,0:T(8,128)(2,1)S(1)}, u32[]{:S(2)}, u32[]{:S(2)}) collective-permute-start(f16[64,512]{1,0:T(8,128)(2,1)S(1)} %get-tuple-element.55), channel_id=1, source_target_pairs={{0,4},{1,5},{2,6},{3,7},{4,0},{5,1},{6,2},{7,3},{8,12},{9,13},{10,... | collective-permute-start | bytes 196616 | tf_op jit(solution)/shard_map/ppermute | solution.py:31
  63.1 1.3 %collective-permute-start.19 = (f16[64,512]{1,0:T(8,128)(2,1)S(1)}, f16[64,512]{1,0:T(8,128)(2,1)S(1)}, u32[]{:S(2)}, u32[]{:S(2)}) collective-permute-start(f16[64,512]{1,0:T(8,128)(2,1)S(1)} %get-tuple-element.54), channel_id=1, source_target_pairs={{0,6},{1,7},{2,4},{3,5},{4,2},{5,3},{6,0},{7,1},{8,14},{9,15},{10,... | collective-permute-start | bytes 196616 | tf_op jit(solution)/shard_map/ppermute | solution.py:31
  64.4 6.5 %collective-permute-done.15 = f16[2,64,512]{2,1,0:T(8,128)(2,1)S(1)} collective-permute-done((f16[2,64,512]{2,1,0:T(8,128)(2,1)S(1)}, f16[2,64,512]{2,1,0:T(8,128)(2,1)S(1)}, u32[]{:S(2)}, u32[]{:S(2)}) %collective-permute-start.15) | collective-permute-done | bytes 131104 | tf_op jit(solution)/shard_map/ppermute | solution.py:31
  71.1 0.6 collective-permute-start.25
  71.9 1.3 %collective-permute-start.20 = (f16[64,512]{1,0:T(8,128)(2,1)S(1)}, f16[64,512]{1,0:T(8,128)(2,1)S(1)}, u32[]{:S(2)}, u32[]{:S(2)}) collective-permute-start(f16[64,512]{1,0:T(8,128)(2,1)S(1)} %fusion.10), channel_id=1, source_target_pairs={{0,2},{1,3},{2,0},{3,1},{4,6},{5,7},{6,4},{7,5},{8,10},{9,11},{10,... | collective-permute-start | bytes 196616 | tf_op jit(solution)/shard_map/ppermute | solution.py:31
  73.4 3.0 %collective-permute-start.22 = (f16[64,512]{1,0:T(8,128)(2,1)S(1)}, f16[64,512]{1,0:T(8,128)(2,1)S(1)}, u32[]{:S(2)}, u32[]{:S(2)}) collective-permute-start(f16[64,512]{1,0:T(8,128)(2,1)S(1)} %fusion.10), channel_id=1, source_target_pairs={{0,6},{1,7},{2,4},{3,5},{4,2},{5,3},{6,0},{7,1},{8,14},{9,15},{10,... | collective-permute-start | bytes 196616 | tf_op jit(solution)/shard_map/ppermute | solution.py:31
  76.9 1.1 %collective-permute-start.27 = (f16[2,64,512]{2,1,0:T(8,128)(2,1)S(1)}, f16[2,64,512]{2,1,0:T(8,128)(2,1)S(1)}, u32[]{:S(2)}, u32[]{:S(2)}) collective-permute-start(f16[2,64,512]{2,1,0:T(8,128)(2,1)S(1)} %add_convert_fusion), channel_id=1, source_target_pairs={{0,4},{1,5},{2,6},{3,7},{4,0},{5,1},{6,2},{7,3},{8,12},{9,13},{10,... | collective-permute-start | bytes 393224 | tf_op jit(solution)/shard_map/ppermute | solution.py:31
  78.0 2.9 %collective-permute-start.28 = (f16[2,64,512]{2,1,0:T(8,128)(2,1)S(1)}, f16[2,64,512]{2,1,0:T(8,128)(2,1)S(1)}, u32[]{:S(2)}, u32[]{:S(2)}) collective-permute-start(f16[2,64,512]{2,1,0:T(8,128)(2,1)S(1)} %add_convert_fusion), channel_id=1, source_target_pairs={{0,6},{1,7},{2,4},{3,5},{4,2},{5,3},{6,0},{7,1},{8,14},{9,15},{10,... | collective-permute-start | bytes 393224 | tf_op jit(solution)/shard_map/ppermute | solution.py:31
  81.1 1.4 %collective-permute-start.23 = (f16[4,64,512]{2,1,0:T(8,128)(2,1)S(1)}, f16[4,64,512]{2,1,0:T(8,128)(2,1)S(1)}, u32[]{:S(2)}, u32[]{:S(2)}) collective-permute-start(f16[4,64,512]{2,1,0:T(8,128)(2,1)S(1)} %get-tuple-element.52), channel_id=1, source_target_pairs={{0,1},{1,0},{2,3},{3,2},{4,5},{5,4},{6,7},{7,6},{8,9},{9,8},{10,11... | collective-permute-start | bytes 786440 | tf_op jit(solution)/shard_map/ppermute | solution.py:31
  82.5 2.2 %collective-permute-done.26 = f16[2,64,512]{2,1,0:T(8,128)(2,1)S(1)} collective-permute-done((f16[2,64,512]{2,1,0:T(8,128)(2,1)S(1)}, f16[2,64,512]{2,1,0:T(8,128)(2,1)S(1)}, u32[]{:S(2)}, u32[]{:S(2)}) %collective-permute-start.26) | collective-permute-done | bytes 131104 | tf_op jit(solution)/shard_map/ppermute | solution.py:31
  84.7 5.9 %collective-permute-done.27 = f16[2,64,512]{2,1,0:T(8,128)(2,1)S(1)} collective-permute-done((f16[2,64,512]{2,1,0:T(8,128)(2,1)S(1)}, f16[2,64,512]{2,1,0:T(8,128)(2,1)S(1)}, u32[]{:S(2)}, u32[]{:S(2)}) %collective-permute-start.27) | collective-permute-done | bytes 131104 | tf_op jit(solution)/shard_map/ppermute | solution.py:31
  91.1 2.9 %finish.1 = (bf16[64,8192]{1,0:T(8,128)(2,1)}, bf16[64,8192]{1,0:T(8,128)(2,1)}) custom-call(s32[2]{0:T(128)S(1)} %pad_add_fusion.place, f32[1]{0:T(128)} %bitcast.14.bound, bf16[64,8192]{1,0:T(8,128)(2,1)S(1)} %bitcast.65, bf16[1,8192]{1,0:T(2,128)(2,1)S(1)} %broadcast_in_dim.7.gain, f32[8,64,512]{2,1,0:T(8,128)S(1)} %bitcast.66, ...), custom_call_target="tpu_custom_call" | custom-call | flops 4194304 | bytes 7340032 | tf_op jit(solution)/shard_map/finish/pallas_call | solution.py:389
  (91 shorter events, 4.8 us)
Async XLA Ops:
  0.6 9.5 %copy-start = (bf16[8,8,8192]{2,1,0:T(8,128)(2,1)S(1)}, bf16[8,8,8192]{2,1,0:T(8,128)(2,1)}, u32[]{:S(2)}) copy-start(bf16[8,8,8192]{2,1,0:T(8,128)(2,1)} %param.14) | copy-start | bytes 3145732
  0.6 12.5 %collective-permute-start.1 = (bf16[64,512]{1,0:T(8,128)(2,1)}, bf16[64,512]{1,0:T(8,128)(2,1)S(1)}, u32[]{:S(2)}, u32[]{:S(2)}) collective-permute-start(bf16[64,512]{1,0:T(8,128)(2,1)} %bitcast.86), channel_id=1, source_target_pairs={{0,2},{1,3},{2,0},{3,1},{4,6},{5,7},{6,4},{7,5},{8,10},{9,11},{10,... | collective-permute-start | bytes 196616 | tf_op jit(solution)/shard_map/ppermute | solution.py:31
  3.7 9.4 %collective-permute-start.2 = (bf16[64,512]{1,0:T(8,128)(2,1)}, bf16[64,512]{1,0:T(8,128)(2,1)S(1)}, u32[]{:S(2)}, u32[]{:S(2)}) collective-permute-start(bf16[64,512]{1,0:T(8,128)(2,1)} %bitcast.87), channel_id=1, source_target_pairs={{0,4},{1,5},{2,6},{3,7},{4,0},{5,1},{6,2},{7,3},{8,12},{9,13},{10,... | collective-permute-start | bytes 196616 | tf_op jit(solution)/shard_map/ppermute | solution.py:31
  6.3 6.8 %collective-permute-start.3 = (bf16[64,512]{1,0:T(8,128)(2,1)}, bf16[64,512]{1,0:T(8,128)(2,1)S(1)}, u32[]{:S(2)}, u32[]{:S(2)}) collective-permute-start(bf16[64,512]{1,0:T(8,128)(2,1)} %bitcast.88), channel_id=1, source_target_pairs={{0,6},{1,7},{2,4},{3,5},{4,2},{5,3},{6,0},{7,1},{8,14},{9,15},{10,... | collective-permute-start | bytes 196616 | tf_op jit(solution)/shard_map/ppermute | solution.py:31
  7.0 6.2 %copy-start.5 = (bf16[512,64]{0,1:T(8,128)(2,1)S(1)}, bf16[512,64]{0,1:T(8,128)(2,1)}, u32[]{:S(2)}) copy-start(bf16[512,64]{0,1:T(8,128)(2,1)} %param.20) | copy-start | bytes 196612
  11.0 7.8 %collective-permute-start.10 = (bf16[64,4096]{1,0:T(8,128)(2,1)S(1)}, bf16[64,4096]{1,0:T(8,128)(2,1)S(1)}, u32[]{:S(2)}, u32[]{:S(2)}) collective-permute-start(bf16[64,4096]{1,0:T(8,128)(2,1)S(1)} %get-tuple-element.49), channel_id=1, source_target_pairs={{0,8},{8,0},{1,9},{9,1},{2,10},{10,2},{3,11},{11,3},{4,12},{12,4},... | collective-permute-start | bytes 1572872 | tf_op jit(solution)/shard_map/ppermute | solution.py:35
  11.1 1.9 %collective-permute-start = (bf16[16,128]{1,0:T(8,128)(2,1)S(1)}, bf16[16,128]{1,0:T(8,128)(2,1)S(1)}, u32[]{:S(2)}, u32[]{:S(2)}) collective-permute-start(bf16[16,128]{1,0:T(8,128)(2,1)S(1)} %slice.64), channel_id=1, source_target_pairs={{0,8},{8,0},{1,9},{9,1},{2,10},{10,2},{3,11},{11,3},{4,12},{12,4},... | collective-permute-start | bytes 12296 | tf_op jit(solution)/shard_map/ppermute | solution.py:35
  13.0 5.8 %collective-permute-start.8 = (bf16[64,1024]{1,0:T(8,128)(2,1)S(1)}, bf16[64,1024]{1,0:T(8,128)(2,1)S(1)}, u32[]{:S(2)}, u32[]{:S(2)}) collective-permute-start(bf16[64,1024]{1,0:T(8,128)(2,1)S(1)} %pad_maximum_fusion.5), channel_id=1, source_target_pairs={{0,8},{8,0},{1,9},{9,1},{2,10},{10,2},{3,11},{11,3},{4,12},{12,4},... | collective-permute-start | bytes 393224 | tf_op jit(solution)/shard_map/ppermute | solution.py:35
  13.2 9.3 %collective-permute-start.9 = (bf16[4,64,512]{2,1,0:T(8,128)(2,1)S(1)}, bf16[4,64,512]{2,1,0:T(8,128)(2,1)S(1)}, u32[]{:S(2)}, u32[]{:S(2)}) collective-permute-start(bf16[4,64,512]{2,1,0:T(8,128)(2,1)S(1)} %pad_maximum_fusion.2.lower), channel_id=1, source_target_pairs={{0,1},{1,0},{2,3},{3,2},{4,5},{5,4},{6,7},{7,6},{8,9},{9,8},{10,11... | collective-permute-start | bytes 786440 | tf_op jit(solution)/shard_map/ppermute | solution.py:31
  18.4 7.7 %collective-permute-start.4 = (bf16[272,128]{1,0:T(8,128)(2,1)S(1)}, bf16[272,128]{1,0:T(8,128)(2,1)S(1)}, u32[]{:S(2)}, u32[]{:S(2)}) collective-permute-start(bf16[272,128]{1,0:T(8,128)(2,1)S(1)} %pad_maximum_fusion.8), channel_id=1, source_target_pairs={{0,1},{1,0},{2,3},{3,2},{4,5},{5,4},{6,7},{7,6},{8,9},{9,8},{10,11... | collective-permute-start | bytes 208904 | tf_op jit(solution)/shard_map/ppermute | solution.py:31
  26.0 4.8 %collective-permute-start.11 = (f32[64,1024]{1,0:T(8,128)S(1)}, f32[64,1024]{1,0:T(8,128)S(1)}, u32[]{:S(2)}, u32[]{:S(2)}) collective-permute-start(f32[64,1024]{1,0:T(8,128)S(1)} %get-tuple-element.33), channel_id=1, source_target_pairs={{0,8},{8,0},{1,9},{9,1},{2,10},{10,2},{3,11},{11,3},{4,12},{12,4},... | collective-permute-start | bytes 786440 | tf_op jit(solution)/shard_map/ppermute | solution.py:35
  26.2 12.0 %collective-permute-start.5 = (bf16[2,272,128]{2,1,0:T(8,128)(2,1)S(1)}, bf16[2,272,128]{2,1,0:T(8,128)(2,1)S(1)}, u32[]{:S(2)}, u32[]{:S(2)}) collective-permute-start(bf16[2,272,128]{2,1,0:T(8,128)(2,1)S(1)} %get-tuple-element.57), channel_id=1, source_target_pairs={{0,6},{1,7},{2,4},{3,5},{4,2},{5,3},{6,0},{7,1},{8,14},{9,15},{10,... | collective-permute-start | bytes 417800 | tf_op jit(solution)/shard_map/ppermute | solution.py:31
  30.1 11.5 %collective-permute-start.6 = (bf16[2,272,128]{2,1,0:T(8,128)(2,1)S(1)}, bf16[2,272,128]{2,1,0:T(8,128)(2,1)S(1)}, u32[]{:S(2)}, u32[]{:S(2)}) collective-permute-start(bf16[2,272,128]{2,1,0:T(8,128)(2,1)S(1)} %get-tuple-element.57), channel_id=1, source_target_pairs={{0,4},{1,5},{2,6},{3,7},{4,0},{5,1},{6,2},{7,3},{8,12},{9,13},{10,... | collective-permute-start | bytes 417800 | tf_op jit(solution)/shard_map/ppermute | solution.py:31
  30.1 11.5 %collective-permute-start.7 = (bf16[2,272,128]{2,1,0:T(8,128)(2,1)S(1)}, bf16[2,272,128]{2,1,0:T(8,128)(2,1)S(1)}, u32[]{:S(2)}, u32[]{:S(2)}) collective-permute-start(bf16[2,272,128]{2,1,0:T(8,128)(2,1)S(1)} %get-tuple-element.57), channel_id=1, source_target_pairs={{0,2},{1,3},{2,0},{3,1},{4,6},{5,7},{6,4},{7,5},{8,10},{9,11},{10,... | collective-permute-start | bytes 417800 | tf_op jit(solution)/shard_map/ppermute | solution.py:31
  38.1 4.9 %collective-permute-start.12 = (bf16[64,1024]{1,0:T(8,128)(2,1)S(1)}, bf16[64,1024]{1,0:T(8,128)(2,1)S(1)}, u32[]{:S(2)}, u32[]{:S(2)}) collective-permute-start(bf16[64,1024]{1,0:T(8,128)(2,1)S(1)} %attend.1.mine), channel_id=1, source_target_pairs={{0,8},{8,0},{1,9},{9,1},{2,10},{10,2},{3,11},{11,3},{4,12},{12,4},... | collective-permute-start | bytes 393224 | tf_op jit(solution)/shard_map/ppermute | solution.py:35
  51.7 29.3 %copy-start.7 = (bf16[8192]{0:T(1024)(128)(2,1)S(1)}, bf16[8192]{0:T(1024)(128)(2,1)}, u32[]{:S(2)}) copy-start(bf16[8192]{0:T(1024)(128)(2,1)} %param.16) | copy-start | bytes 49156
  51.8 8.0 %collective-permute-start.13 = (f16[4,64,512]{2,1,0:T(8,128)(2,1)S(1)}, f16[4,64,512]{2,1,0:T(8,128)(2,1)S(1)}, u32[]{:S(2)}, u32[]{:S(2)}) collective-permute-start(f16[4,64,512]{2,1,0:T(8,128)(2,1)S(1)} %fusion), channel_id=1, source_target_pairs={{0,1},{1,0},{2,3},{3,2},{4,5},{5,4},{6,7},{7,6},{8,9},{9,8},{10,11... | collective-permute-start | bytes 786440 | tf_op jit(solution)/shard_map/ppermute | solution.py:31
  53.5 9.6 %collective-permute-start.14 = (f16[2,64,512]{2,1,0:T(8,128)(2,1)S(1)}, f16[2,64,512]{2,1,0:T(8,128)(2,1)S(1)}, u32[]{:S(2)}, u32[]{:S(2)}) collective-permute-start(f16[2,64,512]{2,1,0:T(8,128)(2,1)S(1)} %get-tuple-element.48), channel_id=1, source_target_pairs={{0,6},{1,7},{2,4},{3,5},{4,2},{5,3},{6,0},{7,1},{8,14},{9,15},{10,... | collective-permute-start | bytes 393224 | tf_op jit(solution)/shard_map/ppermute | solution.py:31
  56.1 14.8 %collective-permute-start.15 = (f16[2,64,512]{2,1,0:T(8,128)(2,1)S(1)}, f16[2,64,512]{2,1,0:T(8,128)(2,1)S(1)}, u32[]{:S(2)}, u32[]{:S(2)}) collective-permute-start(f16[2,64,512]{2,1,0:T(8,128)(2,1)S(1)} %get-tuple-element.47), channel_id=1, source_target_pairs={{0,4},{1,5},{2,6},{3,7},{4,0},{5,1},{6,2},{7,3},{8,12},{9,13},{10,... | collective-permute-start | bytes 393224 | tf_op jit(solution)/shard_map/ppermute | solution.py:31
  56.1 14.8 %collective-permute-start.16 = (f16[2,64,512]{2,1,0:T(8,128)(2,1)S(1)}, f16[2,64,512]{2,1,0:T(8,128)(2,1)S(1)}, u32[]{:S(2)}, u32[]{:S(2)}) collective-permute-start(f16[2,64,512]{2,1,0:T(8,128)(2,1)S(1)} %get-tuple-element.46), channel_id=1, source_target_pairs={{0,2},{1,3},{2,0},{3,1},{4,6},{5,7},{6,4},{7,5},{8,10},{9,11},{10,... | collective-permute-start | bytes 393224 | tf_op jit(solution)/shard_map/ppermute | solution.py:31
  60.0 10.9 %collective-permute-start.17 = (f16[64,512]{1,0:T(8,128)(2,1)S(1)}, f16[64,512]{1,0:T(8,128)(2,1)S(1)}, u32[]{:S(2)}, u32[]{:S(2)}) collective-permute-start(f16[64,512]{1,0:T(8,128)(2,1)S(1)} %get-tuple-element.53), channel_id=1, source_target_pairs={{0,2},{1,3},{2,0},{3,1},{4,6},{5,7},{6,4},{7,5},{8,10},{9,11},{10,... | collective-permute-start | bytes 196616 | tf_op jit(solution)/shard_map/ppermute | solution.py:31
  60.6 11.3 %collective-permute-start.18 = (f16[64,512]{1,0:T(8,128)(2,1)S(1)}, f16[64,512]{1,0:T(8,128)(2,1)S(1)}, u32[]{:S(2)}, u32[]{:S(2)}) collective-permute-start(f16[64,512]{1,0:T(8,128)(2,1)S(1)} %get-tuple-element.55), channel_id=1, source_target_pairs={{0,4},{1,5},{2,6},{3,7},{4,0},{5,1},{6,2},{7,3},{8,12},{9,13},{10,... | collective-permute-start | bytes 196616 | tf_op jit(solution)/shard_map/ppermute | solution.py:31
  63.1 8.8 %collective-permute-start.19 = (f16[64,512]{1,0:T(8,128)(2,1)S(1)}, f16[64,512]{1,0:T(8,128)(2,1)S(1)}, u32[]{:S(2)}, u32[]{:S(2)}) collective-permute-start(f16[64,512]{1,0:T(8,128)(2,1)S(1)} %get-tuple-element.54), channel_id=1, source_target_pairs={{0,6},{1,7},{2,4},{3,5},{4,2},{5,3},{6,0},{7,1},{8,14},{9,15},{10,... | collective-permute-start | bytes 196616 | tf_op jit(solution)/shard_map/ppermute | solution.py:31
  71.0 5.4 %collective-permute-start.24 = (f16[2,64,512]{2,1,0:T(8,128)(2,1)S(1)}, f16[2,64,512]{2,1,0:T(8,128)(2,1)S(1)}, u32[]{:S(2)}, u32[]{:S(2)}) collective-permute-start(f16[2,64,512]{2,1,0:T(8,128)(2,1)S(1)} %fusion.1), channel_id=1, source_target_pairs={{0,8},{8,0},{1,9},{9,1},{2,10},{10,2},{3,11},{11,3},{4,12},{12,4},... | collective-permute-start | bytes 393224 | tf_op jit(solution)/shard_map/ppermute | solution.py:35
  71.1 5.4 %collective-permute-start.25 = (f16[2,64,512]{2,1,0:T(8,128)(2,1)S(1)}, f16[2,64,512]{2,1,0:T(8,128)(2,1)S(1)}, u32[]{:S(2)}, u32[]{:S(2)}) collective-permute-start(f16[2,64,512]{2,1,0:T(8,128)(2,1)S(1)} %fusion.1), channel_id=1, source_target_pairs={{0,9},{1,8},{2,11},{3,10},{4,13},{5,12},{6,15},{7,14},{8,1},{9,0},... | collective-permute-start | bytes 393224 | tf_op jit(solution)/shard_map/ppermute | solution.py:408
  71.9 6.1 %collective-permute-start.20 = (f16[64,512]{1,0:T(8,128)(2,1)S(1)}, f16[64,512]{1,0:T(8,128)(2,1)S(1)}, u32[]{:S(2)}, u32[]{:S(2)}) collective-permute-start(f16[64,512]{1,0:T(8,128)(2,1)S(1)} %fusion.10), channel_id=1, source_target_pairs={{0,2},{1,3},{2,0},{3,1},{4,6},{5,7},{6,4},{7,5},{8,10},{9,11},{10,... | collective-permute-start | bytes 196616 | tf_op jit(solution)/shard_map/ppermute | solution.py:31
  73.3 7.7 %collective-permute-start.21 = (f16[64,512]{1,0:T(8,128)(2,1)S(1)}, f16[64,512]{1,0:T(8,128)(2,1)S(1)}, u32[]{:S(2)}, u32[]{:S(2)}) collective-permute-start(f16[64,512]{1,0:T(8,128)(2,1)S(1)} %fusion.10), channel_id=1, source_target_pairs={{0,4},{1,5},{2,6},{3,7},{4,0},{5,1},{6,2},{7,3},{8,12},{9,13},{10,... | collective-permute-start | bytes 196616 | tf_op jit(solution)/shard_map/ppermute | solution.py:31
  73.4 7.7 %collective-permute-start.22 = (f16[64,512]{1,0:T(8,128)(2,1)S(1)}, f16[64,512]{1,0:T(8,128)(2,1)S(1)}, u32[]{:S(2)}, u32[]{:S(2)}) collective-permute-start(f16[64,512]{1,0:T(8,128)(2,1)S(1)} %fusion.10), channel_id=1, source_target_pairs={{0,6},{1,7},{2,4},{3,5},{4,2},{5,3},{6,0},{7,1},{8,14},{9,15},{10,... | collective-permute-start | bytes 196616 | tf_op jit(solution)/shard_map/ppermute | solution.py:31
  76.5 8.2 %collective-permute-start.26 = (f16[2,64,512]{2,1,0:T(8,128)(2,1)S(1)}, f16[2,64,512]{2,1,0:T(8,128)(2,1)S(1)}, u32[]{:S(2)}, u32[]{:S(2)}) collective-permute-start(f16[2,64,512]{2,1,0:T(8,128)(2,1)S(1)} %add_convert_fusion), channel_id=1, source_target_pairs={{0,2},{1,3},{2,0},{3,1},{4,6},{5,7},{6,4},{7,5},{8,10},{9,11},{10,... | collective-permute-start | bytes 393224 | tf_op jit(solution)/shard_map/ppermute | solution.py:31
  76.9 13.7 %collective-permute-start.27 = (f16[2,64,512]{2,1,0:T(8,128)(2,1)S(1)}, f16[2,64,512]{2,1,0:T(8,128)(2,1)S(1)}, u32[]{:S(2)}, u32[]{:S(2)}) collective-permute-start(f16[2,64,512]{2,1,0:T(8,128)(2,1)S(1)} %add_convert_fusion), channel_id=1, source_target_pairs={{0,4},{1,5},{2,6},{3,7},{4,0},{5,1},{6,2},{7,3},{8,12},{9,13},{10,... | collective-permute-start | bytes 393224 | tf_op jit(solution)/shard_map/ppermute | solution.py:31
  78.0 12.6 %collective-permute-start.28 = (f16[2,64,512]{2,1,0:T(8,128)(2,1)S(1)}, f16[2,64,512]{2,1,0:T(8,128)(2,1)S(1)}, u32[]{:S(2)}, u32[]{:S(2)}) collective-permute-start(f16[2,64,512]{2,1,0:T(8,128)(2,1)S(1)} %add_convert_fusion), channel_id=1, source_target_pairs={{0,6},{1,7},{2,4},{3,5},{4,2},{5,3},{6,0},{7,1},{8,14},{9,15},{10,... | collective-permute-start | bytes 393224 | tf_op jit(solution)/shard_map/ppermute | solution.py:31
  81.1 9.8 %collective-permute-start.23 = (f16[4,64,512]{2,1,0:T(8,128)(2,1)S(1)}, f16[4,64,512]{2,1,0:T(8,128)(2,1)S(1)}, u32[]{:S(2)}, u32[]{:S(2)}) collective-permute-start(f16[4,64,512]{2,1,0:T(8,128)(2,1)S(1)} %get-tuple-element.52), channel_id=1, source_target_pairs={{0,1},{1,0},{2,3},{3,2},{4,5},{5,4},{6,7},{7,6},{8,9},{9,8},{10,11... | collective-permute-start | bytes 786440 | tf_op jit(solution)/shard_map/ppermute | solution.py:31
  (7 other events, 27.2 us)

commit v7 on v6

--- a/solution.py
+++ b/solution.py
@@ -366,7 +366,8 @@
         squares = jnp.zeros((tall, 128), F32)
         for pieces, which in ((near, place[1]), (far, 1 - place[1])):
             for k in range(blocks):
-                start = pl.multiple_of(which * half + (place[0] ^ k) * width, width)
+                at = (blocks - k // 2 * 2) % blocks + k % 2 if pieces is near else k
+                start = pl.multiple_of(which * half + (place[0] ^ at) * width, width)
                 total = hidden[first : first + tall, pl.ds(start, width)].astype(F32)
                 total += pieces[k, first : first + tall] * bound[0]
                 combined[:, pl.ds(start, width)] = total
@@ -532,7 +533,7 @@
 
     near, far = reduce_blocks(own, other, shrink)
 
-    near = along_z(near)
+    near = along_z_far_first(near)
     near = jnp.stack([near, hop(near, 1)], axis=1)
     far = along_z(far)
     near = near.reshape((2 * outer,) + near.shape[2:]).astype(F32)

time: 94.3 us -> 93.6 us (level)
  waiting for transfers between devices: 21.1 us -> 19.4 us
  starting transfers between devices: 34.7 us -> 35.7 us
    ppermute x22, waiting for transfers between devices: 20.1 us -> 18.4 us  [hop(): return lax.ppermute(value, 'tp', [(i, i ^ distance) for i in range(total)])]
    ppermute x22, starting transfers between devices: 33.1 us -> 34.1 us  [hop(): return lax.ppermute(value, 'tp', [(i, i ^ distance) for i in range(total)])]
  transfers between devices with their start and end apart: 29 -> 29, of which waited for: 7 -> 9; matrix products, arithmetic and copies ran while one was open for 3% -> 3% of each run, Pallas kernels for 22% -> 22%
where the time goes in v7:
time: 93.6 us; the launch traced here: 93.4 us
  starting transfers between devices  35.7 us (38%)
  Pallas kernels  32.5 us (35%)
  waiting for transfers between devices  19.4 us (21%)
  other arithmetic  2.88 us (3%)
  between operations  1.95 us (2%)
  local copies, waits for them, and re-layouts  1.09 us (1%)
    ppermute x22, starting transfers between devices, hop(): return lax.ppermute(value, 'tp', [(i, i ^ distance) for i in range(total)])  34.1 us
    ppermute x22, waiting for transfers between devices, hop(): return lax.ppermute(value, 'tp', [(i, i ^ distance) for i in range(total)])  18.4 us
    pallas_call x1, Pallas kernels, output_project(): pl.pallas_call(output_kernel, in_specs=[SMEM, VMEM, VMEM, ANY, VMEM, VMEM...  8.68 us
    pallas_call x1, Pallas kernels, attend(): pl.pallas_call(functools.partial(attend_kernel, steps, scale), in_specs=[...  7.33 us
    pallas_call x2, Pallas kernels, query_project(): pl.pallas_call(functools.partial(query_kernel, y), in_specs=[SMEM] + [VME...  7.08 us
    pallas_call x1, Pallas kernels, fetch(): pl.pallas_call(fetch_kernel, in_specs=[ANY], out_specs=VMEM, out_shape=pl...  3.39 us
    pallas_call x1, Pallas kernels, with_largest_in_reach(): pl.pallas_call(reach_kernel, in_specs=[SMEM, ANY, ANY], out_specs=VMEM, o...  3.15 us
    pallas_call x1, Pallas kernels, finish(): pl.pallas_call(finish_kernel, in_specs=[SMEM, SMEM] + [VMEM] * 4, out_spe...  2.86 us
  transfers between devices with their start and end apart: 29, of which 9 were waited for; matrix products, arithmetic and copies ran while one was open for 3% of the time, Pallas kernels for 22%

profile of v7, /device:TPU:0, one launch (start us, length us, event | category | flops | bytes accessed | tf_op | source)
XLA Modules:
  0.0 93.4 jit_solution(7269982266554485939)
XLA Ops:
  0.6 3.1 %collective-permute-start.1 = (bf16[64,512]{1,0:T(8,128)(2,1)}, bf16[64,512]{1,0:T(8,128)(2,1)S(1)}, u32[]{:S(2)}, u32[]{:S(2)}) collective-permute-start(bf16[64,512]{1,0:T(8,128)(2,1)} %bitcast.86), channel_id=1, source_target_pairs={{0,2},{1,3},{2,0},{3,1},{4,6},{5,7},{6,4},{7,5},{8,10},{9,11},{10,... | collective-permute-start | bytes 196616 | tf_op jit(solution)/shard_map/ppermute | solution.py:31
  3.7 2.6 %collective-permute-start.2 = (bf16[64,512]{1,0:T(8,128)(2,1)}, bf16[64,512]{1,0:T(8,128)(2,1)S(1)}, u32[]{:S(2)}, u32[]{:S(2)}) collective-permute-start(bf16[64,512]{1,0:T(8,128)(2,1)} %bitcast.87), channel_id=1, source_target_pairs={{0,4},{1,5},{2,6},{3,7},{4,0},{5,1},{6,2},{7,3},{8,12},{9,13},{10,... | collective-permute-start | bytes 196616 | tf_op jit(solution)/shard_map/ppermute | solution.py:31
  6.3 0.7 copy-done.1
  7.0 3.1 %with_largest_in_reach.1 = bf16[272,128]{1,0:T(8,128)(2,1)S(1)} custom-call(s32[8]{0:T(128)S(1)} %copy-done.1, bf16[8,2048,128]{2,1,0:T(8,128)(2,1)} %bitcast.67, bf16[64,512]{1,0:T(8,128)(2,1)} %upper.1), custom_call_target="tpu_custom_call" | custom-call | flops 8388608 | bytes 4194304 | tf_op jit(solution)/shard_map/with_largest_in_reach/pallas_call | solution.py:110
  12.0 1.0 %collective-permute-done = bf16[16,128]{1,0:T(8,128)(2,1)S(1)} collective-permute-done((bf16[16,128]{1,0:T(8,128)(2,1)S(1)}, bf16[16,128]{1,0:T(8,128)(2,1)S(1)}, u32[]{:S(2)}, u32[]{:S(2)}) %collective-permute-start) | collective-permute-done | bytes 4128 | tf_op jit(solution)/shard_map/ppermute | solution.py:35
  13.2 1.8 %collective-permute-start.9 = (bf16[4,64,512]{2,1,0:T(8,128)(2,1)S(1)}, bf16[4,64,512]{2,1,0:T(8,128)(2,1)S(1)}, u32[]{:S(2)}, u32[]{:S(2)}) collective-permute-start(bf16[4,64,512]{2,1,0:T(8,128)(2,1)S(1)} %pad_maximum_fusion.2.lower), channel_id=1, source_target_pairs={{0,1},{1,0},{2,3},{3,2},{4,5},{5,4},{6,7},{7,6},{8,9},{9,8},{10,11... | collective-permute-start | bytes 786440 | tf_op jit(solution)/shard_map/ppermute | solution.py:31
  15.0 3.4 %fetch_query.1.base = bf16[4096,1024]{1,0:T(8,128)(2,1)S(1)} custom-call(bf16[4096,1024]{1,0:T(8,128)(2,1)} %source), custom_call_target="tpu_custom_call" | custom-call | bytes 8388608 | tf_op jit(solution)/shard_map/fetch_query/pallas_call | solution.py:62
  18.9 3.6 %query_project.2 = (bf16[4096,1024]{1,0:T(8,128)(2,1)}, f32[64,1024]{1,0:T(8,128)S(1)}, f32[64,1024]{1,0:T(8,128)S(1)}) custom-call(s32[1]{0:T(128)} %bitcast.place, bf16[4,64,512]{2,1,0:T(8,128)(2,1)S(1)} %pad_maximum_fusion.2.lower, bf16[64,1024]{1,0:T(8,128)(2,1)S(1)} %fusion.3.upper, bf16[4096,1024]{1,0:T(8,128)(2,1)S(1)} %fetch_query.1.base, ...), custom_call_target="tpu_custom_call" | custom-call | flops 805306368 | bytes 4194304 | tf_op jit(solution)/shard_map/query_project/pallas_call | solution.py:168
  22.5 3.5 %query_project.3 = (bf16[4096,1024]{1,0:T(8,128)(2,1)}, f32[64,1024]{1,0:T(8,128)S(1)}, f32[64,1024]{1,0:T(8,128)S(1)}) custom-call(s32[1]{0:T(128)} %bitcast.place, bf16[4,64,512]{2,1,0:T(8,128)(2,1)S(1)} %collective-permute-done.9.lower, bf16[64,1024]{1,0:T(8,128)(2,1)S(1)} %fusion.3.upper, ...), custom_call_target="tpu_custom_call", output_to_operand_aliasing={{0}: (6, {})} | custom-call | flops 805306368 | bytes 4194304 | tf_op jit(solution)/shard_map/query_project/pallas_call | solution.py:168
  26.2 3.9 %collective-permute-start.5 = (bf16[2,272,128]{2,1,0:T(8,128)(2,1)S(1)}, bf16[2,272,128]{2,1,0:T(8,128)(2,1)S(1)}, u32[]{:S(2)}, u32[]{:S(2)}) collective-permute-start(bf16[2,272,128]{2,1,0:T(8,128)(2,1)S(1)} %get-tuple-element.57), channel_id=1, source_target_pairs={{0,6},{1,7},{2,4},{3,5},{4,2},{5,3},{6,0},{7,1},{8,14},{9,15},{10,... | collective-permute-start | bytes 417800 | tf_op jit(solution)/shard_map/ppermute | solution.py:31
  30.1 0.6 collective-permute-start.7
  30.8 7.3 %attend.1.mine = bf16[64,1024]{1,0:T(8,128)(2,1)S(1)} custom-call(s32[8]{0:T(128)S(1)} %copy-done.2, f32[64,1024]{1,0:T(8,128)S(1)} %get-tuple-element.32.own, f32[64,1024]{1,0:T(8,128)S(1)} %collective-permute-done.11.other, bf16[1,1024]{1,0:T(2,128)(2,1)S(1)} %broadcast_in_dim.8.bias, f32[64,128]{1,0:T(8,128)S(1)} %get-tuple-element.63.cosine, ...), custom_call_target="tpu_custom_call" | custom-call | flops 536870912 | bytes 8388608 | tf_op jit(solution)/shard_map/attend/pallas_call | solution.py:263
  38.2 3.4 %collective-permute-done.6 = bf16[2,272,128]{2,1,0:T(8,128)(2,1)S(1)} collective-permute-done((bf16[2,272,128]{2,1,0:T(8,128)(2,1)S(1)}, bf16[2,272,128]{2,1,0:T(8,128)(2,1)S(1)}, u32[]{:S(2)}, u32[]{:S(2)}) %collective-permute-start.6) | collective-permute-done | bytes 139296 | tf_op jit(solution)/shard_map/ppermute | solution.py:31
  43.0 8.7 %output_project.1 = (bf16[1024,4096]{1,0:T(8,128)(2,1)}, f32[2,4,64,512]{3,2,1,0:T(8,128)S(1)}, f32[4,2,64,512]{3,2,1,0:T(8,128)S(1)}) custom-call(s32[1]{0:T(128)} %bitcast.place, bf16[64,1024]{1,0:T(8,128)(2,1)S(1)} %fusion.5.lower, bf16[4,2,272,128]{3,2,1,0:T(8,128)(2,1)S(1)} %pad_maximum_fusion.upper, bf16[1024,4096]{1,0:T(8,128)(2,1)} %base.1, ...), custom_call_target="tpu_custom_call" | custom-call | flops 1610612736 | bytes 16777216 | tf_op jit(solution)/shard_map/output_project/pallas_call | solution.py:329
  51.8 1.6 %collective-permute-start.13 = (f16[4,64,512]{2,1,0:T(8,128)(2,1)S(1)}, f16[4,64,512]{2,1,0:T(8,128)(2,1)S(1)}, u32[]{:S(2)}, u32[]{:S(2)}) collective-permute-start(f16[4,64,512]{2,1,0:T(8,128)(2,1)S(1)} %fusion), channel_id=1, source_target_pairs={{0,1},{1,0},{2,3},{3,2},{4,5},{5,4},{6,7},{7,6},{8,9},{9,8},{10,11... | collective-permute-start | bytes 786440 | tf_op jit(solution)/shard_map/ppermute | solution.py:31
  53.5 2.6 %collective-permute-start.14 = (f16[2,64,512]{2,1,0:T(8,128)(2,1)S(1)}, f16[2,64,512]{2,1,0:T(8,128)(2,1)S(1)}, u32[]{:S(2)}, u32[]{:S(2)}) collective-permute-start(f16[2,64,512]{2,1,0:T(8,128)(2,1)S(1)} %get-tuple-element.48), channel_id=1, source_target_pairs={{0,6},{1,7},{2,4},{3,5},{4,2},{5,3},{6,0},{7,1},{8,14},{9,15},{10,... | collective-permute-start | bytes 393224 | tf_op jit(solution)/shard_map/ppermute | solution.py:31
  56.1 1.9 %collective-permute-start.16 = (f16[2,64,512]{2,1,0:T(8,128)(2,1)S(1)}, f16[2,64,512]{2,1,0:T(8,128)(2,1)S(1)}, u32[]{:S(2)}, u32[]{:S(2)}) collective-permute-start(f16[2,64,512]{2,1,0:T(8,128)(2,1)S(1)} %get-tuple-element.46), channel_id=1, source_target_pairs={{0,2},{1,3},{2,0},{3,1},{4,6},{5,7},{6,4},{7,5},{8,10},{9,11},{10,... | collective-permute-start | bytes 393224 | tf_op jit(solution)/shard_map/ppermute | solution.py:31
  58.0 1.8 %collective-permute-done.13 = f16[4,64,512]{2,1,0:T(8,128)(2,1)S(1)} collective-permute-done((f16[4,64,512]{2,1,0:T(8,128)(2,1)S(1)}, f16[4,64,512]{2,1,0:T(8,128)(2,1)S(1)}, u32[]{:S(2)}, u32[]{:S(2)}) %collective-permute-start.13) | collective-permute-done | bytes 262176 | tf_op jit(solution)/shard_map/ppermute | solution.py:31
  60.0 0.7 collective-permute-start.17
  60.6 2.5 %collective-permute-start.18 = (f16[64,512]{1,0:T(8,128)(2,1)S(1)}, f16[64,512]{1,0:T(8,128)(2,1)S(1)}, u32[]{:S(2)}, u32[]{:S(2)}) collective-permute-start(f16[64,512]{1,0:T(8,128)(2,1)S(1)} %get-tuple-element.55), channel_id=1, source_target_pairs={{0,4},{1,5},{2,6},{3,7},{4,0},{5,1},{6,2},{7,3},{8,12},{9,13},{10,... | collective-permute-start | bytes 196616 | tf_op jit(solution)/shard_map/ppermute | solution.py:31
  63.1 1.3 %collective-permute-start.19 = (f16[64,512]{1,0:T(8,128)(2,1)S(1)}, f16[64,512]{1,0:T(8,128)(2,1)S(1)}, u32[]{:S(2)}, u32[]{:S(2)}) collective-permute-start(f16[64,512]{1,0:T(8,128)(2,1)S(1)} %get-tuple-element.54), channel_id=1, source_target_pairs={{0,6},{1,7},{2,4},{3,5},{4,2},{5,3},{6,0},{7,1},{8,14},{9,15},{10,... | collective-permute-start | bytes 196616 | tf_op jit(solution)/shard_map/ppermute | solution.py:31
  64.4 6.4 %collective-permute-done.15 = f16[2,64,512]{2,1,0:T(8,128)(2,1)S(1)} collective-permute-done((f16[2,64,512]{2,1,0:T(8,128)(2,1)S(1)}, f16[2,64,512]{2,1,0:T(8,128)(2,1)S(1)}, u32[]{:S(2)}, u32[]{:S(2)}) %collective-permute-start.15) | collective-permute-done | bytes 131104 | tf_op jit(solution)/shard_map/ppermute | solution.py:31
  71.9 0.9 collective-permute-start.20
  72.8 1.9 %collective-permute-start.21 = (f16[64,512]{1,0:T(8,128)(2,1)S(1)}, f16[64,512]{1,0:T(8,128)(2,1)S(1)}, u32[]{:S(2)}, u32[]{:S(2)}) collective-permute-start(f16[64,512]{1,0:T(8,128)(2,1)S(1)} %fusion.10), channel_id=1, source_target_pairs={{0,4},{1,5},{2,6},{3,7},{4,0},{5,1},{6,2},{7,3},{8,12},{9,13},{10,... | collective-permute-start | bytes 196616 | tf_op jit(solution)/shard_map/ppermute | solution.py:31
  74.7 1.7 %collective-permute-start.22 = (f16[64,512]{1,0:T(8,128)(2,1)S(1)}, f16[64,512]{1,0:T(8,128)(2,1)S(1)}, u32[]{:S(2)}, u32[]{:S(2)}) collective-permute-start(f16[64,512]{1,0:T(8,128)(2,1)S(1)} %fusion.10), channel_id=1, source_target_pairs={{0,2},{1,3},{2,0},{3,1},{4,6},{5,7},{6,4},{7,5},{8,10},{9,11},{10,... | collective-permute-start | bytes 196616 | tf_op jit(solution)/shard_map/ppermute | solution.py:31
  76.9 1.1 %collective-permute-start.27 = (f16[2,64,512]{2,1,0:T(8,128)(2,1)S(1)}, f16[2,64,512]{2,1,0:T(8,128)(2,1)S(1)}, u32[]{:S(2)}, u32[]{:S(2)}) collective-permute-start(f16[2,64,512]{2,1,0:T(8,128)(2,1)S(1)} %add_convert_fusion), channel_id=1, source_target_pairs={{0,4},{1,5},{2,6},{3,7},{4,0},{5,1},{6,2},{7,3},{8,12},{9,13},{10,... | collective-permute-start | bytes 393224 | tf_op jit(solution)/shard_map/ppermute | solution.py:31
  78.0 0.8 collective-permute-done.20
  78.8 2.1 %collective-permute-start.28 = (f16[2,64,512]{2,1,0:T(8,128)(2,1)S(1)}, f16[2,64,512]{2,1,0:T(8,128)(2,1)S(1)}, u32[]{:S(2)}, u32[]{:S(2)}) collective-permute-start(f16[2,64,512]{2,1,0:T(8,128)(2,1)S(1)} %add_convert_fusion), channel_id=1, source_target_pairs={{0,6},{1,7},{2,4},{3,5},{4,2},{5,3},{6,0},{7,1},{8,14},{9,15},{10,... | collective-permute-start | bytes 393224 | tf_op jit(solution)/shard_map/ppermute | solution.py:31
  81.6 3.1 %collective-permute-start.23 = (f16[4,64,512]{2,1,0:T(8,128)(2,1)S(1)}, f16[4,64,512]{2,1,0:T(8,128)(2,1)S(1)}, u32[]{:S(2)}, u32[]{:S(2)}) collective-permute-start(f16[4,64,512]{2,1,0:T(8,128)(2,1)S(1)} %get-tuple-element.52), channel_id=1, source_target_pairs={{0,1},{1,0},{2,3},{3,2},{4,5},{5,4},{6,7},{7,6},{8,9},{9,8},{10,11... | collective-permute-start | bytes 786440 | tf_op jit(solution)/shard_map/ppermute | solution.py:31
  84.7 1.3 %collective-permute-done.26 = f16[2,64,512]{2,1,0:T(8,128)(2,1)S(1)} collective-permute-done((f16[2,64,512]{2,1,0:T(8,128)(2,1)S(1)}, f16[2,64,512]{2,1,0:T(8,128)(2,1)S(1)}, u32[]{:S(2)}, u32[]{:S(2)}) %collective-permute-start.26) | collective-permute-done | bytes 131104 | tf_op jit(solution)/shard_map/ppermute | solution.py:31
  86.0 3.9 %collective-permute-done.27 = f16[2,64,512]{2,1,0:T(8,128)(2,1)S(1)} collective-permute-done((f16[2,64,512]{2,1,0:T(8,128)(2,1)S(1)}, f16[2,64,512]{2,1,0:T(8,128)(2,1)S(1)}, u32[]{:S(2)}, u32[]{:S(2)}) %collective-permute-start.27) | collective-permute-done | bytes 131104 | tf_op jit(solution)/shard_map/ppermute | solution.py:31
  90.4 2.9 %finish.1 = (bf16[64,8192]{1,0:T(8,128)(2,1)}, bf16[64,8192]{1,0:T(8,128)(2,1)}) custom-call(s32[2]{0:T(128)S(1)} %pad_add_fusion.place, f32[1]{0:T(128)} %bitcast.14.bound, bf16[64,8192]{1,0:T(8,128)(2,1)S(1)} %bitcast.65, bf16[1,8192]{1,0:T(2,128)(2,1)S(1)} %broadcast_in_dim.7.gain, f32[8,64,512]{2,1,0:T(8,128)S(1)} %bitcast.66, ...), custom_call_target="tpu_custom_call" | custom-call | flops 4194304 | bytes 7340032 | tf_op jit(solution)/shard_map/finish/pallas_call | solution.py:390
  (91 shorter events, 6.4 us)
Async XLA Ops:
  0.6 9.5 %copy-start = (bf16[8,8,8192]{2,1,0:T(8,128)(2,1)S(1)}, bf16[8,8,8192]{2,1,0:T(8,128)(2,1)}, u32[]{:S(2)}) copy-start(bf16[8,8,8192]{2,1,0:T(8,128)(2,1)} %param.14) | copy-start | bytes 3145732
  0.6 12.5 %collective-permute-start.1 = (bf16[64,512]{1,0:T(8,128)(2,1)}, bf16[64,512]{1,0:T(8,128)(2,1)S(1)}, u32[]{:S(2)}, u32[]{:S(2)}) collective-permute-start(bf16[64,512]{1,0:T(8,128)(2,1)} %bitcast.86), channel_id=1, source_target_pairs={{0,2},{1,3},{2,0},{3,1},{4,6},{5,7},{6,4},{7,5},{8,10},{9,11},{10,... | collective-permute-start | bytes 196616 | tf_op jit(solution)/shard_map/ppermute | solution.py:31
  3.7 9.4 %collective-permute-start.2 = (bf16[64,512]{1,0:T(8,128)(2,1)}, bf16[64,512]{1,0:T(8,128)(2,1)S(1)}, u32[]{:S(2)}, u32[]{:S(2)}) collective-permute-start(bf16[64,512]{1,0:T(8,128)(2,1)} %bitcast.87), channel_id=1, source_target_pairs={{0,4},{1,5},{2,6},{3,7},{4,0},{5,1},{6,2},{7,3},{8,12},{9,13},{10,... | collective-permute-start | bytes 196616 | tf_op jit(solution)/shard_map/ppermute | solution.py:31
  6.3 6.8 %collective-permute-start.3 = (bf16[64,512]{1,0:T(8,128)(2,1)}, bf16[64,512]{1,0:T(8,128)(2,1)S(1)}, u32[]{:S(2)}, u32[]{:S(2)}) collective-permute-start(bf16[64,512]{1,0:T(8,128)(2,1)} %bitcast.88), channel_id=1, source_target_pairs={{0,6},{1,7},{2,4},{3,5},{4,2},{5,3},{6,0},{7,1},{8,14},{9,15},{10,... | collective-permute-start | bytes 196616 | tf_op jit(solution)/shard_map/ppermute | solution.py:31
  7.0 6.2 %copy-start.5 = (bf16[512,64]{0,1:T(8,128)(2,1)S(1)}, bf16[512,64]{0,1:T(8,128)(2,1)}, u32[]{:S(2)}) copy-start(bf16[512,64]{0,1:T(8,128)(2,1)} %param.20) | copy-start | bytes 196612
  11.0 7.8 %collective-permute-start.10 = (bf16[64,4096]{1,0:T(8,128)(2,1)S(1)}, bf16[64,4096]{1,0:T(8,128)(2,1)S(1)}, u32[]{:S(2)}, u32[]{:S(2)}) collective-permute-start(bf16[64,4096]{1,0:T(8,128)(2,1)S(1)} %get-tuple-element.49), channel_id=1, source_target_pairs={{0,8},{8,0},{1,9},{9,1},{2,10},{10,2},{3,11},{11,3},{4,12},{12,4},... | collective-permute-start | bytes 1572872 | tf_op jit(solution)/shard_map/ppermute | solution.py:35
  11.1 1.9 %collective-permute-start = (bf16[16,128]{1,0:T(8,128)(2,1)S(1)}, bf16[16,128]{1,0:T(8,128)(2,1)S(1)}, u32[]{:S(2)}, u32[]{:S(2)}) collective-permute-start(bf16[16,128]{1,0:T(8,128)(2,1)S(1)} %slice.64), channel_id=1, source_target_pairs={{0,8},{8,0},{1,9},{9,1},{2,10},{10,2},{3,11},{11,3},{4,12},{12,4},... | collective-permute-start | bytes 12296 | tf_op jit(solution)/shard_map/ppermute | solution.py:35
  13.0 5.8 %collective-permute-start.8 = (bf16[64,1024]{1,0:T(8,128)(2,1)S(1)}, bf16[64,1024]{1,0:T(8,128)(2,1)S(1)}, u32[]{:S(2)}, u32[]{:S(2)}) collective-permute-start(bf16[64,1024]{1,0:T(8,128)(2,1)S(1)} %pad_maximum_fusion.5), channel_id=1, source_target_pairs={{0,8},{8,0},{1,9},{9,1},{2,10},{10,2},{3,11},{11,3},{4,12},{12,4},... | collective-permute-start | bytes 393224 | tf_op jit(solution)/shard_map/ppermute | solution.py:35
  13.2 9.3 %collective-permute-start.9 = (bf16[4,64,512]{2,1,0:T(8,128)(2,1)S(1)}, bf16[4,64,512]{2,1,0:T(8,128)(2,1)S(1)}, u32[]{:S(2)}, u32[]{:S(2)}) collective-permute-start(bf16[4,64,512]{2,1,0:T(8,128)(2,1)S(1)} %pad_maximum_fusion.2.lower), channel_id=1, source_target_pairs={{0,1},{1,0},{2,3},{3,2},{4,5},{5,4},{6,7},{7,6},{8,9},{9,8},{10,11... | collective-permute-start | bytes 786440 | tf_op jit(solution)/shard_map/ppermute | solution.py:31
  18.4 7.7 %collective-permute-start.4 = (bf16[272,128]{1,0:T(8,128)(2,1)S(1)}, bf16[272,128]{1,0:T(8,128)(2,1)S(1)}, u32[]{:S(2)}, u32[]{:S(2)}) collective-permute-start(bf16[272,128]{1,0:T(8,128)(2,1)S(1)} %pad_maximum_fusion.8), channel_id=1, source_target_pairs={{0,1},{1,0},{2,3},{3,2},{4,5},{5,4},{6,7},{7,6},{8,9},{9,8},{10,11... | collective-permute-start | bytes 208904 | tf_op jit(solution)/shard_map/ppermute | solution.py:31
  26.0 4.8 %collective-permute-start.11 = (f32[64,1024]{1,0:T(8,128)S(1)}, f32[64,1024]{1,0:T(8,128)S(1)}, u32[]{:S(2)}, u32[]{:S(2)}) collective-permute-start(f32[64,1024]{1,0:T(8,128)S(1)} %get-tuple-element.33), channel_id=1, source_target_pairs={{0,8},{8,0},{1,9},{9,1},{2,10},{10,2},{3,11},{11,3},{4,12},{12,4},... | collective-permute-start | bytes 786440 | tf_op jit(solution)/shard_map/ppermute | solution.py:35
  26.2 12.0 %collective-permute-start.5 = (bf16[2,272,128]{2,1,0:T(8,128)(2,1)S(1)}, bf16[2,272,128]{2,1,0:T(8,128)(2,1)S(1)}, u32[]{:S(2)}, u32[]{:S(2)}) collective-permute-start(bf16[2,272,128]{2,1,0:T(8,128)(2,1)S(1)} %get-tuple-element.57), channel_id=1, source_target_pairs={{0,6},{1,7},{2,4},{3,5},{4,2},{5,3},{6,0},{7,1},{8,14},{9,15},{10,... | collective-permute-start | bytes 417800 | tf_op jit(solution)/shard_map/ppermute | solution.py:31
  30.1 11.5 %collective-permute-start.6 = (bf16[2,272,128]{2,1,0:T(8,128)(2,1)S(1)}, bf16[2,272,128]{2,1,0:T(8,128)(2,1)S(1)}, u32[]{:S(2)}, u32[]{:S(2)}) collective-permute-start(bf16[2,272,128]{2,1,0:T(8,128)(2,1)S(1)} %get-tuple-element.57), channel_id=1, source_target_pairs={{0,4},{1,5},{2,6},{3,7},{4,0},{5,1},{6,2},{7,3},{8,12},{9,13},{10,... | collective-permute-start | bytes 417800 | tf_op jit(solution)/shard_map/ppermute | solution.py:31
  30.1 11.5 %collective-permute-start.7 = (bf16[2,272,128]{2,1,0:T(8,128)(2,1)S(1)}, bf16[2,272,128]{2,1,0:T(8,128)(2,1)S(1)}, u32[]{:S(2)}, u32[]{:S(2)}) collective-permute-start(bf16[2,272,128]{2,1,0:T(8,128)(2,1)S(1)} %get-tuple-element.57), channel_id=1, source_target_pairs={{0,2},{1,3},{2,0},{3,1},{4,6},{5,7},{6,4},{7,5},{8,10},{9,11},{10,... | collective-permute-start | bytes 417800 | tf_op jit(solution)/shard_map/ppermute | solution.py:31
  38.1 4.9 %collective-permute-start.12 = (bf16[64,1024]{1,0:T(8,128)(2,1)S(1)}, bf16[64,1024]{1,0:T(8,128)(2,1)S(1)}, u32[]{:S(2)}, u32[]{:S(2)}) collective-permute-start(bf16[64,1024]{1,0:T(8,128)(2,1)S(1)} %attend.1.mine), channel_id=1, source_target_pairs={{0,8},{8,0},{1,9},{9,1},{2,10},{10,2},{3,11},{11,3},{4,12},{12,4},... | collective-permute-start | bytes 393224 | tf_op jit(solution)/shard_map/ppermute | solution.py:35
  51.7 29.3 %copy-start.7 = (bf16[8192]{0:T(1024)(128)(2,1)S(1)}, bf16[8192]{0:T(1024)(128)(2,1)}, u32[]{:S(2)}) copy-start(bf16[8192]{0:T(1024)(128)(2,1)} %param.16) | copy-start | bytes 49156
  51.8 8.0 %collective-permute-start.13 = (f16[4,64,512]{2,1,0:T(8,128)(2,1)S(1)}, f16[4,64,512]{2,1,0:T(8,128)(2,1)S(1)}, u32[]{:S(2)}, u32[]{:S(2)}) collective-permute-start(f16[4,64,512]{2,1,0:T(8,128)(2,1)S(1)} %fusion), channel_id=1, source_target_pairs={{0,1},{1,0},{2,3},{3,2},{4,5},{5,4},{6,7},{7,6},{8,9},{9,8},{10,11... | collective-permute-start | bytes 786440 | tf_op jit(solution)/shard_map/ppermute | solution.py:31
  53.5 9.6 %collective-permute-start.14 = (f16[2,64,512]{2,1,0:T(8,128)(2,1)S(1)}, f16[2,64,512]{2,1,0:T(8,128)(2,1)S(1)}, u32[]{:S(2)}, u32[]{:S(2)}) collective-permute-start(f16[2,64,512]{2,1,0:T(8,128)(2,1)S(1)} %get-tuple-element.48), channel_id=1, source_target_pairs={{0,6},{1,7},{2,4},{3,5},{4,2},{5,3},{6,0},{7,1},{8,14},{9,15},{10,... | collective-permute-start | bytes 393224 | tf_op jit(solution)/shard_map/ppermute | solution.py:31
  56.1 14.8 %collective-permute-start.15 = (f16[2,64,512]{2,1,0:T(8,128)(2,1)S(1)}, f16[2,64,512]{2,1,0:T(8,128)(2,1)S(1)}, u32[]{:S(2)}, u32[]{:S(2)}) collective-permute-start(f16[2,64,512]{2,1,0:T(8,128)(2,1)S(1)} %get-tuple-element.47), channel_id=1, source_target_pairs={{0,4},{1,5},{2,6},{3,7},{4,0},{5,1},{6,2},{7,3},{8,12},{9,13},{10,... | collective-permute-start | bytes 393224 | tf_op jit(solution)/shard_map/ppermute | solution.py:31
  56.1 14.8 %collective-permute-start.16 = (f16[2,64,512]{2,1,0:T(8,128)(2,1)S(1)}, f16[2,64,512]{2,1,0:T(8,128)(2,1)S(1)}, u32[]{:S(2)}, u32[]{:S(2)}) collective-permute-start(f16[2,64,512]{2,1,0:T(8,128)(2,1)S(1)} %get-tuple-element.46), channel_id=1, source_target_pairs={{0,2},{1,3},{2,0},{3,1},{4,6},{5,7},{6,4},{7,5},{8,10},{9,11},{10,... | collective-permute-start | bytes 393224 | tf_op jit(solution)/shard_map/ppermute | solution.py:31
  60.0 10.9 %collective-permute-start.17 = (f16[64,512]{1,0:T(8,128)(2,1)S(1)}, f16[64,512]{1,0:T(8,128)(2,1)S(1)}, u32[]{:S(2)}, u32[]{:S(2)}) collective-permute-start(f16[64,512]{1,0:T(8,128)(2,1)S(1)} %get-tuple-element.53), channel_id=1, source_target_pairs={{0,2},{1,3},{2,0},{3,1},{4,6},{5,7},{6,4},{7,5},{8,10},{9,11},{10,... | collective-permute-start | bytes 196616 | tf_op jit(solution)/shard_map/ppermute | solution.py:31
  60.6 11.3 %collective-permute-start.18 = (f16[64,512]{1,0:T(8,128)(2,1)S(1)}, f16[64,512]{1,0:T(8,128)(2,1)S(1)}, u32[]{:S(2)}, u32[]{:S(2)}) collective-permute-start(f16[64,512]{1,0:T(8,128)(2,1)S(1)} %get-tuple-element.55), channel_id=1, source_target_pairs={{0,4},{1,5},{2,6},{3,7},{4,0},{5,1},{6,2},{7,3},{8,12},{9,13},{10,... | collective-permute-start | bytes 196616 | tf_op jit(solution)/shard_map/ppermute | solution.py:31
  63.1 8.8 %collective-permute-start.19 = (f16[64,512]{1,0:T(8,128)(2,1)S(1)}, f16[64,512]{1,0:T(8,128)(2,1)S(1)}, u32[]{:S(2)}, u32[]{:S(2)}) collective-permute-start(f16[64,512]{1,0:T(8,128)(2,1)S(1)} %get-tuple-element.54), channel_id=1, source_target_pairs={{0,6},{1,7},{2,4},{3,5},{4,2},{5,3},{6,0},{7,1},{8,14},{9,15},{10,... | collective-permute-start | bytes 196616 | tf_op jit(solution)/shard_map/ppermute | solution.py:31
  71.0 5.4 %collective-permute-start.24 = (f16[2,64,512]{2,1,0:T(8,128)(2,1)S(1)}, f16[2,64,512]{2,1,0:T(8,128)(2,1)S(1)}, u32[]{:S(2)}, u32[]{:S(2)}) collective-permute-start(f16[2,64,512]{2,1,0:T(8,128)(2,1)S(1)} %fusion.1), channel_id=1, source_target_pairs={{0,8},{8,0},{1,9},{9,1},{2,10},{10,2},{3,11},{11,3},{4,12},{12,4},... | collective-permute-start | bytes 393224 | tf_op jit(solution)/shard_map/ppermute | solution.py:35
  71.0 5.4 %collective-permute-start.25 = (f16[2,64,512]{2,1,0:T(8,128)(2,1)S(1)}, f16[2,64,512]{2,1,0:T(8,128)(2,1)S(1)}, u32[]{:S(2)}, u32[]{:S(2)}) collective-permute-start(f16[2,64,512]{2,1,0:T(8,128)(2,1)S(1)} %fusion.1), channel_id=1, source_target_pairs={{0,9},{1,8},{2,11},{3,10},{4,13},{5,12},{6,15},{7,14},{8,1},{9,0},... | collective-permute-start | bytes 393224 | tf_op jit(solution)/shard_map/ppermute | solution.py:409
  71.9 6.8 %collective-permute-start.20 = (f16[64,512]{1,0:T(8,128)(2,1)S(1)}, f16[64,512]{1,0:T(8,128)(2,1)S(1)}, u32[]{:S(2)}, u32[]{:S(2)}) collective-permute-start(f16[64,512]{1,0:T(8,128)(2,1)S(1)} %fusion.10), channel_id=1, source_target_pairs={{0,6},{1,7},{2,4},{3,5},{4,2},{5,3},{6,0},{7,1},{8,14},{9,15},{10,... | collective-permute-start | bytes 196616 | tf_op jit(solution)/shard_map/ppermute | solution.py:31
  72.8 8.7 %collective-permute-start.21 = (f16[64,512]{1,0:T(8,128)(2,1)S(1)}, f16[64,512]{1,0:T(8,128)(2,1)S(1)}, u32[]{:S(2)}, u32[]{:S(2)}) collective-permute-start(f16[64,512]{1,0:T(8,128)(2,1)S(1)} %fusion.10), channel_id=1, source_target_pairs={{0,4},{1,5},{2,6},{3,7},{4,0},{5,1},{6,2},{7,3},{8,12},{9,13},{10,... | collective-permute-start | bytes 196616 | tf_op jit(solution)/shard_map/ppermute | solution.py:31
  74.7 6.7 %collective-permute-start.22 = (f16[64,512]{1,0:T(8,128)(2,1)S(1)}, f16[64,512]{1,0:T(8,128)(2,1)S(1)}, u32[]{:S(2)}, u32[]{:S(2)}) collective-permute-start(f16[64,512]{1,0:T(8,128)(2,1)S(1)} %fusion.10), channel_id=1, source_target_pairs={{0,2},{1,3},{2,0},{3,1},{4,6},{5,7},{6,4},{7,5},{8,10},{9,11},{10,... | collective-permute-start | bytes 196616 | tf_op jit(solution)/shard_map/ppermute | solution.py:31
  76.5 9.5 %collective-permute-start.26 = (f16[2,64,512]{2,1,0:T(8,128)(2,1)S(1)}, f16[2,64,512]{2,1,0:T(8,128)(2,1)S(1)}, u32[]{:S(2)}, u32[]{:S(2)}) collective-permute-start(f16[2,64,512]{2,1,0:T(8,128)(2,1)S(1)} %add_convert_fusion), channel_id=1, source_target_pairs={{0,2},{1,3},{2,0},{3,1},{4,6},{5,7},{6,4},{7,5},{8,10},{9,11},{10,... | collective-permute-start | bytes 393224 | tf_op jit(solution)/shard_map/ppermute | solution.py:31
  76.9 13.0 %collective-permute-start.27 = (f16[2,64,512]{2,1,0:T(8,128)(2,1)S(1)}, f16[2,64,512]{2,1,0:T(8,128)(2,1)S(1)}, u32[]{:S(2)}, u32[]{:S(2)}) collective-permute-start(f16[2,64,512]{2,1,0:T(8,128)(2,1)S(1)} %add_convert_fusion), channel_id=1, source_target_pairs={{0,4},{1,5},{2,6},{3,7},{4,0},{5,1},{6,2},{7,3},{8,12},{9,13},{10,... | collective-permute-start | bytes 393224 | tf_op jit(solution)/shard_map/ppermute | solution.py:31
  78.8 11.1 %collective-permute-start.28 = (f16[2,64,512]{2,1,0:T(8,128)(2,1)S(1)}, f16[2,64,512]{2,1,0:T(8,128)(2,1)S(1)}, u32[]{:S(2)}, u32[]{:S(2)}) collective-permute-start(f16[2,64,512]{2,1,0:T(8,128)(2,1)S(1)} %add_convert_fusion), channel_id=1, source_target_pairs={{0,6},{1,7},{2,4},{3,5},{4,2},{5,3},{6,0},{7,1},{8,14},{9,15},{10,... | collective-permute-start | bytes 393224 | tf_op jit(solution)/shard_map/ppermute | solution.py:31
  81.6 8.6 %collective-permute-start.23 = (f16[4,64,512]{2,1,0:T(8,128)(2,1)S(1)}, f16[4,64,512]{2,1,0:T(8,128)(2,1)S(1)}, u32[]{:S(2)}, u32[]{:S(2)}) collective-permute-start(f16[4,64,512]{2,1,0:T(8,128)(2,1)S(1)} %get-tuple-element.52), channel_id=1, source_target_pairs={{0,1},{1,0},{2,3},{3,2},{4,5},{5,4},{6,7},{7,6},{8,9},{9,8},{10,11... | collective-permute-start | bytes 786440 | tf_op jit(solution)/shard_map/ppermute | solution.py:31
  (7 other events, 27.2 us)

commit v8 on v7

--- a/solution.py
+++ b/solution.py
@@ -386,7 +386,7 @@
 
 def finish(place, bound, hidden, gain, near, far):
     rows, whole = hidden.shape
-    tall = 16
+    tall = 32
     return pl.pallas_call(
         finish_kernel,
         in_specs=[SMEM, SMEM] + [VMEM] * 4,

time: 93.6 us -> 93.3 us (level)
  transfers between devices with their start and end apart: 29 -> 29, of which waited for: 9 -> 9; matrix products, arithmetic and copies ran while one was open for 3% -> 3% of each run, Pallas kernels for 22% -> 23%
where the time goes in v8:
time: 93.3 us; the launch traced here: 93.2 us
  starting transfers between devices  35.6 us (38%)
  Pallas kernels  32.2 us (35%)
  waiting for transfers between devices  19.4 us (21%)
  other arithmetic  2.88 us (3%)
  between operations  1.95 us (2%)
  local copies, waits for them, and re-layouts  1.09 us (1%)
    ppermute x22, starting transfers between devices, hop(): return lax.ppermute(value, 'tp', [(i, i ^ distance) for i in range(total)])  34.1 us
    ppermute x22, waiting for transfers between devices, hop(): return lax.ppermute(value, 'tp', [(i, i ^ distance) for i in range(total)])  18.5 us
    pallas_call x1, Pallas kernels, output_project(): pl.pallas_call(output_kernel, in_specs=[SMEM, VMEM, VMEM, ANY, VMEM, VMEM...  8.68 us
    pallas_call x1, Pallas kernels, attend(): pl.pallas_call(functools.partial(attend_kernel, steps, scale), in_specs=[...  7.34 us
    pallas_call x2, Pallas kernels, query_project(): pl.pallas_call(functools.partial(query_kernel, y), in_specs=[SMEM] + [VME...  7.08 us
    pallas_call x1, Pallas kernels, fetch(): pl.pallas_call(fetch_kernel, in_specs=[ANY], out_specs=VMEM, out_shape=pl...  3.39 us
    pallas_call x1, Pallas kernels, with_largest_in_reach(): pl.pallas_call(reach_kernel, in_specs=[SMEM, ANY, ANY], out_specs=VMEM, o...  3.3 us
    pallas_call x1, Pallas kernels, finish(): pl.pallas_call(finish_kernel, in_specs=[SMEM, SMEM] + [VMEM] * 4, out_spe...  2.44 us
  transfers between devices with their start and end apart: 29, of which 9 were waited for; matrix products, arithmetic and copies ran while one was open for 3% of the time, Pallas kernels for 23%

profile of v8, /device:TPU:0, one launch (start us, length us, event | category | flops | bytes accessed | tf_op | source)
XLA Modules:
  0.0 93.2 jit_solution(7212143825605228815)
XLA Ops:
  0.6 3.1 %collective-permute-start.1 = (bf16[64,512]{1,0:T(8,128)(2,1)}, bf16[64,512]{1,0:T(8,128)(2,1)S(1)}, u32[]{:S(2)}, u32[]{:S(2)}) collective-permute-start(bf16[64,512]{1,0:T(8,128)(2,1)} %bitcast.86), channel_id=1, source_target_pairs={{0,2},{1,3},{2,0},{3,1},{4,6},{5,7},{6,4},{7,5},{8,10},{9,11},{10,... | collective-permute-start | bytes 196616 | tf_op jit(solution)/shard_map/ppermute | solution.py:31
  3.7 2.6 %collective-permute-start.2 = (bf16[64,512]{1,0:T(8,128)(2,1)}, bf16[64,512]{1,0:T(8,128)(2,1)S(1)}, u32[]{:S(2)}, u32[]{:S(2)}) collective-permute-start(bf16[64,512]{1,0:T(8,128)(2,1)} %bitcast.87), channel_id=1, source_target_pairs={{0,4},{1,5},{2,6},{3,7},{4,0},{5,1},{6,2},{7,3},{8,12},{9,13},{10,... | collective-permute-start | bytes 196616 | tf_op jit(solution)/shard_map/ppermute | solution.py:31
  6.3 0.7 copy-done.1
  7.0 3.3 %with_largest_in_reach.1 = bf16[272,128]{1,0:T(8,128)(2,1)S(1)} custom-call(s32[8]{0:T(128)S(1)} %copy-done.1, bf16[8,2048,128]{2,1,0:T(8,128)(2,1)} %bitcast.67, bf16[64,512]{1,0:T(8,128)(2,1)} %upper.1), custom_call_target="tpu_custom_call" | custom-call | flops 8388608 | bytes 4194304 | tf_op jit(solution)/shard_map/with_largest_in_reach/pallas_call | solution.py:110
  12.2 1.0 %collective-permute-done = bf16[16,128]{1,0:T(8,128)(2,1)S(1)} collective-permute-done((bf16[16,128]{1,0:T(8,128)(2,1)S(1)}, bf16[16,128]{1,0:T(8,128)(2,1)S(1)}, u32[]{:S(2)}, u32[]{:S(2)}) %collective-permute-start) | collective-permute-done | bytes 4128 | tf_op jit(solution)/shard_map/ppermute | solution.py:35
  13.4 1.8 %collective-permute-start.9 = (bf16[4,64,512]{2,1,0:T(8,128)(2,1)S(1)}, bf16[4,64,512]{2,1,0:T(8,128)(2,1)S(1)}, u32[]{:S(2)}, u32[]{:S(2)}) collective-permute-start(bf16[4,64,512]{2,1,0:T(8,128)(2,1)S(1)} %pad_maximum_fusion.2.lower), channel_id=1, source_target_pairs={{0,1},{1,0},{2,3},{3,2},{4,5},{5,4},{6,7},{7,6},{8,9},{9,8},{10,11... | collective-permute-start | bytes 786440 | tf_op jit(solution)/shard_map/ppermute | solution.py:31
  15.2 3.4 %fetch_query.1.base = bf16[4096,1024]{1,0:T(8,128)(2,1)S(1)} custom-call(bf16[4096,1024]{1,0:T(8,128)(2,1)} %source), custom_call_target="tpu_custom_call" | custom-call | bytes 8388608 | tf_op jit(solution)/shard_map/fetch_query/pallas_call | solution.py:62
  19.0 3.6 %query_project.2 = (bf16[4096,1024]{1,0:T(8,128)(2,1)}, f32[64,1024]{1,0:T(8,128)S(1)}, f32[64,1024]{1,0:T(8,128)S(1)}) custom-call(s32[1]{0:T(128)} %bitcast.place, bf16[4,64,512]{2,1,0:T(8,128)(2,1)S(1)} %pad_maximum_fusion.2.lower, bf16[64,1024]{1,0:T(8,128)(2,1)S(1)} %fusion.3.upper, bf16[4096,1024]{1,0:T(8,128)(2,1)S(1)} %fetch_query.1.base, ...), custom_call_target="tpu_custom_call" | custom-call | flops 805306368 | bytes 4194304 | tf_op jit(solution)/shard_map/query_project/pallas_call | solution.py:168
  22.6 3.5 %query_project.3 = (bf16[4096,1024]{1,0:T(8,128)(2,1)}, f32[64,1024]{1,0:T(8,128)S(1)}, f32[64,1024]{1,0:T(8,128)S(1)}) custom-call(s32[1]{0:T(128)} %bitcast.place, bf16[4,64,512]{2,1,0:T(8,128)(2,1)S(1)} %collective-permute-done.9.lower, bf16[64,1024]{1,0:T(8,128)(2,1)S(1)} %fusion.3.upper, ...), custom_call_target="tpu_custom_call", output_to_operand_aliasing={{0}: (6, {})} | custom-call | flops 805306368 | bytes 4194304 | tf_op jit(solution)/shard_map/query_project/pallas_call | solution.py:168
  26.4 3.9 %collective-permute-start.5 = (bf16[2,272,128]{2,1,0:T(8,128)(2,1)S(1)}, bf16[2,272,128]{2,1,0:T(8,128)(2,1)S(1)}, u32[]{:S(2)}, u32[]{:S(2)}) collective-permute-start(bf16[2,272,128]{2,1,0:T(8,128)(2,1)S(1)} %get-tuple-element.57), channel_id=1, source_target_pairs={{0,6},{1,7},{2,4},{3,5},{4,2},{5,3},{6,0},{7,1},{8,14},{9,15},{10,... | collective-permute-start | bytes 417800 | tf_op jit(solution)/shard_map/ppermute | solution.py:31
  30.2 0.6 collective-permute-start.7
  30.9 7.3 %attend.1.mine = bf16[64,1024]{1,0:T(8,128)(2,1)S(1)} custom-call(s32[8]{0:T(128)S(1)} %copy-done.2, f32[64,1024]{1,0:T(8,128)S(1)} %get-tuple-element.32.own, f32[64,1024]{1,0:T(8,128)S(1)} %collective-permute-done.11.other, bf16[1,1024]{1,0:T(2,128)(2,1)S(1)} %broadcast_in_dim.8.bias, f32[64,128]{1,0:T(8,128)S(1)} %get-tuple-element.63.cosine, ...), custom_call_target="tpu_custom_call" | custom-call | flops 536870912 | bytes 8388608 | tf_op jit(solution)/shard_map/attend/pallas_call | solution.py:263
  38.4 3.4 %collective-permute-done.6 = bf16[2,272,128]{2,1,0:T(8,128)(2,1)S(1)} collective-permute-done((bf16[2,272,128]{2,1,0:T(8,128)(2,1)S(1)}, bf16[2,272,128]{2,1,0:T(8,128)(2,1)S(1)}, u32[]{:S(2)}, u32[]{:S(2)}) %collective-permute-start.6) | collective-permute-done | bytes 139296 | tf_op jit(solution)/shard_map/ppermute | solution.py:31
  43.2 8.7 %output_project.1 = (bf16[1024,4096]{1,0:T(8,128)(2,1)}, f32[2,4,64,512]{3,2,1,0:T(8,128)S(1)}, f32[4,2,64,512]{3,2,1,0:T(8,128)S(1)}) custom-call(s32[1]{0:T(128)} %bitcast.place, bf16[64,1024]{1,0:T(8,128)(2,1)S(1)} %fusion.5.lower, bf16[4,2,272,128]{3,2,1,0:T(8,128)(2,1)S(1)} %pad_maximum_fusion.upper, bf16[1024,4096]{1,0:T(8,128)(2,1)} %base.1, ...), custom_call_target="tpu_custom_call" | custom-call | flops 1610612736 | bytes 16777216 | tf_op jit(solution)/shard_map/output_project/pallas_call | solution.py:329
  52.0 1.6 %collective-permute-start.13 = (f16[4,64,512]{2,1,0:T(8,128)(2,1)S(1)}, f16[4,64,512]{2,1,0:T(8,128)(2,1)S(1)}, u32[]{:S(2)}, u32[]{:S(2)}) collective-permute-start(f16[4,64,512]{2,1,0:T(8,128)(2,1)S(1)} %fusion), channel_id=1, source_target_pairs={{0,1},{1,0},{2,3},{3,2},{4,5},{5,4},{6,7},{7,6},{8,9},{9,8},{10,11... | collective-permute-start | bytes 786440 | tf_op jit(solution)/shard_map/ppermute | solution.py:31
  53.6 2.6 %collective-permute-start.14 = (f16[2,64,512]{2,1,0:T(8,128)(2,1)S(1)}, f16[2,64,512]{2,1,0:T(8,128)(2,1)S(1)}, u32[]{:S(2)}, u32[]{:S(2)}) collective-permute-start(f16[2,64,512]{2,1,0:T(8,128)(2,1)S(1)} %get-tuple-element.48), channel_id=1, source_target_pairs={{0,6},{1,7},{2,4},{3,5},{4,2},{5,3},{6,0},{7,1},{8,14},{9,15},{10,... | collective-permute-start | bytes 393224 | tf_op jit(solution)/shard_map/ppermute | solution.py:31
  56.2 1.9 %collective-permute-start.16 = (f16[2,64,512]{2,1,0:T(8,128)(2,1)S(1)}, f16[2,64,512]{2,1,0:T(8,128)(2,1)S(1)}, u32[]{:S(2)}, u32[]{:S(2)}) collective-permute-start(f16[2,64,512]{2,1,0:T(8,128)(2,1)S(1)} %get-tuple-element.46), channel_id=1, source_target_pairs={{0,2},{1,3},{2,0},{3,1},{4,6},{5,7},{6,4},{7,5},{8,10},{9,11},{10,... | collective-permute-start | bytes 393224 | tf_op jit(solution)/shard_map/ppermute | solution.py:31
  58.1 1.9 %collective-permute-done.13 = f16[4,64,512]{2,1,0:T(8,128)(2,1)S(1)} collective-permute-done((f16[4,64,512]{2,1,0:T(8,128)(2,1)S(1)}, f16[4,64,512]{2,1,0:T(8,128)(2,1)S(1)}, u32[]{:S(2)}, u32[]{:S(2)}) %collective-permute-start.13) | collective-permute-done | bytes 262176 | tf_op jit(solution)/shard_map/ppermute | solution.py:31
  60.1 0.7 collective-permute-start.17
  60.8 2.5 %collective-permute-start.18 = (f16[64,512]{1,0:T(8,128)(2,1)S(1)}, f16[64,512]{1,0:T(8,128)(2,1)S(1)}, u32[]{:S(2)}, u32[]{:S(2)}) collective-permute-start(f16[64,512]{1,0:T(8,128)(2,1)S(1)} %get-tuple-element.55), channel_id=1, source_target_pairs={{0,4},{1,5},{2,6},{3,7},{4,0},{5,1},{6,2},{7,3},{8,12},{9,13},{10,... | collective-permute-start | bytes 196616 | tf_op jit(solution)/shard_map/ppermute | solution.py:31
  63.3 1.3 %collective-permute-start.19 = (f16[64,512]{1,0:T(8,128)(2,1)S(1)}, f16[64,512]{1,0:T(8,128)(2,1)S(1)}, u32[]{:S(2)}, u32[]{:S(2)}) collective-permute-start(f16[64,512]{1,0:T(8,128)(2,1)S(1)} %get-tuple-element.54), channel_id=1, source_target_pairs={{0,6},{1,7},{2,4},{3,5},{4,2},{5,3},{6,0},{7,1},{8,14},{9,15},{10,... | collective-permute-start | bytes 196616 | tf_op jit(solution)/shard_map/ppermute | solution.py:31
  64.6 6.5 %collective-permute-done.15 = f16[2,64,512]{2,1,0:T(8,128)(2,1)S(1)} collective-permute-done((f16[2,64,512]{2,1,0:T(8,128)(2,1)S(1)}, f16[2,64,512]{2,1,0:T(8,128)(2,1)S(1)}, u32[]{:S(2)}, u32[]{:S(2)}) %collective-permute-start.15) | collective-permute-done | bytes 131104 | tf_op jit(solution)/shard_map/ppermute | solution.py:31
  72.1 0.9 collective-permute-start.20
  72.9 1.9 %collective-permute-start.21 = (f16[64,512]{1,0:T(8,128)(2,1)S(1)}, f16[64,512]{1,0:T(8,128)(2,1)S(1)}, u32[]{:S(2)}, u32[]{:S(2)}) collective-permute-start(f16[64,512]{1,0:T(8,128)(2,1)S(1)} %fusion.10), channel_id=1, source_target_pairs={{0,4},{1,5},{2,6},{3,7},{4,0},{5,1},{6,2},{7,3},{8,12},{9,13},{10,... | collective-permute-start | bytes 196616 | tf_op jit(solution)/shard_map/ppermute | solution.py:31
  74.9 1.7 %collective-permute-start.22 = (f16[64,512]{1,0:T(8,128)(2,1)S(1)}, f16[64,512]{1,0:T(8,128)(2,1)S(1)}, u32[]{:S(2)}, u32[]{:S(2)}) collective-permute-start(f16[64,512]{1,0:T(8,128)(2,1)S(1)} %fusion.10), channel_id=1, source_target_pairs={{0,2},{1,3},{2,0},{3,1},{4,6},{5,7},{6,4},{7,5},{8,10},{9,11},{10,... | collective-permute-start | bytes 196616 | tf_op jit(solution)/shard_map/ppermute | solution.py:31
  77.0 1.1 %collective-permute-start.27 = (f16[2,64,512]{2,1,0:T(8,128)(2,1)S(1)}, f16[2,64,512]{2,1,0:T(8,128)(2,1)S(1)}, u32[]{:S(2)}, u32[]{:S(2)}) collective-permute-start(f16[2,64,512]{2,1,0:T(8,128)(2,1)S(1)} %add_convert_fusion), channel_id=1, source_target_pairs={{0,4},{1,5},{2,6},{3,7},{4,0},{5,1},{6,2},{7,3},{8,12},{9,13},{10,... | collective-permute-start | bytes 393224 | tf_op jit(solution)/shard_map/ppermute | solution.py:31
  78.2 0.8 collective-permute-done.20
  78.9 2.1 %collective-permute-start.28 = (f16[2,64,512]{2,1,0:T(8,128)(2,1)S(1)}, f16[2,64,512]{2,1,0:T(8,128)(2,1)S(1)}, u32[]{:S(2)}, u32[]{:S(2)}) collective-permute-start(f16[2,64,512]{2,1,0:T(8,128)(2,1)S(1)} %add_convert_fusion), channel_id=1, source_target_pairs={{0,6},{1,7},{2,4},{3,5},{4,2},{5,3},{6,0},{7,1},{8,14},{9,15},{10,... | collective-permute-start | bytes 393224 | tf_op jit(solution)/shard_map/ppermute | solution.py:31
  81.7 3.1 %collective-permute-start.23 = (f16[4,64,512]{2,1,0:T(8,128)(2,1)S(1)}, f16[4,64,512]{2,1,0:T(8,128)(2,1)S(1)}, u32[]{:S(2)}, u32[]{:S(2)}) collective-permute-start(f16[4,64,512]{2,1,0:T(8,128)(2,1)S(1)} %get-tuple-element.52), channel_id=1, source_target_pairs={{0,1},{1,0},{2,3},{3,2},{4,5},{5,4},{6,7},{7,6},{8,9},{9,8},{10,11... | collective-permute-start | bytes 786440 | tf_op jit(solution)/shard_map/ppermute | solution.py:31
  84.8 1.3 %collective-permute-done.26 = f16[2,64,512]{2,1,0:T(8,128)(2,1)S(1)} collective-permute-done((f16[2,64,512]{2,1,0:T(8,128)(2,1)S(1)}, f16[2,64,512]{2,1,0:T(8,128)(2,1)S(1)}, u32[]{:S(2)}, u32[]{:S(2)}) %collective-permute-start.26) | collective-permute-done | bytes 131104 | tf_op jit(solution)/shard_map/ppermute | solution.py:31
  86.1 3.9 %collective-permute-done.27 = f16[2,64,512]{2,1,0:T(8,128)(2,1)S(1)} collective-permute-done((f16[2,64,512]{2,1,0:T(8,128)(2,1)S(1)}, f16[2,64,512]{2,1,0:T(8,128)(2,1)S(1)}, u32[]{:S(2)}, u32[]{:S(2)}) %collective-permute-start.27) | collective-permute-done | bytes 131104 | tf_op jit(solution)/shard_map/ppermute | solution.py:31
  90.6 2.4 %finish.1 = (bf16[64,8192]{1,0:T(8,128)(2,1)}, bf16[64,8192]{1,0:T(8,128)(2,1)}) custom-call(s32[2]{0:T(128)S(1)} %pad_add_fusion.place, f32[1]{0:T(128)} %bitcast.14.bound, bf16[64,8192]{1,0:T(8,128)(2,1)S(1)} %bitcast.65, bf16[1,8192]{1,0:T(2,128)(2,1)S(1)} %broadcast_in_dim.7.gain, f32[8,64,512]{2,1,0:T(8,128)S(1)} %bitcast.66, ...), custom_call_target="tpu_custom_call" | custom-call | flops 4194304 | bytes 7340032 | tf_op jit(solution)/shard_map/finish/pallas_call | solution.py:390
  (91 shorter events, 6.4 us)
Async XLA Ops:
  0.6 9.7 %copy-start = (bf16[8,8,8192]{2,1,0:T(8,128)(2,1)S(1)}, bf16[8,8,8192]{2,1,0:T(8,128)(2,1)}, u32[]{:S(2)}) copy-start(bf16[8,8,8192]{2,1,0:T(8,128)(2,1)} %param.14) | copy-start | bytes 3145732
  0.6 12.6 %collective-permute-start.1 = (bf16[64,512]{1,0:T(8,128)(2,1)}, bf16[64,512]{1,0:T(8,128)(2,1)S(1)}, u32[]{:S(2)}, u32[]{:S(2)}) collective-permute-start(bf16[64,512]{1,0:T(8,128)(2,1)} %bitcast.86), channel_id=1, source_target_pairs={{0,2},{1,3},{2,0},{3,1},{4,6},{5,7},{6,4},{7,5},{8,10},{9,11},{10,... | collective-permute-start | bytes 196616 | tf_op jit(solution)/shard_map/ppermute | solution.py:31
  3.7 9.6 %collective-permute-start.2 = (bf16[64,512]{1,0:T(8,128)(2,1)}, bf16[64,512]{1,0:T(8,128)(2,1)S(1)}, u32[]{:S(2)}, u32[]{:S(2)}) collective-permute-start(bf16[64,512]{1,0:T(8,128)(2,1)} %bitcast.87), channel_id=1, source_target_pairs={{0,4},{1,5},{2,6},{3,7},{4,0},{5,1},{6,2},{7,3},{8,12},{9,13},{10,... | collective-permute-start | bytes 196616 | tf_op jit(solution)/shard_map/ppermute | solution.py:31
  6.3 7.0 %collective-permute-start.3 = (bf16[64,512]{1,0:T(8,128)(2,1)}, bf16[64,512]{1,0:T(8,128)(2,1)S(1)}, u32[]{:S(2)}, u32[]{:S(2)}) collective-permute-start(bf16[64,512]{1,0:T(8,128)(2,1)} %bitcast.88), channel_id=1, source_target_pairs={{0,6},{1,7},{2,4},{3,5},{4,2},{5,3},{6,0},{7,1},{8,14},{9,15},{10,... | collective-permute-start | bytes 196616 | tf_op jit(solution)/shard_map/ppermute | solution.py:31
  7.0 6.3 %copy-start.5 = (bf16[512,64]{0,1:T(8,128)(2,1)S(1)}, bf16[512,64]{0,1:T(8,128)(2,1)}, u32[]{:S(2)}) copy-start(bf16[512,64]{0,1:T(8,128)(2,1)} %param.20) | copy-start | bytes 196612
  11.1 7.8 %collective-permute-start.10 = (bf16[64,4096]{1,0:T(8,128)(2,1)S(1)}, bf16[64,4096]{1,0:T(8,128)(2,1)S(1)}, u32[]{:S(2)}, u32[]{:S(2)}) collective-permute-start(bf16[64,4096]{1,0:T(8,128)(2,1)S(1)} %get-tuple-element.49), channel_id=1, source_target_pairs={{0,8},{8,0},{1,9},{9,1},{2,10},{10,2},{3,11},{11,3},{4,12},{12,4},... | collective-permute-start | bytes 1572872 | tf_op jit(solution)/shard_map/ppermute | solution.py:35
  11.2 1.9 %collective-permute-start = (bf16[16,128]{1,0:T(8,128)(2,1)S(1)}, bf16[16,128]{1,0:T(8,128)(2,1)S(1)}, u32[]{:S(2)}, u32[]{:S(2)}) collective-permute-start(bf16[16,128]{1,0:T(8,128)(2,1)S(1)} %slice.64), channel_id=1, source_target_pairs={{0,8},{8,0},{1,9},{9,1},{2,10},{10,2},{3,11},{11,3},{4,12},{12,4},... | collective-permute-start | bytes 12296 | tf_op jit(solution)/shard_map/ppermute | solution.py:35
  13.1 5.8 %collective-permute-start.8 = (bf16[64,1024]{1,0:T(8,128)(2,1)S(1)}, bf16[64,1024]{1,0:T(8,128)(2,1)S(1)}, u32[]{:S(2)}, u32[]{:S(2)}) collective-permute-start(bf16[64,1024]{1,0:T(8,128)(2,1)S(1)} %pad_maximum_fusion.5), channel_id=1, source_target_pairs={{0,8},{8,0},{1,9},{9,1},{2,10},{10,2},{3,11},{11,3},{4,12},{12,4},... | collective-permute-start | bytes 393224 | tf_op jit(solution)/shard_map/ppermute | solution.py:35
  13.4 9.3 %collective-permute-start.9 = (bf16[4,64,512]{2,1,0:T(8,128)(2,1)S(1)}, bf16[4,64,512]{2,1,0:T(8,128)(2,1)S(1)}, u32[]{:S(2)}, u32[]{:S(2)}) collective-permute-start(bf16[4,64,512]{2,1,0:T(8,128)(2,1)S(1)} %pad_maximum_fusion.2.lower), channel_id=1, source_target_pairs={{0,1},{1,0},{2,3},{3,2},{4,5},{5,4},{6,7},{7,6},{8,9},{9,8},{10,11... | collective-permute-start | bytes 786440 | tf_op jit(solution)/shard_map/ppermute | solution.py:31
  18.6 7.7 %collective-permute-start.4 = (bf16[272,128]{1,0:T(8,128)(2,1)S(1)}, bf16[272,128]{1,0:T(8,128)(2,1)S(1)}, u32[]{:S(2)}, u32[]{:S(2)}) collective-permute-start(bf16[272,128]{1,0:T(8,128)(2,1)S(1)} %pad_maximum_fusion.8), channel_id=1, source_target_pairs={{0,1},{1,0},{2,3},{3,2},{4,5},{5,4},{6,7},{7,6},{8,9},{9,8},{10,11... | collective-permute-start | bytes 208904 | tf_op jit(solution)/shard_map/ppermute | solution.py:31
  26.1 4.8 %collective-permute-start.11 = (f32[64,1024]{1,0:T(8,128)S(1)}, f32[64,1024]{1,0:T(8,128)S(1)}, u32[]{:S(2)}, u32[]{:S(2)}) collective-permute-start(f32[64,1024]{1,0:T(8,128)S(1)} %get-tuple-element.33), channel_id=1, source_target_pairs={{0,8},{8,0},{1,9},{9,1},{2,10},{10,2},{3,11},{11,3},{4,12},{12,4},... | collective-permute-start | bytes 786440 | tf_op jit(solution)/shard_map/ppermute | solution.py:35
  26.4 12.0 %collective-permute-start.5 = (bf16[2,272,128]{2,1,0:T(8,128)(2,1)S(1)}, bf16[2,272,128]{2,1,0:T(8,128)(2,1)S(1)}, u32[]{:S(2)}, u32[]{:S(2)}) collective-permute-start(bf16[2,272,128]{2,1,0:T(8,128)(2,1)S(1)} %get-tuple-element.57), channel_id=1, source_target_pairs={{0,6},{1,7},{2,4},{3,5},{4,2},{5,3},{6,0},{7,1},{8,14},{9,15},{10,... | collective-permute-start | bytes 417800 | tf_op jit(solution)/shard_map/ppermute | solution.py:31
  30.2 11.5 %collective-permute-start.6 = (bf16[2,272,128]{2,1,0:T(8,128)(2,1)S(1)}, bf16[2,272,128]{2,1,0:T(8,128)(2,1)S(1)}, u32[]{:S(2)}, u32[]{:S(2)}) collective-permute-start(bf16[2,272,128]{2,1,0:T(8,128)(2,1)S(1)} %get-tuple-element.57), channel_id=1, source_target_pairs={{0,4},{1,5},{2,6},{3,7},{4,0},{5,1},{6,2},{7,3},{8,12},{9,13},{10,... | collective-permute-start | bytes 417800 | tf_op jit(solution)/shard_map/ppermute | solution.py:31
  30.2 11.5 %collective-permute-start.7 = (bf16[2,272,128]{2,1,0:T(8,128)(2,1)S(1)}, bf16[2,272,128]{2,1,0:T(8,128)(2,1)S(1)}, u32[]{:S(2)}, u32[]{:S(2)}) collective-permute-start(bf16[2,272,128]{2,1,0:T(8,128)(2,1)S(1)} %get-tuple-element.57), channel_id=1, source_target_pairs={{0,2},{1,3},{2,0},{3,1},{4,6},{5,7},{6,4},{7,5},{8,10},{9,11},{10,... | collective-permute-start | bytes 417800 | tf_op jit(solution)/shard_map/ppermute | solution.py:31
  38.3 4.9 %collective-permute-start.12 = (bf16[64,1024]{1,0:T(8,128)(2,1)S(1)}, bf16[64,1024]{1,0:T(8,128)(2,1)S(1)}, u32[]{:S(2)}, u32[]{:S(2)}) collective-permute-start(bf16[64,1024]{1,0:T(8,128)(2,1)S(1)} %attend.1.mine), channel_id=1, source_target_pairs={{0,8},{8,0},{1,9},{9,1},{2,10},{10,2},{3,11},{11,3},{4,12},{12,4},... | collective-permute-start | bytes 393224 | tf_op jit(solution)/shard_map/ppermute | solution.py:35
  51.9 29.3 %copy-start.7 = (bf16[8192]{0:T(1024)(128)(2,1)S(1)}, bf16[8192]{0:T(1024)(128)(2,1)}, u32[]{:S(2)}) copy-start(bf16[8192]{0:T(1024)(128)(2,1)} %param.16) | copy-start | bytes 49156
  52.0 8.0 %collective-permute-start.13 = (f16[4,64,512]{2,1,0:T(8,128)(2,1)S(1)}, f16[4,64,512]{2,1,0:T(8,128)(2,1)S(1)}, u32[]{:S(2)}, u32[]{:S(2)}) collective-permute-start(f16[4,64,512]{2,1,0:T(8,128)(2,1)S(1)} %fusion), channel_id=1, source_target_pairs={{0,1},{1,0},{2,3},{3,2},{4,5},{5,4},{6,7},{7,6},{8,9},{9,8},{10,11... | collective-permute-start | bytes 786440 | tf_op jit(solution)/shard_map/ppermute | solution.py:31
  53.6 9.6 %collective-permute-start.14 = (f16[2,64,512]{2,1,0:T(8,128)(2,1)S(1)}, f16[2,64,512]{2,1,0:T(8,128)(2,1)S(1)}, u32[]{:S(2)}, u32[]{:S(2)}) collective-permute-start(f16[2,64,512]{2,1,0:T(8,128)(2,1)S(1)} %get-tuple-element.48), channel_id=1, source_target_pairs={{0,6},{1,7},{2,4},{3,5},{4,2},{5,3},{6,0},{7,1},{8,14},{9,15},{10,... | collective-permute-start | bytes 393224 | tf_op jit(solution)/shard_map/ppermute | solution.py:31
  56.2 14.8 %collective-permute-start.15 = (f16[2,64,512]{2,1,0:T(8,128)(2,1)S(1)}, f16[2,64,512]{2,1,0:T(8,128)(2,1)S(1)}, u32[]{:S(2)}, u32[]{:S(2)}) collective-permute-start(f16[2,64,512]{2,1,0:T(8,128)(2,1)S(1)} %get-tuple-element.47), channel_id=1, source_target_pairs={{0,4},{1,5},{2,6},{3,7},{4,0},{5,1},{6,2},{7,3},{8,12},{9,13},{10,... | collective-permute-start | bytes 393224 | tf_op jit(solution)/shard_map/ppermute | solution.py:31
  56.2 14.8 %collective-permute-start.16 = (f16[2,64,512]{2,1,0:T(8,128)(2,1)S(1)}, f16[2,64,512]{2,1,0:T(8,128)(2,1)S(1)}, u32[]{:S(2)}, u32[]{:S(2)}) collective-permute-start(f16[2,64,512]{2,1,0:T(8,128)(2,1)S(1)} %get-tuple-element.46), channel_id=1, source_target_pairs={{0,2},{1,3},{2,0},{3,1},{4,6},{5,7},{6,4},{7,5},{8,10},{9,11},{10,... | collective-permute-start | bytes 393224 | tf_op jit(solution)/shard_map/ppermute | solution.py:31
  60.1 10.9 %collective-permute-start.17 = (f16[64,512]{1,0:T(8,128)(2,1)S(1)}, f16[64,512]{1,0:T(8,128)(2,1)S(1)}, u32[]{:S(2)}, u32[]{:S(2)}) collective-permute-start(f16[64,512]{1,0:T(8,128)(2,1)S(1)} %get-tuple-element.53), channel_id=1, source_target_pairs={{0,2},{1,3},{2,0},{3,1},{4,6},{5,7},{6,4},{7,5},{8,10},{9,11},{10,... | collective-permute-start | bytes 196616 | tf_op jit(solution)/shard_map/ppermute | solution.py:31
  60.8 11.3 %collective-permute-start.18 = (f16[64,512]{1,0:T(8,128)(2,1)S(1)}, f16[64,512]{1,0:T(8,128)(2,1)S(1)}, u32[]{:S(2)}, u32[]{:S(2)}) collective-permute-start(f16[64,512]{1,0:T(8,128)(2,1)S(1)} %get-tuple-element.55), channel_id=1, source_target_pairs={{0,4},{1,5},{2,6},{3,7},{4,0},{5,1},{6,2},{7,3},{8,12},{9,13},{10,... | collective-permute-start | bytes 196616 | tf_op jit(solution)/shard_map/ppermute | solution.py:31
  63.3 8.8 %collective-permute-start.19 = (f16[64,512]{1,0:T(8,128)(2,1)S(1)}, f16[64,512]{1,0:T(8,128)(2,1)S(1)}, u32[]{:S(2)}, u32[]{:S(2)}) collective-permute-start(f16[64,512]{1,0:T(8,128)(2,1)S(1)} %get-tuple-element.54), channel_id=1, source_target_pairs={{0,6},{1,7},{2,4},{3,5},{4,2},{5,3},{6,0},{7,1},{8,14},{9,15},{10,... | collective-permute-start | bytes 196616 | tf_op jit(solution)/shard_map/ppermute | solution.py:31
  71.1 5.4 %collective-permute-start.24 = (f16[2,64,512]{2,1,0:T(8,128)(2,1)S(1)}, f16[2,64,512]{2,1,0:T(8,128)(2,1)S(1)}, u32[]{:S(2)}, u32[]{:S(2)}) collective-permute-start(f16[2,64,512]{2,1,0:T(8,128)(2,1)S(1)} %fusion.1), channel_id=1, source_target_pairs={{0,8},{8,0},{1,9},{9,1},{2,10},{10,2},{3,11},{11,3},{4,12},{12,4},... | collective-permute-start | bytes 393224 | tf_op jit(solution)/shard_map/ppermute | solution.py:35
  71.2 5.4 %collective-permute-start.25 = (f16[2,64,512]{2,1,0:T(8,128)(2,1)S(1)}, f16[2,64,512]{2,1,0:T(8,128)(2,1)S(1)}, u32[]{:S(2)}, u32[]{:S(2)}) collective-permute-start(f16[2,64,512]{2,1,0:T(8,128)(2,1)S(1)} %fusion.1), channel_id=1, source_target_pairs={{0,9},{1,8},{2,11},{3,10},{4,13},{5,12},{6,15},{7,14},{8,1},{9,0},... | collective-permute-start | bytes 393224 | tf_op jit(solution)/shard_map/ppermute | solution.py:409
  72.1 6.8 %collective-permute-start.20 = (f16[64,512]{1,0:T(8,128)(2,1)S(1)}, f16[64,512]{1,0:T(8,128)(2,1)S(1)}, u32[]{:S(2)}, u32[]{:S(2)}) collective-permute-start(f16[64,512]{1,0:T(8,128)(2,1)S(1)} %fusion.10), channel_id=1, source_target_pairs={{0,6},{1,7},{2,4},{3,5},{4,2},{5,3},{6,0},{7,1},{8,14},{9,15},{10,... | collective-permute-start | bytes 196616 | tf_op jit(solution)/shard_map/ppermute | solution.py:31
  72.9 8.7 %collective-permute-start.21 = (f16[64,512]{1,0:T(8,128)(2,1)S(1)}, f16[64,512]{1,0:T(8,128)(2,1)S(1)}, u32[]{:S(2)}, u32[]{:S(2)}) collective-permute-start(f16[64,512]{1,0:T(8,128)(2,1)S(1)} %fusion.10), channel_id=1, source_target_pairs={{0,4},{1,5},{2,6},{3,7},{4,0},{5,1},{6,2},{7,3},{8,12},{9,13},{10,... | collective-permute-start | bytes 196616 | tf_op jit(solution)/shard_map/ppermute | solution.py:31
  74.9 6.8 %collective-permute-start.22 = (f16[64,512]{1,0:T(8,128)(2,1)S(1)}, f16[64,512]{1,0:T(8,128)(2,1)S(1)}, u32[]{:S(2)}, u32[]{:S(2)}) collective-permute-start(f16[64,512]{1,0:T(8,128)(2,1)S(1)} %fusion.10), channel_id=1, source_target_pairs={{0,2},{1,3},{2,0},{3,1},{4,6},{5,7},{6,4},{7,5},{8,10},{9,11},{10,... | collective-permute-start | bytes 196616 | tf_op jit(solution)/shard_map/ppermute | solution.py:31
  76.6 9.5 %collective-permute-start.26 = (f16[2,64,512]{2,1,0:T(8,128)(2,1)S(1)}, f16[2,64,512]{2,1,0:T(8,128)(2,1)S(1)}, u32[]{:S(2)}, u32[]{:S(2)}) collective-permute-start(f16[2,64,512]{2,1,0:T(8,128)(2,1)S(1)} %add_convert_fusion), channel_id=1, source_target_pairs={{0,2},{1,3},{2,0},{3,1},{4,6},{5,7},{6,4},{7,5},{8,10},{9,11},{10,... | collective-permute-start | bytes 393224 | tf_op jit(solution)/shard_map/ppermute | solution.py:31
  77.0 13.0 %collective-permute-start.27 = (f16[2,64,512]{2,1,0:T(8,128)(2,1)S(1)}, f16[2,64,512]{2,1,0:T(8,128)(2,1)S(1)}, u32[]{:S(2)}, u32[]{:S(2)}) collective-permute-start(f16[2,64,512]{2,1,0:T(8,128)(2,1)S(1)} %add_convert_fusion), channel_id=1, source_target_pairs={{0,4},{1,5},{2,6},{3,7},{4,0},{5,1},{6,2},{7,3},{8,12},{9,13},{10,... | collective-permute-start | bytes 393224 | tf_op jit(solution)/shard_map/ppermute | solution.py:31
  78.9 11.1 %collective-permute-start.28 = (f16[2,64,512]{2,1,0:T(8,128)(2,1)S(1)}, f16[2,64,512]{2,1,0:T(8,128)(2,1)S(1)}, u32[]{:S(2)}, u32[]{:S(2)}) collective-permute-start(f16[2,64,512]{2,1,0:T(8,128)(2,1)S(1)} %add_convert_fusion), channel_id=1, source_target_pairs={{0,6},{1,7},{2,4},{3,5},{4,2},{5,3},{6,0},{7,1},{8,14},{9,15},{10,... | collective-permute-start | bytes 393224 | tf_op jit(solution)/shard_map/ppermute | solution.py:31
  81.7 8.6 %collective-permute-start.23 = (f16[4,64,512]{2,1,0:T(8,128)(2,1)S(1)}, f16[4,64,512]{2,1,0:T(8,128)(2,1)S(1)}, u32[]{:S(2)}, u32[]{:S(2)}) collective-permute-start(f16[4,64,512]{2,1,0:T(8,128)(2,1)S(1)} %get-tuple-element.52), channel_id=1, source_target_pairs={{0,1},{1,0},{2,3},{3,2},{4,5},{5,4},{6,7},{7,6},{8,9},{9,8},{10,11... | collective-permute-start | bytes 786440 | tf_op jit(solution)/shard_map/ppermute | solution.py:31
  (7 other events, 27.9 us)
